TPU v7x, 1024 devices: a whole 4x8x16 slice. The times are simulated.
1024 devices in a mesh: enc: 8 (over y), dp: 64 (over x, z), rep: 2 (over core).
Axes of the slice: x: 4, y: 8, z: 16, core: 2. Of those that a mesh axis runs over, the one named last changes fastest.
Arguments:
- feat_sig: bfloat16 [32768, 1152], P(('dp', 'rep'), 'enc'), may hold values from -6 to 6
- feat_cnx: bfloat16 [32768, 3072], P(('dp', 'rep'), 'enc'), may hold values from -6 to 6
- cotangent: bfloat16 [32768, 2048], P(('dp', 'rep'), 'enc'), may hold values from -24 to 24
- w_sig: bfloat16 [2048, 1152], P(None, 'enc'), may hold values from -0.09375 to 0.09375
- w_cnx: bfloat16 [2048, 3072], P(None, 'enc'), may hold values from -0.09375 to 0.09375
- lengths: int32 [128, 64], P(('dp', 'rep')), may hold values from 1 to 4, as said below
- enc_of: int32 [128, 64], P(('dp', 'rep')), may hold values from 0 to 63, each once within a row
- owner_of: int32 [128, 64], P(('dp', 'rep')), may hold values from 0 to 63, each once within a row
- pre_sig: bfloat16 [32768, 1152], P(('dp', 'rep'), 'enc'), may hold values from -6 to 6
- pre_cnx: bfloat16 [32768, 3072], P(('dp', 'rep'), 'enc'), may hold values from -6 to 6
- gain_sig: float32 [1152], P('enc'), may hold values from 0.5 to 2
- gain_cnx: float32 [3072], P('enc'), may hold values from 0.5 to 2
Outputs:
- grad_w_sig: float32 [2048, 1152], P(('dp', 'rep'), 'enc')
- grad_w_cnx: float32 [2048, 3072], P(('dp', 'rep'), 'enc')
- gradient_before_siglip: bfloat16 [32768, 1152], P(('dp', 'rep'), 'enc')
- gradient_before_convnext: bfloat16 [32768, 3072], P(('dp', 'rep'), 'enc')
Inputs may be any that keep to these rules, and one draw needn't show every extreme that they name: `lengths`: every entry is 1, 2, 3 or 4; every row holds at least one entry equal to 4. `enc_of`: each row is a permutation of 0 .. 63. `owner_of`: each row is a permutation of 0 .. 63.
All inputs are finite; a program needn't handle non-finite values.
Results may differ from a plain program's by a relative error of at most 0.0049.
Values may be sent and summed in bfloat16 or wider, within the bound.
No kernel may reach another device: no remote copies, remote signals or barrier semaphores. Data moves between devices by JAX's collectives and lax.ppermute only.
A program may use at most 32 MiB of HBM per device.

v0:
```python
import math

import jax
import jax.numpy as jnp
from jax import lax
from jax.sharding import PartitionSpec as P

EPS = 1e-06


def row_statistics_pair(row_height, sum_h, sum_hh, feature_width):
    hidden_mean = sum_h[:, None] / feature_width
    var_h = sum_hh[:, None] / feature_width - hidden_mean * hidden_mean
    inverse_deviation = lax.rsqrt(var_h + EPS)
    return (hidden_mean, inverse_deviation, (row_height - hidden_mean) * inverse_deviation)


def shards(
    feat_sig,
    feat_cnx,
    cotangent,
    w_sig,
    w_cnx,
    lengths,
    enc_of,
    owner_of,
    pre_sig,
    pre_cnx,
    gain_sig,
    gain_cnx,
):
    slots = lengths.shape[1]
    rows = cotangent.shape[0]
    depth = rows // slots
    spots = lax.broadcasted_iota(jnp.int32, (slots, depth), 1)
    live = (spots < lengths[0][:, None]).reshape(rows, 1)
    masked = jnp.where(live, cotangent, jnp.zeros_like(cotangent))
    full_grad = lax.all_gather(masked, "enc", axis=1, tiled=True)
    back_sig = jnp.dot(full_grad, w_sig, preferred_element_type=jnp.float32).astype(jnp.bfloat16)
    back_cnx = jnp.dot(full_grad, w_cnx, preferred_element_type=jnp.float32).astype(jnp.bfloat16)
    inverse = jnp.argsort(enc_of[0])
    send_sig = jnp.take(back_sig.reshape(slots, depth, back_sig.shape[1]), inverse, axis=0)
    send_cnx = jnp.take(back_cnx.reshape(slots, depth, back_cnx.shape[1]), inverse, axis=0)
    recv_sig, recv_cnx = (
        lax.all_to_all(send_sig, "dp", split_axis=0, concat_axis=0, tiled=True),
        lax.all_to_all(send_cnx, "dp", split_axis=0, concat_axis=0, tiled=True),
    )
    sources = owner_of[0]
    dy_sig = jnp.take(recv_sig, sources, axis=0).reshape(rows, recv_sig.shape[2])
    dy_cnx = jnp.take(recv_cnx, sources, axis=0).reshape(rows, recv_cnx.shape[2])
    enc_count = lax.axis_size("enc")
    siglip_width = gain_sig.shape[0] * enc_count
    convnext_width = gain_cnx.shape[0] * enc_count
    siglip_height = pre_sig.astype(jnp.float32)
    convnext_height = pre_cnx.astype(jnp.float32)
    siglip_scaled_gradient = dy_sig.astype(jnp.float32) * gain_sig
    convnext_scaled_gradient = dy_cnx.astype(jnp.float32) * gain_cnx
    row_totals = lax.psum(
        (
            jnp.sum(siglip_height, axis=1),
            jnp.sum(siglip_height * siglip_height, axis=1),
            jnp.sum(convnext_height, axis=1),
            jnp.sum(convnext_height * convnext_height, axis=1),
        ),
        "enc",
    )
    siglip_mean, siglip_inverse_deviation, siglip_normalized = row_statistics_pair(
        siglip_height, row_totals[0], row_totals[1], siglip_width
    )
    convnext_mean, convnext_inverse_deviation, convnext_normalized = row_statistics_pair(
        convnext_height, row_totals[2], row_totals[3], convnext_width
    )
    later = lax.psum(
        (
            jnp.sum(siglip_scaled_gradient, axis=1),
            jnp.sum(siglip_scaled_gradient * siglip_normalized, axis=1),
            jnp.sum(convnext_scaled_gradient, axis=1),
            jnp.sum(convnext_scaled_gradient * convnext_normalized, axis=1),
        ),
        "enc",
    )
    siglip_gradient_mean = later[0][:, None] / siglip_width
    siglip_product_mean = later[1][:, None] / siglip_width
    convnext_gradient_mean = later[2][:, None] / convnext_width
    convnext_product_mean = later[3][:, None] / convnext_width
    gradient_before_siglip = (
        siglip_inverse_deviation
        * (siglip_scaled_gradient - siglip_gradient_mean - siglip_normalized * siglip_product_mean)
    ).astype(jnp.bfloat16)
    gradient_before_convnext = (
        convnext_inverse_deviation
        * (
            convnext_scaled_gradient
            - convnext_gradient_mean
            - convnext_normalized * convnext_product_mean
        )
    ).astype(jnp.bfloat16)
    dp_count = lax.axis_size("dp")
    rep_count = lax.axis_size("rep")
    scale = 1.0 / math.sqrt(rows * dp_count * rep_count)
    split = feat_sig.shape[1]
    features = jnp.concatenate([feat_sig, feat_cnx], axis=1)
    summed = lax.psum_scatter(
        lax.dot_general(
            full_grad, features, (((0,), (0,)), ((), ())), preferred_element_type=jnp.float32
        ),
        ("dp", "rep"),
        scatter_dimension=0,
        tiled=True,
    )
    summed = summed * scale
    return (summed[:, :split], summed[:, split:], gradient_before_siglip, gradient_before_convnext)


def solution(mesh):
    in_specs = (
        P(("dp", "rep"), "enc"),
        P(("dp", "rep"), "enc"),
        P(("dp", "rep"), "enc"),
        P(None, "enc"),
        P(None, "enc"),
        P(("dp", "rep"), None),
        P(("dp", "rep"), None),
        P(("dp", "rep"), None),
        P(("dp", "rep"), "enc"),
        P(("dp", "rep"), "enc"),
        P("enc"),
        P("enc"),
    )
    out_specs = (
        P(("dp", "rep"), "enc"),
        P(("dp", "rep"), "enc"),
        P(("dp", "rep"), "enc"),
        P(("dp", "rep"), "enc"),
    )
    return jax.shard_map(shards, mesh=mesh, in_specs=in_specs, out_specs=out_specs, check_vma=False)
```

profile of v0, /device:TPU:6, one launch (start us, length us, event | category | flops | bytes accessed | tf_op | source)
XLA Modules:
  0.0 357.0 jit_solution(4566711349907331282)
XLA Ops:
  7.2 0.8 iota_compare_fusion
  8.2 1.7 broadcast_select_fusion.2
  9.9 1.0 copy.17
  10.9 55.4 %all-gather.2.cloned.1.call-done = bf16[256,2048]{1,0:T(8,128)(2,1)} async-done(((bf16[256,256]{1,0:T(8,128)(2,1)}), bf16[256,2048]{1,0:T(8,128)(2,1)}) %all-gather.2.cloned.1.call-update) | async-done | bytes 1048592 | tf_op jit(solution)/shard_map/all_gather | solution.py:38
  66.3 4.7 %fusion.8 = f32[2048,528]{1,0:T(8,128)} fusion(bf16[256,2048]{1,0:T(8,128)(2,1)} %all-gather.2.cloned.1.call-done, bf16[256,384]{1,0:T(8,128)(2,1)} %param.17, bf16[256,144]{1,0:T(8,128)(2,1)S(1)} %copy.17), kind=kOutput, calls=%fused_computation.21 | convolution fusion | flops 554188800 | bytes 5644288 | tf_op jit(solution)/shard_map/dot_general | solution.py:104
  71.0 1.1 copy.18
  72.2 2.0 sort.17
  74.5 17.3 %all-reduce.1 = (f32[256]{0:T(256)}, f32[256]{0:T(256)}, f32[256]{0:T(256)}, f32[256]{0:T(256)}) all-reduce(f32[256]{0:T(256)S(1)} %get-tuple-element.15, f32[256]{0:T(256)S(1)} %get-tuple-element.14, f32[256]{0:T(256)S(1)} %get-tuple-element.13, f32[256]{0:T(256)S(1)} %get-tuple-element.12), channel_id=1, replica_groups=mesh['enc'=8,'dp'=64,'rep'=2] {'enc'}, use_global_device_ids=true, to_apply=%region_4.5 | all-reduce | flops 1024 | bytes 8192 | tf_op jit(solution)/shard_map/psum | solution.py:58
  91.8 0.7 compare_select_fusion.1
  92.5 1.2 compare_and_fusion.1
  93.7 1.2 compare_select_fusion
  94.9 0.7 compare_and_fusion
  95.6 0.7 add_rsqrt_fusion.1
  96.3 1.1 convolution_convert_fusion.1
  97.4 1.0 copy.19
  98.4 0.7 gather_fusion
  99.1 1.4 broadcast_select_fusion.1
  100.6 16.7 %all-to-all-start = ((bf16[64,4,144]{2,1,0:T(4,128)(2,1)}), bf16[64,4,144]{2,1,0:T(4,128)(2,1)S(1)}, u32[]{:S(2)}, u32[]{:S(2)}) async-start(bf16[64,4,144]{2,1,0:T(4,128)(2,1)} %broadcast_select_fusion.1), calls=%async_computation.1 | async-start | bytes 262144 | tf_op jit(solution)/shard_map/all_to_all | solution.py:45
  117.3 0.7 convolution_convert_fusion
  118.1 0.8 gather_fusion.2
  118.9 0.9 broadcast_select_fusion
  119.7 11.4 %all-to-all-done = bf16[64,4,144]{2,1,0:T(4,128)(2,1)S(1)} async-done(((bf16[64,4,144]{2,1,0:T(4,128)(2,1)}), bf16[64,4,144]{2,1,0:T(4,128)(2,1)S(1)}, u32[]{:S(2)}, u32[]{:S(2)}) %all-to-all-start) | async-done | bytes 73760 | tf_op jit(solution)/shard_map/all_to_all | solution.py:45
  131.2 6.7 %all-to-all-start.1 = ((bf16[64,4,384]{2,1,0:T(4,128)(2,1)}), bf16[64,4,384]{2,1,0:T(4,128)(2,1)S(1)}, u32[]{:S(2)}, u32[]{:S(2)}) async-start(bf16[64,4,384]{2,1,0:T(4,128)(2,1)} %broadcast_select_fusion), calls=%async_computation.2 | async-start | bytes 393216 | tf_op jit(solution)/shard_map/all_to_all | solution.py:46
  137.9 0.7 gather_fusion.1
  139.4 13.7 %all-to-all-done.1 = bf16[64,4,384]{2,1,0:T(4,128)(2,1)S(1)} async-done(((bf16[64,4,384]{2,1,0:T(4,128)(2,1)}), bf16[64,4,384]{2,1,0:T(4,128)(2,1)S(1)}, u32[]{:S(2)}, u32[]{:S(2)}) %all-to-all-start.1) | async-done | bytes 196640 | tf_op jit(solution)/shard_map/all_to_all | solution.py:46
  153.2 0.8 gather_fusion.3
  154.9 14.2 %all-reduce = (f32[256]{0:T(256)S(1)}, f32[256]{0:T(256)S(1)}, f32[256]{0:T(256)S(1)}, f32[256]{0:T(256)S(1)}) all-reduce(f32[256]{0:T(256)S(1)} %fusion.16, f32[256]{0:T(256)S(1)} %reduce_sum.79, f32[256]{0:T(256)S(1)} %fusion.4, f32[256]{0:T(256)S(1)} %reduce_sum.84), channel_id=1, replica_groups=mesh['enc'=8,'dp'=64,'rep'=2] {'enc'}, use_global_device_ids=true, to_apply=%region_9.11 | all-reduce | flops 1024 | bytes 8192 | tf_op jit(solution)/shard_map/psum | solution.py:73
  169.3 0.7 copy.20
  170.0 0.9 fusion.7
  170.9 177.2 %reduce-scatter.2.cloned.1.call-done = f32[16,528]{1,0:T(8,128)} async-done(((f32[2048,528]{1,0:T(8,128)}), f32[16,528]{1,0:T(8,128)}) %reduce-scatter.2.cloned.1.call-update) | async-done | bytes 33808 | tf_op jit(solution)/shard_map/reduce_scatter | solution.py:103
  348.1 0.8 broadcast_multiply_fusion
  349.5 0.7 slice.17
  (49 shorter events, 3.2 us)
Async XLA Ops:
  7.2 110.1 %copy-start = (bf16[2048,384]{1,0:T(8,128)(2,1)S(1)}, bf16[2048,384]{1,0:T(8,128)(2,1)}, u32[]{:S(2)}) copy-start(bf16[2048,384]{1,0:T(8,128)(2,1)} %param.20) | copy-start | bytes 4718596
  7.2 59.1 %all-gather.2.cloned.1.call-start = ((), (), s32[]{:S(2)}) async-start(), calls=%async_computation.3 | async-start | bytes 1179648 | tf_op jit(solution)/shard_map/all_gather | solution.py:38
  9.9 338.2 %reduce-scatter.2.cloned.1.call-start = ((), (), s32[]{:S(2)}) async-start(), calls=%async_computation.4 | async-start | bytes 5283840 | tf_op jit(solution)/shard_map/reduce_scatter | solution.py:103
  71.0 1.2 copy-start.10
  71.0 3.4 copy-start.2
  71.0 25.3 %copy-start.1 = (bf16[256,2048]{1,0:T(8,128)(2,1)S(1)}, bf16[256,2048]{1,0:T(8,128)(2,1)}, u32[]{:S(2)}) copy-start(bf16[256,2048]{1,0:T(8,128)(2,1)} %all-gather.2.cloned.1.call-done) | copy-start | bytes 3145732
  71.0 25.3 %copy-start.3 = (bf16[2048,144]{0,1:T(8,128)(2,1)S(1)}, bf16[2048,144]{0,1:T(8,128)(2,1)}, u32[]{:S(2)}) copy-start(bf16[2048,144]{0,1:T(8,128)(2,1)} %param.19) | copy-start | bytes 1769476
  100.6 30.6 %all-to-all-start = ((bf16[64,4,144]{2,1,0:T(4,128)(2,1)}), bf16[64,4,144]{2,1,0:T(4,128)(2,1)S(1)}, u32[]{:S(2)}, u32[]{:S(2)}) async-start(bf16[64,4,144]{2,1,0:T(4,128)(2,1)} %broadcast_select_fusion.1), calls=%async_computation.1 | async-start | bytes 262144 | tf_op jit(solution)/shard_map/all_to_all | solution.py:45
  117.3 1.6 copy-start.6
  117.3 20.6 %copy-start.9 = (s32[64]{0:T(128)S(1)}, s32[64]{0:T(128)}, u32[]{:S(2)}) copy-start(s32[64]{0:T(128)} %compare_select_fusion) | copy-start | bytes 772
  117.3 20.6 %copy-start.7 = (f32[256]{0:T(256)S(1)}, f32[256]{0:T(256)}, u32[]{:S(2)}) copy-start(f32[256]{0:T(256)} %get-tuple-element.22) | copy-start | bytes 3076
  117.3 20.6 %copy-start.8 = (f32[256]{0:T(256)S(1)}, f32[256]{0:T(256)}, u32[]{:S(2)}) copy-start(f32[256]{0:T(256)} %get-tuple-element.23) | copy-start | bytes 3076
  118.0 20.8 %copy-start.5 = (f32[144]{0:T(256)S(1)}, f32[144]{0:T(256)}, u32[]{:S(2)}) copy-start(f32[144]{0:T(256)} %param.26) | copy-start | bytes 1732
  131.2 22.0 %all-to-all-start.1 = ((bf16[64,4,384]{2,1,0:T(4,128)(2,1)}), bf16[64,4,384]{2,1,0:T(4,128)(2,1)S(1)}, u32[]{:S(2)}, u32[]{:S(2)}) async-start(bf16[64,4,384]{2,1,0:T(4,128)(2,1)} %broadcast_select_fusion), calls=%async_computation.2 | async-start | bytes 393216 | tf_op jit(solution)/shard_map/all_to_all | solution.py:46
  138.6 15.7 %copy-start.4 = (f32[384]{0:T(512)S(1)}, f32[384]{0:T(512)}, u32[]{:S(2)}) copy-start(f32[384]{0:T(512)} %param.27) | copy-start | bytes 4612
Sparse Core Ops, SparseCore 0:
  11.2 55.0 all-gather.1
  72.2 275.8 reduce-scatter.1
where the time goes:
time: 358 us; the launch traced here: 357 us
  waiting for transfers between devices  258 us (72%)
  blocking collectives  31.4 us (9%)
  starting transfers between devices  23.4 us (7%)
  other arithmetic  14.8 us (4%)
  between operations  14.3 us (4%)
  local copies, waits for them, and re-layouts  8.73 us (2%)
  matrix products  6.53 us (2%)
    reduce_scatter x1, waiting for transfers between devices, shards(): lax.psum_scatter(lax.dot_general(full_grad, features, (((0,), (0,)), ((),...  177 us
    all_gather x1, waiting for transfers between devices, shards(): full_grad = lax.all_gather(masked, 'enc', axis=1, tiled=True)  55.4 us
    psum x1, blocking collectives, shards(): lax.psum((jnp.sum(siglip_height, axis=1), jnp.sum(siglip_height * siglip_...  17.3 us
    all_to_all x1, starting transfers between devices, shards(): lax.all_to_all(send_sig, 'dp', split_axis=0, concat_axis=0, tiled=True)  16.7 us
    psum x1, blocking collectives, shards(): lax.psum((jnp.sum(siglip_scaled_gradient, axis=1), jnp.sum(siglip_scaled_...  14.2 us
    all_to_all x1, waiting for transfers between devices, shards(): lax.all_to_all(send_cnx, 'dp', split_axis=0, concat_axis=0, tiled=True)  13.7 us
    all_to_all x1, waiting for transfers between devices, shards(): lax.all_to_all(send_sig, 'dp', split_axis=0, concat_axis=0, tiled=True)  11.4 us
  transfers between devices with their start and end apart: 4, of which 4 were waited for; matrix products, arithmetic and copies ran while one was open for 6% of the time, Pallas kernels for 0%

commit v1 on v0

v1 whole, which is shorter than its diff:
```python
import math

import jax
import jax.numpy as jnp
from jax import lax
from jax.sharding import Mesh
from jax.sharding import PartitionSpec as P

EPS = 1e-06
F32 = jnp.float32
BF16 = jnp.bfloat16


def shift(count, step):
    return [(i, (i + step) % count) for i in range(count)]


def broadcast_gather(block, axis):
    count = lax.axis_size(axis)
    copies = jnp.broadcast_to(block[None], (count,) + block.shape)
    return lax.all_to_all(copies, axis, 0, 0, tiled=True)


def reduce_stage(part, axis):
    count = lax.axis_size(axis)
    here = lax.axis_index(axis)
    rounded = part.astype(BF16)
    received = []
    for step in range(1, count):
        target = lax.rem(here + step, count)
        block = lax.dynamic_index_in_dim(rounded, target, 0, keepdims=False)
        received.append(lax.ppermute(block, axis, shift(count, step)))
    total = lax.dynamic_index_in_dim(part, here, 0, keepdims=False)
    for block in received:
        total = total + block.astype(F32)
    return total


def hand_on(blocks, axis):
    count = lax.axis_size(axis)
    return [blocks[0]] + [lax.ppermute(blocks[k], axis, shift(count, k)) for k in range(1, count)]


def pick(chosen, source):
    return jnp.dot(chosen.astype(BF16), source, preferred_element_type=F32).astype(BF16)


def shards(
    feat_sig,
    feat_cnx,
    cotangent,
    w_sig,
    w_cnx,
    lengths,
    enc_of,
    owner_of,
    pre_sig,
    pre_cnx,
    gain_sig,
    gain_cnx,
):
    slots = lengths.shape[1]
    rows, cols = cotangent.shape
    depth = rows // slots
    enc_count = lax.axis_size("enc")
    rep_count = lax.axis_size("rep")
    nx, nh, nl = (lax.axis_size(name) for name in ("x", "zh", "zl"))
    core = lax.axis_index("rep")
    swap = shift(rep_count, 1)

    features = jnp.concatenate([feat_cnx, feat_sig], axis=1)
    other_features = lax.ppermute(features, "rep", swap)
    live_t = lax.broadcasted_iota(jnp.int32, (slots, depth), 1) < lengths[0][:, None]
    live_t = live_t.reshape(1, rows)
    turned = jnp.where(live_t, cotangent.T, jnp.zeros((), BF16))
    piece = cols // (slots // enc_count) // rep_count
    turned = turned.reshape(slots // enc_count, rep_count, piece, rows)
    mine = lax.dynamic_index_in_dim(turned, core, 1, keepdims=False).reshape(cols // rep_count, rows)
    theirs = lax.dynamic_index_in_dim(turned, 1 - core, 1, keepdims=False).reshape(cols // rep_count, rows)
    theirs = lax.ppermute(theirs, "rep", swap)
    paired = jnp.stack([mine, theirs])
    all_paired = broadcast_gather(paired, "enc")

    hx, hh, hl = (lax.axis_index(name) for name in ("x", "zh", "zl"))
    token = lax.broadcasted_iota(jnp.int32, (slots, depth), 1)
    goal = enc_of[0]
    kx, kh, kl = (goal // (nh * nl) - hx) % nx, (goal // nl - hh) % nh, (goal - hl) % nl
    goal = (((kx * nh + kh) * nl + kl) * depth)[:, None] + token
    goal = jnp.where(token < lengths[0][:, None], goal, -1).reshape(1, rows)
    row = lax.broadcasted_iota(jnp.int32, (rows, rows), 0)
    column = lax.broadcasted_iota(jnp.int32, (rows, rows), 1)
    held = pick(row == goal, cotangent)
    held = jnp.concatenate(hand_on(jnp.split(held, nx), "x"))
    unit = row // depth
    unit = (unit % nx * nh + unit // nx % nh) * nl + unit // (nx * nh)
    held = pick(column == unit * depth + row % depth, held)
    held = hand_on(jnp.split(held, nl), "zl")
    held = [jnp.split(block, nh) for block in held]
    held = [jnp.concatenate([block[k] for block in held]) for k in range(nh)]
    held = jnp.concatenate(hand_on(held, "zh"))
    sender = owner_of[0]
    kx, kh, kl = (hx - sender // (nh * nl)) % nx, (hh - sender // nl) % nh, (hl - sender) % nl
    place = ((((kh * nl + kl) * nx + kx) * depth)[:, None] + token).reshape(rows, 1)
    routed = pick(column == place, held)
    routed, other_features = lax.optimization_barrier((routed, other_features))
    full = broadcast_gather(routed, "enc")

    parts = all_paired.reshape(enc_count, rep_count, cols // rep_count, rows)
    contract = (((1,), (0,)), ((), ()))
    half = enc_count * cols // rep_count
    partial = lax.dot_general(
        parts[:, 0].reshape(half, rows), features, contract, preferred_element_type=F32
    ) + lax.dot_general(
        parts[:, 1].reshape(half, rows), other_features, contract, preferred_element_type=F32
    )
    width = features.shape[1]
    total = reduce_stage(partial.reshape(nx, half // nx, width), "x")
    total = total.reshape(nh, nl, piece, width).transpose(1, 0, 2, 3).reshape(nl, nh * piece, width)
    total = reduce_stage(total, "zl")
    full, total = lax.optimization_barrier((full, total))
    total = reduce_stage(total.reshape(nh, piece, width), "zh")
    scale = 1.0 / math.sqrt(rows * nx * nh * nl * rep_count)
    total = total * scale
    split = feat_cnx.shape[1]

    full = full.transpose(1, 0, 2).reshape(rows, enc_count * cols)
    sums = []
    kept = []
    for weight, gain, pre in ((w_sig, gain_sig, pre_sig), (w_cnx, gain_cnx, pre_cnx)):
        dy = jnp.dot(full, weight, preferred_element_type=F32).astype(BF16)
        height = pre.astype(F32)
        scaled = dy.astype(F32) * gain
        kept.append((height, scaled, gain.shape[0] * enc_count))
        sums += [
            jnp.sum(height, axis=1),
            jnp.sum(height * height, axis=1),
            jnp.sum(scaled, axis=1),
            jnp.sum(scaled * height, axis=1),
        ]
    sums = jnp.sum(broadcast_gather(jnp.stack(sums), "enc").reshape(enc_count, 8, rows), axis=0)
    grads = []
    for index, (height, scaled, channels) in enumerate(kept):
        means = sums[index * 4 : index * 4 + 4] / channels
        mean = means[0]
        inverse = lax.rsqrt(means[1] - mean * mean + EPS)
        product = inverse * (means[3] - mean * means[2])
        grads.append(
            (
                inverse[:, None]
                * (scaled - means[2][:, None] - (height - mean[:, None]) * inverse[:, None] * product[:, None])
            ).astype(BF16)
        )
    return (total[:, split:], total[:, :split], grads[0], grads[1])


def solution(mesh):
    enc, dp, rep = mesh.devices.shape
    digit = round(dp ** (1 / 3))
    mesh = Mesh(
        mesh.devices.reshape(enc, dp // digit**2, digit, digit, rep), ("enc", "x", "zh", "zl", "rep")
    )
    owners = ("x", "zh", "zl", "rep")
    both = P(owners, "enc")
    in_specs = (
        both,
        both,
        both,
        P(None, "enc"),
        P(None, "enc"),
        P(owners, None),
        P(owners, None),
        P(owners, None),
        both,
        both,
        P("enc"),
        P("enc"),
    )
    return jax.shard_map(
        shards, mesh=mesh, in_specs=in_specs, out_specs=(both,) * 4, check_vma=False
    )
```

time: 358 us -> 171 us (0.48)
  waiting for transfers between devices: 258 us -> 22.2 us
  starting transfers between devices: 23.4 us -> 113 us
  blocking collectives: 31.4 us -> 0 us
  between operations: 14.3 us -> 1.37 us
  local copies, waits for them, and re-layouts: 8.73 us -> 18.4 us
  other arithmetic: 14.8 us -> 9.01 us
    reduce_scatter x1 -> x0, waiting for transfers between devices: 177 us -> none  [shards(): lax.psum_scatter(lax.dot_general(full_grad, features, (((0,), (0,)), ((),...]
    ppermute x0 -> x20, starting transfers between devices: none -> 95.1 us  [the longest x9 52.3 us: hand_on(): lax.ppermute(blocks[k], axis, shift(count, k))]
    all_gather x1 -> x0, waiting for transfers between devices: 55.4 us -> none  [shards(): full_grad = lax.all_gather(masked, 'enc', axis=1, tiled=True)]
    psum x2 -> x0, blocking collectives: 31.4 us -> none  [the longest x1 17.3 us: shards(): lax.psum((jnp.sum(siglip_height, axis=1), jnp.sum(siglip_height * siglip_...]
    all_to_all x2 -> x3, waiting for transfers between devices: 25.2 us -> 6.39 us  [broadcast_gather(): return lax.all_to_all(copies, axis, 0, 0, tiled=True)]
    ppermute x0 -> x20, waiting for transfers between devices: none -> 15.8 us  [the longest x9 7.89 us: hand_on(): lax.ppermute(blocks[k], axis, shift(count, k))]
    select_n x5 -> x2, other arithmetic: 5.88 us -> 0.02 us  [the longest x1 0.02 us: shards(): turned = jnp.where(live_t, cotangent.T, jnp.zeros((), BF16))]
    all_to_all x2 -> x3, starting transfers between devices: 23.3 us -> 17.7 us  [broadcast_gather(): return lax.all_to_all(copies, axis, 0, 0, tiled=True)]
  transfers between devices with their start and end apart: 4 -> 23, of which waited for: 4 -> 8; matrix products, arithmetic and copies ran while one was open for 6% -> 15% of each run, Pallas kernels for 0% -> 0%
where the time goes in v1:
time: 171 us; the launch traced here: 170 us
  starting transfers between devices  113 us (66%)
  waiting for transfers between devices  22.2 us (13%)
  local copies, waits for them, and re-layouts  18.4 us (11%)
  other arithmetic  9.01 us (5%)
  matrix products  6.36 us (4%)
    ppermute x9, starting transfers between devices, hand_on(): lax.ppermute(blocks[k], axis, shift(count, k))  52.3 us
    ppermute x9, starting transfers between devices, reduce_stage(): received.append(lax.ppermute(block, axis, shift(count, step)))  38.5 us
    all_to_all x3, starting transfers between devices, broadcast_gather(): return lax.all_to_all(copies, axis, 0, 0, tiled=True)  17.7 us
    ppermute x9, waiting for transfers between devices, hand_on(): lax.ppermute(blocks[k], axis, shift(count, k))  7.89 us
    ppermute x9, waiting for transfers between devices, reduce_stage(): received.append(lax.ppermute(block, axis, shift(count, step)))  7.8 us
    all_to_all x3, waiting for transfers between devices, broadcast_gather(): return lax.all_to_all(copies, axis, 0, 0, tiled=True)  6.39 us
    dot_general x2, matrix products, shards(): dy = jnp.dot(full, weight, preferred_element_type=F32).astype(BF16)  3.56 us
    reshape x2, local copies, waits for them, and re-layouts, shards(): total = reduce_stage(partial.reshape(nx, half // nx, width), 'x')  3.48 us
  transfers between devices with their start and end apart: 23, of which 8 were waited for; matrix products, arithmetic and copies ran while one was open for 15% of the time, Pallas kernels for 0%

profile of v1, /device:TPU:6, one launch (start us, length us, event | category | flops | bytes accessed | tf_op | source)
XLA Modules:
  0.0 170.2 jit_solution(9385614167261229882)
XLA Ops:
  3.6 15.0 %collective-permute-start = (bf16[64,256]{1,0:T(8,128)(2,1)S(1)}, bf16[64,256]{1,0:T(8,128)(2,1)S(1)}, u32[]{:S(2)}, u32[]{:S(2)}) collective-permute-start(bf16[64,256]{1,0:T(8,128)(2,1)S(1)} %get-tuple-element.40), channel_id=1, source_target_pairs={{0,32},{32,64},{64,96},{96,0},{1,33},{33,65},{65,97},{97,1},{2,34}... | collective-permute-start | bytes 98312 | tf_op jit(solution)/shard_map/ppermute | solution.py:41
  18.7 1.9 %collective-permute-start.1 = (bf16[64,256]{1,0:T(8,128)(2,1)S(1)}, bf16[64,256]{1,0:T(8,128)(2,1)S(1)}, u32[]{:S(2)}, u32[]{:S(2)}) collective-permute-start(bf16[64,256]{1,0:T(8,128)(2,1)S(1)} %get-tuple-element.39), channel_id=1, source_target_pairs={{0,64},{32,96},{64,0},{96,32},{1,65},{33,97},{65,1},{97,33},{2,66}... | collective-permute-start | bytes 98312 | tf_op jit(solution)/shard_map/ppermute | solution.py:41
  20.6 2.8 %collective-permute-start.2 = (bf16[64,256]{1,0:T(8,128)(2,1)S(1)}, bf16[64,256]{1,0:T(8,128)(2,1)S(1)}, u32[]{:S(2)}, u32[]{:S(2)}) collective-permute-start(bf16[64,256]{1,0:T(8,128)(2,1)S(1)} %get-tuple-element.38), channel_id=1, source_target_pairs={{0,96},{32,0},{64,32},{96,64},{1,97},{33,1},{65,33},{97,65},{2,98}... | collective-permute-start | bytes 98312 | tf_op jit(solution)/shard_map/ppermute | solution.py:41
  26.1 1.9 %collective-permute-start.9 = (bf16[256,528]{1,0:T(8,128)(2,1)}, bf16[256,528]{1,0:T(8,128)(2,1)S(1)}, u32[]{:S(2)}, u32[]{:S(2)}) collective-permute-start(bf16[256,528]{1,0:T(8,128)(2,1)} %pad_maximum_fusion), channel_id=1, source_target_pairs={{0,1},{1,0},{2,3},{3,2},{4,5},{5,4},{6,7},{7,6},{8,9},{9,8},{10,11... | collective-permute-start | bytes 811016 | tf_op jit(solution)/shard_map/ppermute | solution.py:72
  29.1 2.4 %collective-permute-start.10 = (bf16[128,256]{1,0:T(8,128)(2,1)S(1)}, bf16[128,256]{1,0:T(8,128)(2,1)S(1)}, u32[]{:S(2)}, u32[]{:S(2)}) collective-permute-start(bf16[128,256]{1,0:T(8,128)(2,1)S(1)} %bitcast.141), channel_id=1, source_target_pairs={{0,1},{1,0},{2,3},{3,2},{4,5},{5,4},{6,7},{7,6},{8,9},{9,8},{10,11... | collective-permute-start | bytes 196616 | tf_op jit(solution)/shard_map/ppermute | solution.py:80
  33.5 3.6 %all-to-all-start.1 = ((bf16[8,2,128,256]{3,2,1,0:T(8,128)(2,1)}), bf16[8,2,128,256]{3,2,1,0:T(8,128)(2,1)S(1)}, u32[]{:S(2)}, u32[]{:S(2)}) async-start(bf16[8,2,128,256]{3,2,1,0:T(8,128)(2,1)} %broadcast_in_dim.23), calls=%async_computation.1 | async-start | bytes 2097152 | tf_op jit(solution)/shard_map/all_to_all | solution.py:21
  37.1 1.9 %collective-permute-start.3 = (bf16[64,256]{1,0:T(8,128)(2,1)S(1)}, bf16[64,256]{1,0:T(8,128)(2,1)S(1)}, u32[]{:S(2)}, u32[]{:S(2)}) collective-permute-start(bf16[64,256]{1,0:T(8,128)(2,1)S(1)} %get-tuple-element.36), channel_id=1, source_target_pairs={{0,2},{2,4},{4,6},{6,0},{1,3},{3,5},{5,7},{7,1},{8,10},{10,12},{12... | collective-permute-start | bytes 98312 | tf_op jit(solution)/shard_map/ppermute | solution.py:41
  39.0 1.9 %collective-permute-start.4 = (bf16[64,256]{1,0:T(8,128)(2,1)S(1)}, bf16[64,256]{1,0:T(8,128)(2,1)S(1)}, u32[]{:S(2)}, u32[]{:S(2)}) collective-permute-start(bf16[64,256]{1,0:T(8,128)(2,1)S(1)} %get-tuple-element.35), channel_id=1, source_target_pairs={{0,4},{2,6},{4,0},{6,2},{1,5},{3,7},{5,1},{7,3},{8,12},{10,14},{12... | collective-permute-start | bytes 98312 | tf_op jit(solution)/shard_map/ppermute | solution.py:41
  40.9 5.7 %collective-permute-start.5 = (bf16[64,256]{1,0:T(8,128)(2,1)S(1)}, bf16[64,256]{1,0:T(8,128)(2,1)S(1)}, u32[]{:S(2)}, u32[]{:S(2)}) collective-permute-start(bf16[64,256]{1,0:T(8,128)(2,1)S(1)} %get-tuple-element.34), channel_id=1, source_target_pairs={{0,6},{2,0},{4,2},{6,4},{1,7},{3,1},{5,3},{7,5},{8,14},{10,8},{12,... | collective-permute-start | bytes 98312 | tf_op jit(solution)/shard_map/ppermute | solution.py:41
  46.7 2.4 %collective-permute-done.5 = bf16[64,256]{1,0:T(8,128)(2,1)S(1)} collective-permute-done((bf16[64,256]{1,0:T(8,128)(2,1)S(1)}, bf16[64,256]{1,0:T(8,128)(2,1)S(1)}, u32[]{:S(2)}, u32[]{:S(2)}) %collective-permute-start.5) | collective-permute-done | bytes 32800 | tf_op jit(solution)/shard_map/ppermute | solution.py:41
  49.1 12.1 %collective-permute-start.8 = (bf16[64,256]{1,0:T(8,128)(2,1)S(1)}, bf16[64,256]{1,0:T(8,128)(2,1)S(1)}, u32[]{:S(2)}, u32[]{:S(2)}) collective-permute-start(bf16[64,256]{1,0:T(8,128)(2,1)S(1)} %pad_maximum_fusion.4), channel_id=1, source_target_pairs={{0,24},{8,0},{16,8},{24,16},{1,25},{9,1},{17,9},{25,17},{2,26},{10... | collective-permute-start | bytes 98312 | tf_op jit(solution)/shard_map/ppermute | solution.py:41
  61.2 1.9 %collective-permute-start.6 = (bf16[64,256]{1,0:T(8,128)(2,1)S(1)}, bf16[64,256]{1,0:T(8,128)(2,1)S(1)}, u32[]{:S(2)}, u32[]{:S(2)}) collective-permute-start(bf16[64,256]{1,0:T(8,128)(2,1)S(1)} %pad_maximum_fusion.2), channel_id=1, source_target_pairs={{0,8},{8,16},{16,24},{24,0},{1,9},{9,17},{17,25},{25,1},{2,10},{10... | collective-permute-start | bytes 98312 | tf_op jit(solution)/shard_map/ppermute | solution.py:41
  63.2 9.0 %collective-permute-start.7 = (bf16[64,256]{1,0:T(8,128)(2,1)S(1)}, bf16[64,256]{1,0:T(8,128)(2,1)S(1)}, u32[]{:S(2)}, u32[]{:S(2)}) collective-permute-start(bf16[64,256]{1,0:T(8,128)(2,1)S(1)} %pad_maximum_fusion.3), channel_id=1, source_target_pairs={{0,16},{8,24},{16,0},{24,8},{1,17},{9,25},{17,1},{25,9},{2,18},{10... | collective-permute-start | bytes 98312 | tf_op jit(solution)/shard_map/ppermute | solution.py:41
  72.2 5.5 %collective-permute-done.7 = bf16[64,256]{1,0:T(8,128)(2,1)S(1)} collective-permute-done((bf16[64,256]{1,0:T(8,128)(2,1)S(1)}, bf16[64,256]{1,0:T(8,128)(2,1)S(1)}, u32[]{:S(2)}, u32[]{:S(2)}) %collective-permute-start.7) | collective-permute-done | bytes 32800 | tf_op jit(solution)/shard_map/ppermute | solution.py:41
  79.4 7.2 %all-to-all-start = ((bf16[8,256,256]{1,2,0:T(8,128)(2,1)}), bf16[8,256,256]{1,2,0:T(8,128)(2,1)S(1)}, u32[]{:S(2)}, u32[]{:S(2)}) async-start(bf16[8,256,256]{1,2,0:T(8,128)(2,1)} %broadcast_in_dim.20), calls=%async_computation | async-start | bytes 2097152 | tf_op jit(solution)/shard_map/all_to_all | solution.py:21
  90.3 5.1 %collective-permute-start.11 = (bf16[256,528]{0,1:T(8,128)(2,1)S(1)}, bf16[256,528]{0,1:T(8,128)(2,1)}, u32[]{:S(2)}, u32[]{:S(2)}) collective-permute-start(bf16[256,528]{0,1:T(8,128)(2,1)S(1)} %get-tuple-element.20), channel_id=1, source_target_pairs={{0,32},{32,64},{64,96},{96,0},{1,33},{33,65},{65,97},{97,1},{2,34}... | collective-permute-start | bytes 811016 | tf_op jit(solution)/shard_map/ppermute | solution.py:32
  95.4 2.0 %collective-permute-start.12 = (bf16[256,528]{0,1:T(8,128)(2,1)S(1)}, bf16[256,528]{0,1:T(8,128)(2,1)}, u32[]{:S(2)}, u32[]{:S(2)}) collective-permute-start(bf16[256,528]{0,1:T(8,128)(2,1)S(1)} %get-tuple-element.22), channel_id=1, source_target_pairs={{0,64},{32,96},{64,0},{96,32},{1,65},{33,97},{65,1},{97,33},{2,66}... | collective-permute-start | bytes 811016 | tf_op jit(solution)/shard_map/ppermute | solution.py:32
  97.4 3.3 %collective-permute-start.13 = (bf16[256,528]{0,1:T(8,128)(2,1)S(1)}, bf16[256,528]{0,1:T(8,128)(2,1)}, u32[]{:S(2)}, u32[]{:S(2)}) collective-permute-start(bf16[256,528]{0,1:T(8,128)(2,1)S(1)} %get-tuple-element.21), channel_id=1, source_target_pairs={{0,96},{32,0},{64,32},{96,64},{1,97},{33,1},{65,33},{97,65},{2,98}... | collective-permute-start | bytes 811016 | tf_op jit(solution)/shard_map/ppermute | solution.py:32
  100.7 3.4 %reshape.327 = f32[4,256,528]{1,0,2:T(4,128)} reshape(f32[1024,528]{0,1:T(8,128)} %copy-done.1) | data formatting | bytes 4325376 | tf_op jit(solution)/shard_map/reshape | solution.py:117
  104.1 2.1 %constant_dynamic-slice_fusion = f32[1,256,528]{1,0,2:T(1,128)S(1)} fusion(f32[4,256,528]{1,0,2:T(4,128)} %reshape.327, s32[]{:T(128)S(6)} %select_n.191), kind=kLoop, calls=%fused_computation.123 | loop fusion | bytes 1081348 | tf_op jit(solution)/shard_map/jit(dynamic_index_in_dim)/dynamic_slice | solution.py:33
  106.7 2.8 %collective-permute-done.13 = bf16[256,528]{0,1:T(8,128)(2,1)} collective-permute-done((bf16[256,528]{0,1:T(8,128)(2,1)S(1)}, bf16[256,528]{0,1:T(8,128)(2,1)}, u32[]{:S(2)}, u32[]{:S(2)}) %collective-permute-start.13) | collective-permute-done | bytes 270368 | tf_op jit(solution)/shard_map/ppermute | solution.py:32
  113.7 2.6 %collective-permute-start.14 = (bf16[64,528]{1,0:T(8,128)(2,1)}, bf16[64,528]{1,0:T(8,128)(2,1)}, u32[]{:S(2)}, u32[]{:S(2)}) collective-permute-start(bf16[64,528]{1,0:T(8,128)(2,1)} %get-tuple-element.25), channel_id=1, source_target_pairs={{0,2},{2,4},{4,6},{6,0},{1,3},{3,5},{5,7},{7,1},{8,10},{10,12},{12... | collective-permute-start | bytes 202760 | tf_op jit(solution)/shard_map/ppermute | solution.py:32
  116.2 5.2 %collective-permute-start.15 = (bf16[64,528]{1,0:T(8,128)(2,1)S(1)}, bf16[64,528]{1,0:T(8,128)(2,1)}, u32[]{:S(2)}, u32[]{:S(2)}) collective-permute-start(bf16[64,528]{1,0:T(8,128)(2,1)S(1)} %get-tuple-element.27), channel_id=1, source_target_pairs={{0,4},{2,6},{4,0},{6,2},{1,5},{3,7},{5,1},{7,3},{8,12},{10,14},{12... | collective-permute-start | bytes 202760 | tf_op jit(solution)/shard_map/ppermute | solution.py:32
  121.5 1.9 %collective-permute-start.16 = (bf16[64,528]{1,0:T(8,128)(2,1)S(1)}, bf16[64,528]{1,0:T(8,128)(2,1)}, u32[]{:S(2)}, u32[]{:S(2)}) collective-permute-start(bf16[64,528]{1,0:T(8,128)(2,1)S(1)} %get-tuple-element.26), channel_id=1, source_target_pairs={{0,6},{2,0},{4,2},{6,4},{1,7},{3,1},{5,3},{7,5},{8,14},{10,8},{12,... | collective-permute-start | bytes 202760 | tf_op jit(solution)/shard_map/ppermute | solution.py:32
  123.4 2.2 %collective-permute-done.15 = bf16[64,528]{1,0:T(8,128)(2,1)} collective-permute-done((bf16[64,528]{1,0:T(8,128)(2,1)S(1)}, bf16[64,528]{1,0:T(8,128)(2,1)}, u32[]{:S(2)}, u32[]{:S(2)}) %collective-permute-start.15) | collective-permute-done | bytes 67616 | tf_op jit(solution)/shard_map/ppermute | solution.py:32
  125.6 2.3 %collective-permute-done.16 = bf16[64,528]{1,0:T(8,128)(2,1)} collective-permute-done((bf16[64,528]{1,0:T(8,128)(2,1)S(1)}, bf16[64,528]{1,0:T(8,128)(2,1)}, u32[]{:S(2)}, u32[]{:S(2)}) %collective-permute-start.16) | collective-permute-done | bytes 67616 | tf_op jit(solution)/shard_map/ppermute | solution.py:32
  129.6 3.6 %collective-permute-start.17 = (bf16[16,528]{1,0:T(8,128)(2,1)}, bf16[16,528]{1,0:T(8,128)(2,1)S(1)}, u32[]{:S(2)}, u32[]{:S(2)}) collective-permute-start(bf16[16,528]{1,0:T(8,128)(2,1)} %get-tuple-element.41), channel_id=1, source_target_pairs={{0,8},{8,16},{16,24},{24,0},{1,9},{9,17},{17,25},{25,1},{2,10},{10... | collective-permute-start | bytes 50696 | tf_op jit(solution)/shard_map/ppermute | solution.py:32
  133.2 11.6 %collective-permute-start.18 = (bf16[16,528]{1,0:T(8,128)(2,1)}, bf16[16,528]{1,0:T(8,128)(2,1)S(1)}, u32[]{:S(2)}, u32[]{:S(2)}) collective-permute-start(bf16[16,528]{1,0:T(8,128)(2,1)} %get-tuple-element.43), channel_id=1, source_target_pairs={{0,16},{8,24},{16,0},{24,8},{1,17},{9,25},{17,1},{25,9},{2,18},{10... | collective-permute-start | bytes 50696 | tf_op jit(solution)/shard_map/ppermute | solution.py:32
  144.8 3.2 %collective-permute-start.19 = (bf16[16,528]{1,0:T(8,128)(2,1)}, bf16[16,528]{1,0:T(8,128)(2,1)}, u32[]{:S(2)}, u32[]{:S(2)}) collective-permute-start(bf16[16,528]{1,0:T(8,128)(2,1)} %get-tuple-element.42), channel_id=1, source_target_pairs={{0,24},{8,0},{16,8},{24,16},{1,25},{9,1},{17,9},{25,17},{2,26},{10... | collective-permute-start | bytes 50696 | tf_op jit(solution)/shard_map/ppermute | solution.py:32
  148.1 1.9 %fusion.7 = (f32[256]{0:T(256)S(1)}, f32[256]{0:T(256)S(1)}, f32[256]{0:T(256)S(1)}, f32[256]{0:T(256)S(1)}, f32[256,384]{1,0:T(8,128)S(1)}) fusion(bf16[256,384]{1,0:T(8,128)(2,1)} %param.21, f32[384]{0:T(512)} %param.23, bf16[256,2048]{0,1:T(8,128)(2,1)S(1)} %bitcast.130, bf16[2048,384]{1,0:T(8,128)(2,1)S(1)} %copy-done), kind=kOutput, calls=%fused_computation.23 | convolution fusion | flops 403635200 | bytes 3216896 | tf_op jit(solution)/shard_map/dot_general | solution.py:130
  152.3 6.9 %all-to-all-start.2 = ((f32[8,8,256]{2,1,0:T(8,128)}), f32[8,8,256]{2,1,0:T(8,128)S(1)}, u32[]{:S(2)}, u32[]{:S(2)}) async-start(f32[8,8,256]{2,1,0:T(8,128)} %broadcast_in_dim.24), calls=%async_computation.2 | async-start | bytes 131072 | tf_op jit(solution)/shard_map/all_to_all | solution.py:21
  161.2 6.4 %all-to-all-done.2 = f32[8,8,256]{2,1,0:T(8,128)S(1)} async-done(((f32[8,8,256]{2,1,0:T(8,128)}), f32[8,8,256]{2,1,0:T(8,128)S(1)}, u32[]{:S(2)}, u32[]{:S(2)}) %all-to-all-start.2) | async-done | bytes 65568 | tf_op jit(solution)/shard_map/all_to_all | solution.py:21
  (93 shorter events, 27.1 us)
Async XLA Ops:
  0.6 147.4 %copy-start = (bf16[2048,384]{1,0:T(8,128)(2,1)S(1)}, bf16[2048,384]{1,0:T(8,128)(2,1)}, u32[]{:S(2)}) copy-start(bf16[2048,384]{1,0:T(8,128)(2,1)} %param.16) | copy-start | bytes 4718596
  3.6 28.1 %collective-permute-start = (bf16[64,256]{1,0:T(8,128)(2,1)S(1)}, bf16[64,256]{1,0:T(8,128)(2,1)S(1)}, u32[]{:S(2)}, u32[]{:S(2)}) collective-permute-start(bf16[64,256]{1,0:T(8,128)(2,1)S(1)} %get-tuple-element.40), channel_id=1, source_target_pairs={{0,32},{32,64},{64,96},{96,0},{1,33},{33,65},{65,97},{97,1},{2,34}... | collective-permute-start | bytes 98312 | tf_op jit(solution)/shard_map/ppermute | solution.py:41
  18.7 13.0 %collective-permute-start.1 = (bf16[64,256]{1,0:T(8,128)(2,1)S(1)}, bf16[64,256]{1,0:T(8,128)(2,1)S(1)}, u32[]{:S(2)}, u32[]{:S(2)}) collective-permute-start(bf16[64,256]{1,0:T(8,128)(2,1)S(1)} %get-tuple-element.39), channel_id=1, source_target_pairs={{0,64},{32,96},{64,0},{96,32},{1,65},{33,97},{65,1},{97,33},{2,66}... | collective-permute-start | bytes 98312 | tf_op jit(solution)/shard_map/ppermute | solution.py:41
  20.6 11.1 %collective-permute-start.2 = (bf16[64,256]{1,0:T(8,128)(2,1)S(1)}, bf16[64,256]{1,0:T(8,128)(2,1)S(1)}, u32[]{:S(2)}, u32[]{:S(2)}) collective-permute-start(bf16[64,256]{1,0:T(8,128)(2,1)S(1)} %get-tuple-element.38), channel_id=1, source_target_pairs={{0,96},{32,0},{64,32},{96,64},{1,97},{33,1},{65,33},{97,65},{2,98}... | collective-permute-start | bytes 98312 | tf_op jit(solution)/shard_map/ppermute | solution.py:41
  26.1 51.9 %collective-permute-start.9 = (bf16[256,528]{1,0:T(8,128)(2,1)}, bf16[256,528]{1,0:T(8,128)(2,1)S(1)}, u32[]{:S(2)}, u32[]{:S(2)}) collective-permute-start(bf16[256,528]{1,0:T(8,128)(2,1)} %pad_maximum_fusion), channel_id=1, source_target_pairs={{0,1},{1,0},{2,3},{3,2},{4,5},{5,4},{6,7},{7,6},{8,9},{9,8},{10,11... | collective-permute-start | bytes 811016 | tf_op jit(solution)/shard_map/ppermute | solution.py:72
  29.1 3.3 %collective-permute-start.10 = (bf16[128,256]{1,0:T(8,128)(2,1)S(1)}, bf16[128,256]{1,0:T(8,128)(2,1)S(1)}, u32[]{:S(2)}, u32[]{:S(2)}) collective-permute-start(bf16[128,256]{1,0:T(8,128)(2,1)S(1)} %bitcast.141), channel_id=1, source_target_pairs={{0,1},{1,0},{2,3},{3,2},{4,5},{5,4},{6,7},{7,6},{8,9},{9,8},{10,11... | collective-permute-start | bytes 196616 | tf_op jit(solution)/shard_map/ppermute | solution.py:80
  33.5 44.6 %all-to-all-start.1 = ((bf16[8,2,128,256]{3,2,1,0:T(8,128)(2,1)}), bf16[8,2,128,256]{3,2,1,0:T(8,128)(2,1)S(1)}, u32[]{:S(2)}, u32[]{:S(2)}) async-start(bf16[8,2,128,256]{3,2,1,0:T(8,128)(2,1)} %broadcast_in_dim.23), calls=%async_computation.1 | async-start | bytes 2097152 | tf_op jit(solution)/shard_map/all_to_all | solution.py:21
  37.1 9.6 %collective-permute-start.3 = (bf16[64,256]{1,0:T(8,128)(2,1)S(1)}, bf16[64,256]{1,0:T(8,128)(2,1)S(1)}, u32[]{:S(2)}, u32[]{:S(2)}) collective-permute-start(bf16[64,256]{1,0:T(8,128)(2,1)S(1)} %get-tuple-element.36), channel_id=1, source_target_pairs={{0,2},{2,4},{4,6},{6,0},{1,3},{3,5},{5,7},{7,1},{8,10},{10,12},{12... | collective-permute-start | bytes 98312 | tf_op jit(solution)/shard_map/ppermute | solution.py:41
  39.0 7.7 %collective-permute-start.4 = (bf16[64,256]{1,0:T(8,128)(2,1)S(1)}, bf16[64,256]{1,0:T(8,128)(2,1)S(1)}, u32[]{:S(2)}, u32[]{:S(2)}) collective-permute-start(bf16[64,256]{1,0:T(8,128)(2,1)S(1)} %get-tuple-element.35), channel_id=1, source_target_pairs={{0,4},{2,6},{4,0},{6,2},{1,5},{3,7},{5,1},{7,3},{8,12},{10,14},{12... | collective-permute-start | bytes 98312 | tf_op jit(solution)/shard_map/ppermute | solution.py:41
  40.9 8.2 %collective-permute-start.5 = (bf16[64,256]{1,0:T(8,128)(2,1)S(1)}, bf16[64,256]{1,0:T(8,128)(2,1)S(1)}, u32[]{:S(2)}, u32[]{:S(2)}) collective-permute-start(bf16[64,256]{1,0:T(8,128)(2,1)S(1)} %get-tuple-element.34), channel_id=1, source_target_pairs={{0,6},{2,0},{4,2},{6,4},{1,7},{3,1},{5,3},{7,5},{8,14},{10,8},{12,... | collective-permute-start | bytes 98312 | tf_op jit(solution)/shard_map/ppermute | solution.py:41
  49.1 28.6 %collective-permute-start.8 = (bf16[64,256]{1,0:T(8,128)(2,1)S(1)}, bf16[64,256]{1,0:T(8,128)(2,1)S(1)}, u32[]{:S(2)}, u32[]{:S(2)}) collective-permute-start(bf16[64,256]{1,0:T(8,128)(2,1)S(1)} %pad_maximum_fusion.4), channel_id=1, source_target_pairs={{0,24},{8,0},{16,8},{24,16},{1,25},{9,1},{17,9},{25,17},{2,26},{10... | collective-permute-start | bytes 98312 | tf_op jit(solution)/shard_map/ppermute | solution.py:41
  61.2 10.9 %collective-permute-start.6 = (bf16[64,256]{1,0:T(8,128)(2,1)S(1)}, bf16[64,256]{1,0:T(8,128)(2,1)S(1)}, u32[]{:S(2)}, u32[]{:S(2)}) collective-permute-start(bf16[64,256]{1,0:T(8,128)(2,1)S(1)} %pad_maximum_fusion.2), channel_id=1, source_target_pairs={{0,8},{8,16},{16,24},{24,0},{1,9},{9,17},{17,25},{25,1},{2,10},{10... | collective-permute-start | bytes 98312 | tf_op jit(solution)/shard_map/ppermute | solution.py:41
  63.2 14.5 %collective-permute-start.7 = (bf16[64,256]{1,0:T(8,128)(2,1)S(1)}, bf16[64,256]{1,0:T(8,128)(2,1)S(1)}, u32[]{:S(2)}, u32[]{:S(2)}) collective-permute-start(bf16[64,256]{1,0:T(8,128)(2,1)S(1)} %pad_maximum_fusion.3), channel_id=1, source_target_pairs={{0,16},{8,24},{16,0},{24,8},{1,17},{9,25},{17,1},{25,9},{2,18},{10... | collective-permute-start | bytes 98312 | tf_op jit(solution)/shard_map/ppermute | solution.py:41
  78.1 1.3 copy-start.2
  79.2 8.6 %copy-start.3 = (bf16[256,384]{1,0:T(8,128)(2,1)S(1)}, bf16[256,384]{1,0:T(8,128)(2,1)}, u32[]{:S(2)}) copy-start(bf16[256,384]{1,0:T(8,128)(2,1)} %param.13) | copy-start | bytes 589828
  79.4 49.5 %all-to-all-start = ((bf16[8,256,256]{1,2,0:T(8,128)(2,1)}), bf16[8,256,256]{1,2,0:T(8,128)(2,1)S(1)}, u32[]{:S(2)}, u32[]{:S(2)}) async-start(bf16[8,256,256]{1,2,0:T(8,128)(2,1)} %broadcast_in_dim.20), calls=%async_computation | async-start | bytes 2097152 | tf_op jit(solution)/shard_map/all_to_all | solution.py:21
  88.9 1.4 copy-start.1
  90.3 15.9 %collective-permute-start.11 = (bf16[256,528]{0,1:T(8,128)(2,1)S(1)}, bf16[256,528]{0,1:T(8,128)(2,1)}, u32[]{:S(2)}, u32[]{:S(2)}) collective-permute-start(bf16[256,528]{0,1:T(8,128)(2,1)S(1)} %get-tuple-element.20), channel_id=1, source_target_pairs={{0,32},{32,64},{64,96},{96,0},{1,33},{33,65},{65,97},{97,1},{2,34}... | collective-permute-start | bytes 811016 | tf_op jit(solution)/shard_map/ppermute | solution.py:32
  95.4 11.3 %collective-permute-start.12 = (bf16[256,528]{0,1:T(8,128)(2,1)S(1)}, bf16[256,528]{0,1:T(8,128)(2,1)}, u32[]{:S(2)}, u32[]{:S(2)}) collective-permute-start(bf16[256,528]{0,1:T(8,128)(2,1)S(1)} %get-tuple-element.22), channel_id=1, source_target_pairs={{0,64},{32,96},{64,0},{96,32},{1,65},{33,97},{65,1},{97,33},{2,66}... | collective-permute-start | bytes 811016 | tf_op jit(solution)/shard_map/ppermute | solution.py:32
  97.4 12.1 %collective-permute-start.13 = (bf16[256,528]{0,1:T(8,128)(2,1)S(1)}, bf16[256,528]{0,1:T(8,128)(2,1)}, u32[]{:S(2)}, u32[]{:S(2)}) collective-permute-start(bf16[256,528]{0,1:T(8,128)(2,1)S(1)} %get-tuple-element.21), channel_id=1, source_target_pairs={{0,96},{32,0},{64,32},{96,64},{1,97},{33,1},{65,33},{97,65},{2,98}... | collective-permute-start | bytes 811016 | tf_op jit(solution)/shard_map/ppermute | solution.py:32
  113.7 36.3 %copy-start.6 = (bf16[256,144]{0,1:T(8,128)(2,1)S(1)}, bf16[256,144]{0,1:T(8,128)(2,1)}, u32[]{:S(2)}) copy-start(bf16[256,144]{0,1:T(8,128)(2,1)} %param.20) | copy-start | bytes 221188
  113.7 9.7 %collective-permute-start.14 = (bf16[64,528]{1,0:T(8,128)(2,1)}, bf16[64,528]{1,0:T(8,128)(2,1)}, u32[]{:S(2)}, u32[]{:S(2)}) collective-permute-start(bf16[64,528]{1,0:T(8,128)(2,1)} %get-tuple-element.25), channel_id=1, source_target_pairs={{0,2},{2,4},{4,6},{6,0},{1,3},{3,5},{5,7},{7,1},{8,10},{10,12},{12... | collective-permute-start | bytes 202760 | tf_op jit(solution)/shard_map/ppermute | solution.py:32
  116.2 9.4 %collective-permute-start.15 = (bf16[64,528]{1,0:T(8,128)(2,1)S(1)}, bf16[64,528]{1,0:T(8,128)(2,1)}, u32[]{:S(2)}, u32[]{:S(2)}) collective-permute-start(bf16[64,528]{1,0:T(8,128)(2,1)S(1)} %get-tuple-element.27), channel_id=1, source_target_pairs={{0,4},{2,6},{4,0},{6,2},{1,5},{3,7},{5,1},{7,3},{8,12},{10,14},{12... | collective-permute-start | bytes 202760 | tf_op jit(solution)/shard_map/ppermute | solution.py:32
  121.5 6.4 %collective-permute-start.16 = (bf16[64,528]{1,0:T(8,128)(2,1)S(1)}, bf16[64,528]{1,0:T(8,128)(2,1)}, u32[]{:S(2)}, u32[]{:S(2)}) collective-permute-start(bf16[64,528]{1,0:T(8,128)(2,1)S(1)} %get-tuple-element.26), channel_id=1, source_target_pairs={{0,6},{2,0},{4,2},{6,4},{1,7},{3,1},{5,3},{7,5},{8,14},{10,8},{12,... | collective-permute-start | bytes 202760 | tf_op jit(solution)/shard_map/ppermute | solution.py:32
  128.9 21.0 %copy-start.5 = (bf16[2048,144]{0,1:T(8,128)(2,1)S(1)}, bf16[2048,144]{0,1:T(8,128)(2,1)}, u32[]{:S(2)}) copy-start(bf16[2048,144]{0,1:T(8,128)(2,1)} %param.15) | copy-start | bytes 1769476
  129.6 29.7 %collective-permute-start.17 = (bf16[16,528]{1,0:T(8,128)(2,1)}, bf16[16,528]{1,0:T(8,128)(2,1)S(1)}, u32[]{:S(2)}, u32[]{:S(2)}) collective-permute-start(bf16[16,528]{1,0:T(8,128)(2,1)} %get-tuple-element.41), channel_id=1, source_target_pairs={{0,8},{8,16},{16,24},{24,0},{1,9},{9,17},{17,25},{25,1},{2,10},{10... | collective-permute-start | bytes 50696 | tf_op jit(solution)/shard_map/ppermute | solution.py:32
  133.2 26.0 %collective-permute-start.18 = (bf16[16,528]{1,0:T(8,128)(2,1)}, bf16[16,528]{1,0:T(8,128)(2,1)S(1)}, u32[]{:S(2)}, u32[]{:S(2)}) collective-permute-start(bf16[16,528]{1,0:T(8,128)(2,1)} %get-tuple-element.43), channel_id=1, source_target_pairs={{0,16},{8,24},{16,0},{24,8},{1,17},{9,25},{17,1},{25,9},{2,18},{10... | collective-permute-start | bytes 50696 | tf_op jit(solution)/shard_map/ppermute | solution.py:32
  144.8 14.4 %collective-permute-start.19 = (bf16[16,528]{1,0:T(8,128)(2,1)}, bf16[16,528]{1,0:T(8,128)(2,1)}, u32[]{:S(2)}, u32[]{:S(2)}) collective-permute-start(bf16[16,528]{1,0:T(8,128)(2,1)} %get-tuple-element.42), channel_id=1, source_target_pairs={{0,24},{8,0},{16,8},{24,16},{1,25},{9,1},{17,9},{25,17},{2,26},{10... | collective-permute-start | bytes 50696 | tf_op jit(solution)/shard_map/ppermute | solution.py:32
  148.0 19.6 %copy-start.4 = (bf16[256,384]{1,0:T(8,128)(2,1)S(1)}, bf16[256,384]{1,0:T(8,128)(2,1)}, u32[]{:S(2)}) copy-start(bf16[256,384]{1,0:T(8,128)(2,1)} %param.21) | copy-start | bytes 589828
  152.3 15.3 %all-to-all-start.2 = ((f32[8,8,256]{2,1,0:T(8,128)}), f32[8,8,256]{2,1,0:T(8,128)S(1)}, u32[]{:S(2)}, u32[]{:S(2)}) async-start(f32[8,8,256]{2,1,0:T(8,128)} %broadcast_in_dim.24), calls=%async_computation.2 | async-start | bytes 131072 | tf_op jit(solution)/shard_map/all_to_all | solution.py:21

commit v2 on v1

v2 whole, which is shorter than its diff:
```python
import functools
import math

import jax
import jax.numpy as jnp
from jax import lax
from jax.experimental import pallas as pl
from jax.experimental.pallas import tpu as pltpu
from jax.sharding import Mesh
from jax.sharding import PartitionSpec as P

EPS = 1e-06
F32 = jnp.float32
BF16 = jnp.bfloat16
VMEM = pl.BlockSpec(memory_space=pltpu.VMEM)
SMEM = pl.BlockSpec(memory_space=pltpu.SMEM)


def shift(count, step):
    return [(i, (i + step) % count) for i in range(count)]


def broadcast_gather(block, axis):
    count = lax.axis_size(axis)
    copies = jnp.broadcast_to(block[None], (count,) + block.shape)
    return lax.all_to_all(copies, axis, 0, 0, tiled=True)


def exchange(blocks, axis):
    return lax.all_to_all(blocks, axis, 0, 0, tiled=True)


def hand_on(blocks, axis):
    count = lax.axis_size(axis)
    return [blocks[0]] + [lax.ppermute(blocks[k], axis, shift(count, k)) for k in range(1, count)]


def pick(chosen, source):
    return jnp.dot(chosen.astype(BF16), source, preferred_element_type=F32).astype(BF16)


def partial_kernel(here_ref, paired_ref, own_ref, other_ref, *outs):
    count = len(outs)
    rows = own_ref.shape[0]
    block = outs[0].shape[0]
    for k, out in enumerate(outs):
        target = lax.rem(here_ref[0] + k, count)
        start = pl.multiple_of(target * block, block)
        lhs = paired_ref[pl.ds(start, block), :]
        out[...] = (
            jnp.dot(lhs[:, :rows], own_ref[...], preferred_element_type=F32)
            + jnp.dot(lhs[:, rows:], other_ref[...], preferred_element_type=F32)
        ).astype(out.dtype)


def first_sum_kernel(nh, nl, piece, own_ref, *refs):
    out = refs[-1]
    for h in range(nh):
        for l in range(nl):
            at = pl.ds((h * nl + l) * piece, piece)
            total = own_ref[at, :]
            for ref in refs[:-1]:
                total += ref[at, :].astype(F32)
            out[l, pl.ds(h * piece, piece), :] = total.astype(BF16)


def sum_kernel(scale, split, parts_ref, *outs):
    total = parts_ref[0].astype(F32)
    for k in range(1, parts_ref.shape[0]):
        total += parts_ref[k].astype(F32)
    if split is None:
        outs[0][...] = total.astype(BF16)
    else:
        total *= scale
        outs[0][...] = total[:, :split]
        outs[1][...] = total[:, split:]


def shards(
    feat_sig,
    feat_cnx,
    cotangent,
    w_sig,
    w_cnx,
    lengths,
    enc_of,
    owner_of,
    pre_sig,
    pre_cnx,
    gain_sig,
    gain_cnx,
):
    slots = lengths.shape[1]
    rows, cols = cotangent.shape
    depth = rows // slots
    enc_count = lax.axis_size("enc")
    rep_count = lax.axis_size("rep")
    nx, nh, nl = (lax.axis_size(name) for name in ("x", "zh", "zl"))
    hx, hh = lax.axis_index("x"), lax.axis_index("zh")
    core = lax.axis_index("rep")
    swap = shift(rep_count, 1)

    token = lax.broadcasted_iota(jnp.int32, (slots, depth), 1)
    live = token < lengths[0][:, None]
    goal = jnp.where(live, (enc_of[0] * depth)[:, None] + token, -1).reshape(1, rows)
    row = lax.broadcasted_iota(jnp.int32, (rows, rows), 0)
    column = lax.broadcasted_iota(jnp.int32, (rows, rows), 1)
    held = pick(row == goal, cotangent)
    held = exchange(held.reshape(nx, rows // nx, cols), "x").reshape(rows, cols)
    line = lax.broadcasted_iota(jnp.int32, (rows, 1), 0)
    unit = line // depth
    unit = (unit % nx * nh + (unit // nx + hh) % nh) * nl + unit // (nx * nh)
    held = pick(column == unit * depth + line % depth, held)
    held = exchange(held.reshape(nl, rows // nl, cols), "zl")

    turned = jnp.where(live.reshape(1, rows), cotangent.T, jnp.zeros((), BF16))
    chips = slots // enc_count
    piece = cols // chips // rep_count
    turned = turned.reshape(chips, rep_count, piece, rows)
    mine = lax.dynamic_index_in_dim(turned, core, 1, keepdims=False).reshape(cols // rep_count, rows)
    theirs = lax.dynamic_index_in_dim(turned, 1 - core, 1, keepdims=False).reshape(cols // rep_count, rows)
    theirs = lax.ppermute(theirs, "rep", swap)
    paired = jnp.concatenate([mine, theirs], axis=1)
    paired, held = lax.optimization_barrier((paired, held))
    paired = broadcast_gather(paired, "enc")
    features = jnp.concatenate([feat_cnx, feat_sig], axis=1)
    other_features = lax.ppermute(features, "rep", swap)

    held = held.reshape(nl, nh, nx * depth, cols)
    held = [held[:, k].reshape(nl * nx * depth, cols) for k in range(nh)]
    held = jnp.concatenate(hand_on(held, "zh"))
    sender = owner_of[0]
    sx, kh, sl = sender // (nh * nl), (hh - sender // nl) % nh, sender % nl
    place = ((((kh * nl + sl) * nx + sx) * depth)[:, None] + token).reshape(rows, 1)
    routed = pick(column == place, held)
    routed, other_features = lax.optimization_barrier((routed, other_features))
    full = broadcast_gather(routed, "enc")

    half = enc_count * cols // rep_count
    width = features.shape[1]
    block = half // nx
    parts = pl.pallas_call(
        partial_kernel,
        out_shape=[
            jax.ShapeDtypeStruct((block, width), F32 if k == 0 else BF16) for k in range(nx)
        ],
        in_specs=[SMEM, VMEM, VMEM, VMEM],
        out_specs=[VMEM] * nx,
        compiler_params=pltpu.CompilerParams(vmem_limit_bytes=32 * 2**20),
        cost_estimate=pl.CostEstimate(
            flops=4 * half * rows * width, bytes_accessed=4 * half * width, transcendentals=0
        ),
        name="partial",
    )(hx.reshape(1), paired.reshape(half, rep_count * rows), features, other_features)
    parts = hand_on(parts, "x")
    total = pl.pallas_call(
        functools.partial(first_sum_kernel, nh, nl, piece),
        out_shape=jax.ShapeDtypeStruct((nl, nh * piece, width), BF16),
        in_specs=[VMEM] * nx,
        out_specs=VMEM,
        name="sum_x",
    )(*parts)
    full, total = lax.optimization_barrier((full, total))
    total = exchange(total, "zl")
    total = pl.pallas_call(
        functools.partial(sum_kernel, None, None),
        out_shape=[jax.ShapeDtypeStruct((nh * piece, width), BF16)],
        in_specs=[VMEM],
        out_specs=[VMEM],
        name="sum_zl",
    )(total)[0]
    total = exchange(total.reshape(nh, piece, width), "zh")

    full = full.transpose(1, 0, 2).reshape(rows, enc_count * cols)
    sums = []
    kept = []
    for weight, gain, pre in ((w_sig, gain_sig, pre_sig), (w_cnx, gain_cnx, pre_cnx)):
        dy = jnp.dot(full, weight, preferred_element_type=F32).astype(BF16)
        height = pre.astype(F32)
        scaled = dy.astype(F32) * gain
        kept.append((height, scaled, gain.shape[0] * enc_count))
        sums += [
            jnp.sum(height, axis=1),
            jnp.sum(height * height, axis=1),
            jnp.sum(scaled, axis=1),
            jnp.sum(scaled * height, axis=1),
        ]
    sums, total = lax.optimization_barrier((jnp.stack(sums), total))
    sums = jnp.sum(broadcast_gather(sums, "enc").reshape(enc_count, 8, rows), axis=0)
    split = feat_cnx.shape[1]
    grad_cnx, grad_sig = pl.pallas_call(
        functools.partial(sum_kernel, 1.0 / math.sqrt(rows * nx * nh * nl * rep_count), split),
        out_shape=[
            jax.ShapeDtypeStruct((piece, split), F32),
            jax.ShapeDtypeStruct((piece, width - split), F32),
        ],
        in_specs=[VMEM],
        out_specs=[VMEM, VMEM],
        name="sum_zh",
    )(total)
    grads = []
    for index, (height, scaled, channels) in enumerate(kept):
        means = sums[index * 4 : index * 4 + 4] / channels
        mean = means[0]
        inverse = lax.rsqrt(means[1] - mean * mean + EPS)
        product = inverse * (means[3] - mean * means[2])
        grads.append(
            (
                inverse[:, None]
                * (scaled - means[2][:, None] - (height - mean[:, None]) * inverse[:, None] * product[:, None])
            ).astype(BF16)
        )
    return (grad_sig, grad_cnx, grads[0], grads[1])


def solution(mesh):
    enc, dp, rep = mesh.devices.shape
    digit = round(dp ** (1 / 3))
    mesh = Mesh(
        mesh.devices.reshape(enc, dp // digit**2, digit, digit, rep), ("enc", "x", "zh", "zl", "rep")
    )
    owners = ("x", "zh", "zl", "rep")
    both = P(owners, "enc")
    in_specs = (
        both,
        both,
        both,
        P(None, "enc"),
        P(None, "enc"),
        P(owners, None),
        P(owners, None),
        P(owners, None),
        both,
        both,
        P("enc"),
        P("enc"),
    )
    return jax.shard_map(
        shards, mesh=mesh, in_specs=in_specs, out_specs=(both,) * 4, check_vma=False
    )
```

time: 171 us -> 163 us (0.953)
  waiting for transfers between devices: 22.2 us -> 52.7 us
  starting transfers between devices: 113 us -> 83 us
  local copies, waits for them, and re-layouts: 18.4 us -> 7.93 us
  Pallas kernels: 0 us -> 6.39 us
  other arithmetic: 9.01 us -> 3.37 us
    ppermute x9 -> x0, starting transfers between devices: 38.5 us -> none  [reduce_stage(): received.append(lax.ppermute(block, axis, shift(count, step)))]
    all_to_all x0 -> x4, starting transfers between devices: none -> 30.4 us  [exchange(): return lax.all_to_all(blocks, axis, 0, 0, tiled=True)]
    all_to_all x0 -> x4, waiting for transfers between devices: none -> 25.1 us  [exchange(): return lax.all_to_all(blocks, axis, 0, 0, tiled=True)]
    ppermute x9 -> x6, starting transfers between devices: 52.3 us -> 31.6 us  [hand_on(): lax.ppermute(blocks[k], axis, shift(count, k))]
    ppermute x9 -> x6, waiting for transfers between devices: 7.89 us -> 18.9 us  [hand_on(): lax.ppermute(blocks[k], axis, shift(count, k))]
    ppermute x9 -> x0, waiting for transfers between devices: 7.8 us -> none  [reduce_stage(): received.append(lax.ppermute(block, axis, shift(count, step)))]
    pallas_call x0 -> x4, Pallas kernels: none -> 6.39 us  [the longest x1 2.25 us: shards(): pl.pallas_call(functools.partial(first_sum_kernel, nh, nl, piece), out_sh...]
    reshape x2 -> x0, local copies, waits for them, and re-layouts: 3.48 us -> none  [shards(): total = reduce_stage(partial.reshape(nx, half // nx, width), 'x')]
  transfers between devices with their start and end apart: 23 -> 15, of which waited for: 8 -> 11; matrix products, arithmetic and copies ran while one was open for 15% -> 4% of each run, Pallas kernels for 0% -> 3%
where the time goes in v2:
time: 163 us; the launch traced here: 162 us
  starting transfers between devices  83 us (51%)
  waiting for transfers between devices  52.7 us (32%)
  local copies, waits for them, and re-layouts  7.93 us (5%)
  matrix products  7.38 us (5%)
  Pallas kernels  6.39 us (4%)
  other arithmetic  3.37 us (2%)
    ppermute x6, starting transfers between devices, hand_on(): lax.ppermute(blocks[k], axis, shift(count, k))  31.6 us
    all_to_all x4, starting transfers between devices, exchange(): return lax.all_to_all(blocks, axis, 0, 0, tiled=True)  30.4 us
    all_to_all x4, waiting for transfers between devices, exchange(): return lax.all_to_all(blocks, axis, 0, 0, tiled=True)  25.1 us
    ppermute x6, waiting for transfers between devices, hand_on(): lax.ppermute(blocks[k], axis, shift(count, k))  18.9 us
    all_to_all x3, starting transfers between devices, broadcast_gather(): return lax.all_to_all(copies, axis, 0, 0, tiled=True)  17.2 us
    all_to_all x3, waiting for transfers between devices, broadcast_gather(): return lax.all_to_all(copies, axis, 0, 0, tiled=True)  7.53 us
    unnamed x34, local copies, waits for them, and re-layouts  4.04 us
    dot_general x2, matrix products, shards(): dy = jnp.dot(full, weight, preferred_element_type=F32).astype(BF16)  3.75 us
  transfers between devices with their start and end apart: 15, of which 11 were waited for; matrix products, arithmetic and copies ran while one was open for 4% of the time, Pallas kernels for 3%

profile of v2, /device:TPU:6, one launch (start us, length us, event | category | flops | bytes accessed | tf_op | source)
XLA Modules:
  0.0 161.8 jit_solution(6247136762511418113)
XLA Ops:
  2.5 1.8 %convolution_convert_fusion.3 = bf16[256,256]{1,0:T(8,128)(2,1)} fusion(bf16[256,256]{1,0:T(8,128)(2,1)} %param.14, s32[256]{0:T(256)S(1)} %broadcast_select_fusion.1), kind=kOutput, calls=%fused_computation.5 | convolution fusion | flops 33685504 | bytes 263168 | tf_op jit(solution)/shard_map/dot_general | solution.py:39
  4.2 16.4 %all-to-all-start = ((bf16[4,64,256]{2,1,0:T(8,128)(2,1)}), bf16[4,64,256]{2,1,0:T(8,128)(2,1)S(1)}, u32[]{:S(2)}, u32[]{:S(2)}) async-start(bf16[4,64,256]{2,1,0:T(8,128)(2,1)} %bitcast.10), calls=%async_computation | async-start | bytes 262144 | tf_op jit(solution)/shard_map/all_to_all | solution.py:30
  21.7 2.9 %all-to-all-done = bf16[4,64,256]{2,1,0:T(8,128)(2,1)S(1)} async-done(((bf16[4,64,256]{2,1,0:T(8,128)(2,1)}), bf16[4,64,256]{2,1,0:T(8,128)(2,1)S(1)}, u32[]{:S(2)}, u32[]{:S(2)}) %all-to-all-start) | async-done | bytes 131104 | tf_op jit(solution)/shard_map/all_to_all | solution.py:30
  25.4 3.3 %all-to-all-start.1 = ((bf16[4,64,256]{2,1,0:T(8,128)(2,1)}), bf16[4,64,256]{2,1,0:T(8,128)(2,1)S(1)}, u32[]{:S(2)}, u32[]{:S(2)}) async-start(bf16[4,64,256]{2,1,0:T(8,128)(2,1)} %bitcast.12), calls=%async_computation.1 | async-start | bytes 262144 | tf_op jit(solution)/shard_map/all_to_all | solution.py:30
  28.8 1.9 %collective-permute-start = (bf16[128,256]{1,0:T(8,128)(2,1)S(1)}, bf16[128,256]{1,0:T(8,128)(2,1)S(1)}, u32[]{:S(2)}, u32[]{:S(2)}) collective-permute-start(bf16[128,256]{1,0:T(8,128)(2,1)S(1)} %bitcast.66), channel_id=1, source_target_pairs={{0,1},{1,0},{2,3},{3,2},{4,5},{5,4},{6,7},{7,6},{8,9},{9,8},{10,11... | collective-permute-start | bytes 196616 | tf_op jit(solution)/shard_map/ppermute | solution.py:122
  30.8 1.2 collective-permute-done
  32.0 2.6 %all-to-all-done.1 = bf16[4,64,256]{2,1,0:T(8,128)(2,1)S(1)} async-done(((bf16[4,64,256]{2,1,0:T(8,128)(2,1)}), bf16[4,64,256]{2,1,0:T(8,128)(2,1)S(1)}, u32[]{:S(2)}, u32[]{:S(2)}) %all-to-all-start.1) | async-done | bytes 131104 | tf_op jit(solution)/shard_map/all_to_all | solution.py:30
  34.7 1.1 broadcast_in_dim.23
  35.7 3.7 %all-to-all-start.3 = ((bf16[8,128,512]{2,1,0:T(8,128)(2,1)}), bf16[8,128,512]{2,1,0:T(8,128)(2,1)S(1)}, u32[]{:S(2)}, u32[]{:S(2)}) async-start(bf16[8,128,512]{2,1,0:T(8,128)(2,1)} %broadcast_in_dim.23), calls=%async_computation.3 | async-start | bytes 2097152 | tf_op jit(solution)/shard_map/all_to_all | solution.py:26
  39.6 1.9 %collective-permute-start.4 = (bf16[256,528]{1,0:T(8,128)(2,1)S(1)}, bf16[256,528]{1,0:T(8,128)(2,1)S(1)}, u32[]{:S(2)}, u32[]{:S(2)}) collective-permute-start(bf16[256,528]{1,0:T(8,128)(2,1)S(1)} %pad_maximum_fusion.own_ref), channel_id=1, source_target_pairs={{0,1},{1,0},{2,3},{3,2},{4,5},{5,4},{6,7},{7,6},{8,9},{9,8},{10,11... | collective-permute-start | bytes 811016 | tf_op jit(solution)/shard_map/ppermute | solution.py:127
  42.2 6.7 %collective-permute-start.1 = (bf16[64,256]{1,0:T(8,128)(2,1)S(1)}, bf16[64,256]{1,0:T(8,128)(2,1)S(1)}, u32[]{:S(2)}, u32[]{:S(2)}) collective-permute-start(bf16[64,256]{1,0:T(8,128)(2,1)S(1)} %bitcast.70), channel_id=1, source_target_pairs={{0,8},{8,16},{16,24},{24,0},{1,9},{9,17},{17,25},{25,1},{2,10},{10... | collective-permute-start | bytes 98312 | tf_op jit(solution)/shard_map/ppermute | solution.py:35
  49.0 11.9 %collective-permute-start.2 = (bf16[64,256]{1,0:T(8,128)(2,1)S(1)}, bf16[64,256]{1,0:T(8,128)(2,1)S(1)}, u32[]{:S(2)}, u32[]{:S(2)}) collective-permute-start(bf16[64,256]{1,0:T(8,128)(2,1)S(1)} %bitcast.69), channel_id=1, source_target_pairs={{0,16},{8,24},{16,0},{24,8},{1,17},{9,25},{17,1},{25,9},{2,18},{10... | collective-permute-start | bytes 98312 | tf_op jit(solution)/shard_map/ppermute | solution.py:35
  60.8 3.6 %collective-permute-start.3 = (bf16[64,256]{1,0:T(8,128)(2,1)S(1)}, bf16[64,256]{1,0:T(8,128)(2,1)S(1)}, u32[]{:S(2)}, u32[]{:S(2)}) collective-permute-start(bf16[64,256]{1,0:T(8,128)(2,1)S(1)} %bitcast.68), channel_id=1, source_target_pairs={{0,24},{8,0},{16,8},{24,16},{1,25},{9,1},{17,9},{25,17},{2,26},{10... | collective-permute-start | bytes 98312 | tf_op jit(solution)/shard_map/ppermute | solution.py:35
  64.7 7.6 %collective-permute-done.3 = bf16[64,256]{1,0:T(8,128)(2,1)S(1)} collective-permute-done((bf16[64,256]{1,0:T(8,128)(2,1)S(1)}, bf16[64,256]{1,0:T(8,128)(2,1)S(1)}, u32[]{:S(2)}, u32[]{:S(2)}) %collective-permute-start.3) | collective-permute-done | bytes 32800 | tf_op jit(solution)/shard_map/ppermute | solution.py:35
  75.0 7.2 %all-to-all-start.2 = ((bf16[8,256,256]{1,2,0:T(8,128)(2,1)}), bf16[8,256,256]{1,2,0:T(8,128)(2,1)}, u32[]{:S(2)}, u32[]{:S(2)}) async-start(bf16[8,256,256]{1,2,0:T(8,128)(2,1)} %broadcast_in_dim.22), calls=%async_computation.2 | async-start | bytes 2097152 | tf_op jit(solution)/shard_map/all_to_all | solution.py:26
  84.1 4.1 %collective-permute-start.5 = (bf16[256,528]{1,0:T(8,128)(2,1)S(1)}, bf16[256,528]{1,0:T(8,128)(2,1)S(1)}, u32[]{:S(2)}, u32[]{:S(2)}) collective-permute-start(bf16[256,528]{1,0:T(8,128)(2,1)S(1)} %get-tuple-element.23), channel_id=1, source_target_pairs={{0,32},{32,64},{64,96},{96,0},{1,33},{33,65},{65,97},{97,1},{2,34}... | collective-permute-start | bytes 811016 | tf_op jit(solution)/shard_map/ppermute | solution.py:35
  88.2 2.1 %collective-permute-start.6 = (bf16[256,528]{1,0:T(8,128)(2,1)S(1)}, bf16[256,528]{1,0:T(8,128)(2,1)S(1)}, u32[]{:S(2)}, u32[]{:S(2)}) collective-permute-start(bf16[256,528]{1,0:T(8,128)(2,1)S(1)} %get-tuple-element.24), channel_id=1, source_target_pairs={{0,64},{32,96},{64,0},{96,32},{1,65},{33,97},{65,1},{97,33},{2,66}... | collective-permute-start | bytes 811016 | tf_op jit(solution)/shard_map/ppermute | solution.py:35
  90.3 3.1 %collective-permute-start.7 = (bf16[256,528]{1,0:T(8,128)(2,1)S(1)}, bf16[256,528]{1,0:T(8,128)(2,1)S(1)}, u32[]{:S(2)}, u32[]{:S(2)}) collective-permute-start(bf16[256,528]{1,0:T(8,128)(2,1)S(1)} %get-tuple-element.25), channel_id=1, source_target_pairs={{0,96},{32,0},{64,32},{96,64},{1,97},{33,1},{65,33},{97,65},{2,98}... | collective-permute-start | bytes 811016 | tf_op jit(solution)/shard_map/ppermute | solution.py:35
  93.4 5.7 %collective-permute-done.5.refs_0_ = bf16[256,528]{1,0:T(8,128)(2,1)S(1)} collective-permute-done((bf16[256,528]{1,0:T(8,128)(2,1)S(1)}, bf16[256,528]{1,0:T(8,128)(2,1)S(1)}, u32[]{:S(2)}, u32[]{:S(2)}) %collective-permute-start.5) | collective-permute-done | bytes 270368 | tf_op jit(solution)/shard_map/ppermute | solution.py:35
  99.2 2.2 %collective-permute-done.6.refs_1_ = bf16[256,528]{1,0:T(8,128)(2,1)S(1)} collective-permute-done((bf16[256,528]{1,0:T(8,128)(2,1)S(1)}, bf16[256,528]{1,0:T(8,128)(2,1)S(1)}, u32[]{:S(2)}, u32[]{:S(2)}) %collective-permute-start.6) | collective-permute-done | bytes 270368 | tf_op jit(solution)/shard_map/ppermute | solution.py:35
  101.3 3.4 %collective-permute-done.7.refs_2_ = bf16[256,528]{1,0:T(8,128)(2,1)S(1)} collective-permute-done((bf16[256,528]{1,0:T(8,128)(2,1)S(1)}, bf16[256,528]{1,0:T(8,128)(2,1)S(1)}, u32[]{:S(2)}, u32[]{:S(2)}) %collective-permute-start.7) | collective-permute-done | bytes 270368 | tf_op jit(solution)/shard_map/ppermute | solution.py:35
  105.5 2.2 %sum_x.1 = bf16[4,64,528]{2,1,0:T(8,128)(2,1)} custom-call(f32[256,528]{1,0:T(8,128)} %copy-done.1, bf16[256,528]{1,0:T(8,128)(2,1)} %copy-done.6, bf16[256,528]{1,0:T(8,128)(2,1)} %copy-done.7, bf16[256,528]{1,0:T(8,128)(2,1)} %copy-done.8), custom_call_target="tpu_custom_call" | custom-call | tf_op jit(solution)/shard_map/sum_x/pallas_call | solution.py:156
  108.4 4.0 %all-to-all-start.4 = ((bf16[4,64,528]{2,1,0:T(8,128)(2,1)}), bf16[4,64,528]{2,1,0:T(8,128)(2,1)S(1)}, u32[]{:S(2)}, u32[]{:S(2)}) async-start(bf16[4,64,528]{2,1,0:T(8,128)(2,1)} %sum_x.1), calls=%async_computation.4 | async-start | bytes 655360 | tf_op jit(solution)/shard_map/all_to_all | solution.py:30
  112.5 2.2 %fusion.5 = (f32[256]{0:T(256)S(1)}, f32[256]{0:T(256)S(1)}, f32[256]{0:T(256)S(1)}, f32[256]{0:T(256)S(1)}, f32[256,384]{1,0:T(8,128)S(1)}) fusion(bf16[256,384]{1,0:T(8,128)(2,1)S(1)} %copy-done.3, f32[384]{0:T(512)S(1)} %copy-done.12, bf16[256,2048]{0,1:T(8,128)(2,1)} %bitcast.21, bf16[2048,384]{1,0:T(8,128)(2,1)S(1)} %copy-done), kind=kOutput, calls=%fused_computation.14 | convolution fusion | flops 403635200 | bytes 3216896 | tf_op jit(solution)/shard_map/dot_general | solution.py:178
  114.6 8.3 %all-to-all-done.4.parts_ref = bf16[4,64,528]{2,1,0:T(8,128)(2,1)S(1)} async-done(((bf16[4,64,528]{2,1,0:T(8,128)(2,1)}), bf16[4,64,528]{2,1,0:T(8,128)(2,1)S(1)}, u32[]{:S(2)}, u32[]{:S(2)}) %all-to-all-start.4) | async-done | bytes 270368 | tf_op jit(solution)/shard_map/all_to_all | solution.py:30
  123.6 1.7 %sum_zl.1 = bf16[64,528]{1,0:T(8,128)(2,1)} custom-call(bf16[4,64,528]{2,1,0:T(8,128)(2,1)} %copy-done.2), custom_call_target="tpu_custom_call" | custom-call | tf_op jit(solution)/shard_map/sum_zl/pallas_call | solution.py:165
  125.3 6.6 %all-to-all-start.5 = ((bf16[4,16,528]{2,1,0:T(8,128)(2,1)}), bf16[4,16,528]{2,1,0:T(8,128)(2,1)S(1)}, u32[]{:S(2)}, u32[]{:S(2)}) async-start(bf16[4,16,528]{2,1,0:T(8,128)(2,1)} %bitcast.64), calls=%async_computation.5 | async-start | bytes 163840 | tf_op jit(solution)/shard_map/all_to_all | solution.py:30
  131.9 1.6 fusion.12
  133.5 11.3 %all-to-all-done.5.parts_ref = bf16[4,16,528]{2,1,0:T(8,128)(2,1)S(1)} async-done(((bf16[4,16,528]{2,1,0:T(8,128)(2,1)}), bf16[4,16,528]{2,1,0:T(8,128)(2,1)S(1)}, u32[]{:S(2)}, u32[]{:S(2)}) %all-to-all-start.5) | async-done | bytes 67616 | tf_op jit(solution)/shard_map/all_to_all | solution.py:30
  145.5 6.3 %all-to-all-start.6 = ((f32[8,8,256]{2,1,0:T(8,128)}), f32[8,8,256]{2,1,0:T(8,128)S(1)}, u32[]{:S(2)}, u32[]{:S(2)}) async-start(f32[8,8,256]{2,1,0:T(8,128)} %broadcast_in_dim.24), calls=%async_computation.6 | async-start | bytes 131072 | tf_op jit(solution)/shard_map/all_to_all | solution.py:26
  151.8 1.5 sum_zh.1
  153.3 6.9 %all-to-all-done.6 = f32[8,8,256]{2,1,0:T(8,128)S(1)} async-done(((f32[8,8,256]{2,1,0:T(8,128)}), f32[8,8,256]{2,1,0:T(8,128)S(1)}, u32[]{:S(2)}, u32[]{:S(2)}) %all-to-all-start.6) | async-done | bytes 65568 | tf_op jit(solution)/shard_map/all_to_all | solution.py:26
  (68 shorter events, 13.8 us)
Async XLA Ops:
  0.6 111.8 %copy-start = (bf16[2048,384]{1,0:T(8,128)(2,1)S(1)}, bf16[2048,384]{1,0:T(8,128)(2,1)}, u32[]{:S(2)}) copy-start(bf16[2048,384]{1,0:T(8,128)(2,1)} %param.16) | copy-start | bytes 4718596
  4.2 20.3 %all-to-all-start = ((bf16[4,64,256]{2,1,0:T(8,128)(2,1)}), bf16[4,64,256]{2,1,0:T(8,128)(2,1)S(1)}, u32[]{:S(2)}, u32[]{:S(2)}) async-start(bf16[4,64,256]{2,1,0:T(8,128)(2,1)} %bitcast.10), calls=%async_computation | async-start | bytes 262144 | tf_op jit(solution)/shard_map/all_to_all | solution.py:30
  25.4 9.2 %all-to-all-start.1 = ((bf16[4,64,256]{2,1,0:T(8,128)(2,1)}), bf16[4,64,256]{2,1,0:T(8,128)(2,1)S(1)}, u32[]{:S(2)}, u32[]{:S(2)}) async-start(bf16[4,64,256]{2,1,0:T(8,128)(2,1)} %bitcast.12), calls=%async_computation.1 | async-start | bytes 262144 | tf_op jit(solution)/shard_map/all_to_all | solution.py:30
  28.8 3.1 %collective-permute-start = (bf16[128,256]{1,0:T(8,128)(2,1)S(1)}, bf16[128,256]{1,0:T(8,128)(2,1)S(1)}, u32[]{:S(2)}, u32[]{:S(2)}) collective-permute-start(bf16[128,256]{1,0:T(8,128)(2,1)S(1)} %bitcast.66), channel_id=1, source_target_pairs={{0,1},{1,0},{2,3},{3,2},{4,5},{5,4},{6,7},{7,6},{8,9},{9,8},{10,11... | collective-permute-start | bytes 196616 | tf_op jit(solution)/shard_map/ppermute | solution.py:122
  32.0 7.4 %copy-start.11 = (bf16[256,144]{0,1:T(8,128)(2,1)S(1)}, bf16[256,144]{0,1:T(8,128)(2,1)}, u32[]{:S(2)}) copy-start(bf16[256,144]{0,1:T(8,128)(2,1)} %param.12) | copy-start | bytes 221188
  32.0 7.6 %copy-start.10 = (bf16[256,384]{1,0:T(8,128)(2,1)S(1)}, bf16[256,384]{1,0:T(8,128)(2,1)}, u32[]{:S(2)}) copy-start(bf16[256,384]{1,0:T(8,128)(2,1)} %param.13) | copy-start | bytes 589828
  35.7 5.8 %copy-start.15 = (s32[1,64]{1,0:T(1,128)S(1)}, s32[1,64]{1,0:T(1,128)}, u32[]{:S(2)}) copy-start(s32[1,64]{1,0:T(1,128)} %param.19) | copy-start | bytes 772
  35.7 38.2 %all-to-all-start.3 = ((bf16[8,128,512]{2,1,0:T(8,128)(2,1)}), bf16[8,128,512]{2,1,0:T(8,128)(2,1)S(1)}, u32[]{:S(2)}, u32[]{:S(2)}) async-start(bf16[8,128,512]{2,1,0:T(8,128)(2,1)} %broadcast_in_dim.23), calls=%async_computation.3 | async-start | bytes 2097152 | tf_op jit(solution)/shard_map/all_to_all | solution.py:26
  39.6 34.2 %collective-permute-start.4 = (bf16[256,528]{1,0:T(8,128)(2,1)S(1)}, bf16[256,528]{1,0:T(8,128)(2,1)S(1)}, u32[]{:S(2)}, u32[]{:S(2)}) collective-permute-start(bf16[256,528]{1,0:T(8,128)(2,1)S(1)} %pad_maximum_fusion.own_ref), channel_id=1, source_target_pairs={{0,1},{1,0},{2,3},{3,2},{4,5},{5,4},{6,7},{7,6},{8,9},{9,8},{10,11... | collective-permute-start | bytes 811016 | tf_op jit(solution)/shard_map/ppermute | solution.py:127
  42.2 22.5 %collective-permute-start.1 = (bf16[64,256]{1,0:T(8,128)(2,1)S(1)}, bf16[64,256]{1,0:T(8,128)(2,1)S(1)}, u32[]{:S(2)}, u32[]{:S(2)}) collective-permute-start(bf16[64,256]{1,0:T(8,128)(2,1)S(1)} %bitcast.70), channel_id=1, source_target_pairs={{0,8},{8,16},{16,24},{24,0},{1,9},{9,17},{17,25},{25,1},{2,10},{10... | collective-permute-start | bytes 98312 | tf_op jit(solution)/shard_map/ppermute | solution.py:35
  49.0 15.7 %collective-permute-start.2 = (bf16[64,256]{1,0:T(8,128)(2,1)S(1)}, bf16[64,256]{1,0:T(8,128)(2,1)S(1)}, u32[]{:S(2)}, u32[]{:S(2)}) collective-permute-start(bf16[64,256]{1,0:T(8,128)(2,1)S(1)} %bitcast.69), channel_id=1, source_target_pairs={{0,16},{8,24},{16,0},{24,8},{1,17},{9,25},{17,1},{25,9},{2,18},{10... | collective-permute-start | bytes 98312 | tf_op jit(solution)/shard_map/ppermute | solution.py:35
  60.8 11.4 %collective-permute-start.3 = (bf16[64,256]{1,0:T(8,128)(2,1)S(1)}, bf16[64,256]{1,0:T(8,128)(2,1)S(1)}, u32[]{:S(2)}, u32[]{:S(2)}) collective-permute-start(bf16[64,256]{1,0:T(8,128)(2,1)S(1)} %bitcast.68), channel_id=1, source_target_pairs={{0,24},{8,0},{16,8},{24,16},{1,25},{9,1},{17,9},{25,17},{2,26},{10... | collective-permute-start | bytes 98312 | tf_op jit(solution)/shard_map/ppermute | solution.py:35
  72.2 0.6 copy-start.14
  75.0 33.3 %all-to-all-start.2 = ((bf16[8,256,256]{1,2,0:T(8,128)(2,1)}), bf16[8,256,256]{1,2,0:T(8,128)(2,1)}, u32[]{:S(2)}, u32[]{:S(2)}) async-start(bf16[8,256,256]{1,2,0:T(8,128)(2,1)} %broadcast_in_dim.22), calls=%async_computation.2 | async-start | bytes 2097152 | tf_op jit(solution)/shard_map/all_to_all | solution.py:26
  83.2 0.8 copy-start.1
  84.1 28.4 %copy-start.3 = (bf16[256,384]{1,0:T(8,128)(2,1)S(1)}, bf16[256,384]{1,0:T(8,128)(2,1)}, u32[]{:S(2)}) copy-start(bf16[256,384]{1,0:T(8,128)(2,1)} %param.21) | copy-start | bytes 589828
  84.1 28.4 %copy-start.12 = (f32[384]{0:T(512)S(1)}, f32[384]{0:T(512)}, u32[]{:S(2)}) copy-start(f32[384]{0:T(512)} %param.23) | copy-start | bytes 4612
  84.1 15.1 %collective-permute-start.5 = (bf16[256,528]{1,0:T(8,128)(2,1)S(1)}, bf16[256,528]{1,0:T(8,128)(2,1)S(1)}, u32[]{:S(2)}, u32[]{:S(2)}) collective-permute-start(bf16[256,528]{1,0:T(8,128)(2,1)S(1)} %get-tuple-element.23), channel_id=1, source_target_pairs={{0,32},{32,64},{64,96},{96,0},{1,33},{33,65},{65,97},{97,1},{2,34}... | collective-permute-start | bytes 811016 | tf_op jit(solution)/shard_map/ppermute | solution.py:35
  88.2 13.2 %collective-permute-start.6 = (bf16[256,528]{1,0:T(8,128)(2,1)S(1)}, bf16[256,528]{1,0:T(8,128)(2,1)S(1)}, u32[]{:S(2)}, u32[]{:S(2)}) collective-permute-start(bf16[256,528]{1,0:T(8,128)(2,1)S(1)} %get-tuple-element.24), channel_id=1, source_target_pairs={{0,64},{32,96},{64,0},{96,32},{1,65},{33,97},{65,1},{97,33},{2,66}... | collective-permute-start | bytes 811016 | tf_op jit(solution)/shard_map/ppermute | solution.py:35
  90.3 14.4 %collective-permute-start.7 = (bf16[256,528]{1,0:T(8,128)(2,1)S(1)}, bf16[256,528]{1,0:T(8,128)(2,1)S(1)}, u32[]{:S(2)}, u32[]{:S(2)}) collective-permute-start(bf16[256,528]{1,0:T(8,128)(2,1)S(1)} %get-tuple-element.25), channel_id=1, source_target_pairs={{0,96},{32,0},{64,32},{96,64},{1,97},{33,1},{65,33},{97,65},{2,98}... | collective-permute-start | bytes 811016 | tf_op jit(solution)/shard_map/ppermute | solution.py:35
  99.2 5.6 %copy-start.6 = (bf16[256,528]{1,0:T(8,128)(2,1)}, bf16[256,528]{1,0:T(8,128)(2,1)S(1)}, u32[]{:S(2)}) copy-start(bf16[256,528]{1,0:T(8,128)(2,1)S(1)} %collective-permute-done.5.refs_0_) | copy-start | bytes 811012
  101.3 3.4 %copy-start.7 = (bf16[256,528]{1,0:T(8,128)(2,1)}, bf16[256,528]{1,0:T(8,128)(2,1)S(1)}, u32[]{:S(2)}) copy-start(bf16[256,528]{1,0:T(8,128)(2,1)S(1)} %collective-permute-done.6.refs_1_) | copy-start | bytes 811012
  104.7 0.7 copy-start.8
  108.4 14.5 %all-to-all-start.4 = ((bf16[4,64,528]{2,1,0:T(8,128)(2,1)}), bf16[4,64,528]{2,1,0:T(8,128)(2,1)S(1)}, u32[]{:S(2)}, u32[]{:S(2)}) async-start(bf16[4,64,528]{2,1,0:T(8,128)(2,1)} %sum_x.1), calls=%async_computation.4 | async-start | bytes 655360 | tf_op jit(solution)/shard_map/all_to_all | solution.py:30
  112.4 19.5 %copy-start.4 = (bf16[2048,144]{0,1:T(8,128)(2,1)S(1)}, bf16[2048,144]{0,1:T(8,128)(2,1)}, u32[]{:S(2)}) copy-start(bf16[2048,144]{0,1:T(8,128)(2,1)} %param.15) | copy-start | bytes 1769476
  112.4 19.5 %copy-start.9 = (bf16[256,144]{0,1:T(8,128)(2,1)S(1)}, bf16[256,144]{0,1:T(8,128)(2,1)}, u32[]{:S(2)}) copy-start(bf16[256,144]{0,1:T(8,128)(2,1)} %param.20) | copy-start | bytes 221188
  112.4 19.5 %copy-start.13 = (f32[144]{0:T(256)S(1)}, f32[144]{0:T(256)}, u32[]{:S(2)}) copy-start(f32[144]{0:T(256)} %param.22) | copy-start | bytes 1732
  122.9 0.7 copy-start.2
  125.3 19.5 %all-to-all-start.5 = ((bf16[4,16,528]{2,1,0:T(8,128)(2,1)}), bf16[4,16,528]{2,1,0:T(8,128)(2,1)S(1)}, u32[]{:S(2)}, u32[]{:S(2)}) async-start(bf16[4,16,528]{2,1,0:T(8,128)(2,1)} %bitcast.64), calls=%async_computation.5 | async-start | bytes 163840 | tf_op jit(solution)/shard_map/all_to_all | solution.py:30
  144.8 6.9 %copy-start.5 = (bf16[4,16,528]{2,1,0:T(8,128)(2,1)}, bf16[4,16,528]{2,1,0:T(8,128)(2,1)S(1)}, u32[]{:S(2)}) copy-start(bf16[4,16,528]{2,1,0:T(8,128)(2,1)S(1)} %all-to-all-done.5.parts_ref) | copy-start | bytes 202756
  145.5 14.6 %all-to-all-start.6 = ((f32[8,8,256]{2,1,0:T(8,128)}), f32[8,8,256]{2,1,0:T(8,128)S(1)}, u32[]{:S(2)}, u32[]{:S(2)}) async-start(f32[8,8,256]{2,1,0:T(8,128)} %broadcast_in_dim.24), calls=%async_computation.6 | async-start | bytes 131072 | tf_op jit(solution)/shard_map/all_to_all | solution.py:26

commit v3 on v2

v3 whole, which is shorter than its diff:
```python
import functools
import math

import jax
import jax.numpy as jnp
from jax import lax
from jax.experimental import pallas as pl
from jax.experimental.pallas import tpu as pltpu
from jax.sharding import Mesh
from jax.sharding import PartitionSpec as P

EPS = 1e-06
F32 = jnp.float32
BF16 = jnp.bfloat16
VMEM = pl.BlockSpec(memory_space=pltpu.VMEM)
SMEM = pl.BlockSpec(memory_space=pltpu.SMEM)


def shift(count, step):
    return [(i, (i + step) % count) for i in range(count)]


def broadcast_gather(block, axis):
    count = lax.axis_size(axis)
    copies = jnp.broadcast_to(block[None], (count,) + block.shape)
    return lax.all_to_all(copies, axis, 0, 0, tiled=True)


def exchange(blocks, axis):
    return lax.all_to_all(blocks, axis, 0, 0, tiled=True)


def hand_on(blocks, axis):
    count = lax.axis_size(axis)
    return [blocks[0]] + [lax.ppermute(blocks[k], axis, shift(count, k)) for k in range(1, count)]


def pick(chosen, source):
    return jnp.dot(chosen.astype(BF16), source, preferred_element_type=F32).astype(BF16)


def partial_kernel(here_ref, gathered_ref, own_ref, paired_ref, other_ref, *outs):
    count = len(outs)
    each = gathered_ref.shape[0] // count
    piece = gathered_ref.shape[2]
    for k, out in enumerate(outs):
        target = lax.rem(here_ref[0] + k, count)
        for j in range(each):
            at = target * each + j
            out[pl.ds(j * piece, piece), :] = (
                jnp.dot(gathered_ref[at, 0], own_ref[...], preferred_element_type=F32)
                + jnp.dot(paired_ref[at], other_ref[...], preferred_element_type=F32)
            ).astype(out.dtype)


def sum_x_kernel(own_ref, *refs):
    total = own_ref[...]
    for ref in refs[:-1]:
        total += ref[...].astype(F32)
    refs[-1][...] = total.astype(BF16)


def sum_z_kernel(scale, split, parts_ref, cnx_ref, sig_ref):
    total = parts_ref[0].astype(F32)
    for k in range(1, parts_ref.shape[0]):
        total += parts_ref[k].astype(F32)
    total *= scale
    cnx_ref[...] = total[:, :split]
    sig_ref[...] = total[:, split:]


def shards(
    feat_sig,
    feat_cnx,
    cotangent,
    w_sig,
    w_cnx,
    lengths,
    enc_of,
    owner_of,
    pre_sig,
    pre_cnx,
    gain_sig,
    gain_cnx,
):
    slots = lengths.shape[1]
    rows, cols = cotangent.shape
    depth = rows // slots
    enc_count = lax.axis_size("enc")
    rep_count = lax.axis_size("rep")
    nx, nz = lax.axis_size("x"), lax.axis_size("z")
    hx = lax.axis_index("x")
    core = lax.axis_index("rep")
    swap = shift(rep_count, 1)

    token = lax.broadcasted_iota(jnp.int32, (slots, depth), 1)
    live = (token < lengths[0][:, None]).reshape(1, rows)
    turned = jnp.where(live, cotangent.T, jnp.zeros((), BF16))
    chips = slots // enc_count
    piece = cols // chips // rep_count
    half = cols // rep_count
    turned = turned.reshape(chips, rep_count, piece, rows)
    turned = jnp.stack(
        [
            lax.dynamic_index_in_dim(turned, index, 1, keepdims=False).reshape(half, rows)
            for index in (core, 1 - core)
        ]
    )
    gathered = broadcast_gather(turned, "enc").reshape(enc_count, rep_count, half, rows)
    features = jnp.concatenate([feat_cnx, feat_sig], axis=1)
    other_features = lax.ppermute(features, "rep", swap)
    weight = jnp.concatenate([w_cnx, w_sig], axis=1)
    width = weight.shape[1]
    weight = weight.reshape(enc_count, chips, rep_count, piece, width)
    weight = jnp.stack(
        [
            lax.dynamic_index_in_dim(weight, index, 2, keepdims=False).reshape(enc_count, half, width)
            for index in (core, 1 - core)
        ],
        axis=1,
    ).reshape(enc_count * cols, width)
    gathered, other_features, weight = lax.optimization_barrier((gathered, other_features, weight))

    paired = lax.ppermute(gathered[:, 1], "rep", swap)

    row = lax.broadcasted_iota(jnp.int32, (rows, rows), 0)
    column = lax.broadcasted_iota(jnp.int32, (rows, rows), 1)
    line = lax.broadcasted_iota(jnp.int32, (rows, 1), 0)
    back = lax.dot_general(
        gathered.reshape(enc_count * cols, rows),
        weight,
        (((0,), (0,)), ((), ())),
        preferred_element_type=F32,
    ).astype(BF16)
    goal = ((enc_of[0] * depth)[:, None] + token).reshape(1, rows)
    held = pick(row == goal, back)
    held = exchange(held.reshape(nx, rows // nx, width), "x").reshape(rows, width)
    unit = line // depth
    unit = unit % nx * nz + unit // nx
    held = pick(column == unit * depth + line % depth, held)
    held = exchange(held.reshape(nz, rows // nz, width), "z").reshape(rows, width)
    sender = owner_of[0]
    place = (((sender % nz * nx + sender // nz) * depth)[:, None] + token).reshape(rows, 1)
    routed = pick(column == place, held)

    block = enc_count * half // nx
    parts = pl.pallas_call(
        partial_kernel,
        out_shape=[
            jax.ShapeDtypeStruct((block, width), F32 if k == 0 else BF16) for k in range(nx)
        ],
        in_specs=[SMEM, VMEM, VMEM, VMEM, VMEM],
        out_specs=[VMEM] * nx,
        compiler_params=pltpu.CompilerParams(vmem_limit_bytes=32 * 2**20),
        cost_estimate=pl.CostEstimate(
            flops=4 * enc_count * half * rows * width,
            bytes_accessed=4 * enc_count * half * width,
            transcendentals=0,
        ),
        name="partial",
    )(hx.reshape(1), gathered, features, paired, other_features)
    parts = hand_on(parts, "x")
    total = pl.pallas_call(
        sum_x_kernel,
        out_shape=jax.ShapeDtypeStruct((block, width), BF16),
        in_specs=[VMEM] * nx,
        out_specs=VMEM,
        name="sum_x",
    )(*parts)
    split = feat_cnx.shape[1]

    sums = []
    kept = []
    for dy, gain, pre in (
        (routed[:, split:], gain_sig, pre_sig),
        (routed[:, :split], gain_cnx, pre_cnx),
    ):
        height = pre.astype(F32)
        scaled = dy.astype(F32) * gain
        kept.append((height, scaled, gain.shape[0] * enc_count))
        sums += [
            jnp.sum(height, axis=1),
            jnp.sum(height * height, axis=1),
            jnp.sum(scaled, axis=1),
            jnp.sum(scaled * height, axis=1),
        ]
    sums = broadcast_gather(jnp.stack(sums), "enc")
    sums, total = lax.optimization_barrier((sums, total))
    sums = jnp.sum(sums.reshape(enc_count, 8, rows), axis=0)
    total = exchange(total.reshape(nz, block // nz, width), "z")
    grad_cnx, grad_sig = pl.pallas_call(
        functools.partial(sum_z_kernel, 1.0 / math.sqrt(rows * nx * nz * rep_count), split),
        out_shape=[
            jax.ShapeDtypeStruct((block // nz, split), F32),
            jax.ShapeDtypeStruct((block // nz, width - split), F32),
        ],
        in_specs=[VMEM],
        out_specs=[VMEM, VMEM],
        name="sum_z",
    )(total)
    grads = []
    for index, (height, scaled, channels) in enumerate(kept):
        means = sums[index * 4 : index * 4 + 4] / channels
        mean = means[0]
        inverse = lax.rsqrt(means[1] - mean * mean + EPS)
        product = inverse * (means[3] - mean * means[2])
        grads.append(
            (
                inverse[:, None]
                * (scaled - means[2][:, None] - (height - mean[:, None]) * inverse[:, None] * product[:, None])
            ).astype(BF16)
        )
    return (grad_sig, grad_cnx, grads[0], grads[1])


def solution(mesh):
    enc, dp, rep = mesh.devices.shape
    along_x = 4 if dp == 64 else 2
    mesh = Mesh(
        mesh.devices.reshape(enc, along_x, dp // along_x, rep), ("enc", "x", "z", "rep")
    )
    owners = ("x", "z", "rep")
    both = P(owners, "enc")
    in_specs = (
        both,
        both,
        both,
        P(None, "enc"),
        P(None, "enc"),
        P(owners, None),
        P(owners, None),
        P(owners, None),
        both,
        both,
        P("enc"),
        P("enc"),
    )
    return jax.shard_map(
        shards, mesh=mesh, in_specs=in_specs, out_specs=(both,) * 4, check_vma=False
    )
```

time: 163 us -> 143 us (0.88)
  starting transfers between devices: 83 us -> 57.9 us
  local copies, waits for them, and re-layouts: 7.93 us -> 22 us
  waiting for transfers between devices: 52.7 us -> 45.9 us
  matrix products: 7.38 us -> 4.17 us
  other arithmetic: 3.37 us -> 5.79 us
    ppermute x6 -> x3, starting transfers between devices: 31.6 us -> 9.21 us  [hand_on(): lax.ppermute(blocks[k], axis, shift(count, k))]
    ppermute x6 -> x3, waiting for transfers between devices: 18.9 us -> 4.05 us  [hand_on(): lax.ppermute(blocks[k], axis, shift(count, k))]
    all_to_all x3 -> x2, starting transfers between devices: 17.2 us -> 10.5 us  [broadcast_gather(): return lax.all_to_all(copies, axis, 0, 0, tiled=True)]
    another operation x1 -> x2, local copies, waits for them, and re-layouts: 0.03 us -> 6.52 us  [the longest x1 6.5 us: shards(): jnp.stack([lax.dynamic_index_in_dim(weight, index, 2, keepdims=False).res...]
    reshape x0 -> x1, local copies, waits for them, and re-layouts: none -> 5.91 us  [shards(): weight = jnp.stack([lax.dynamic_index_in_dim(weight, index, 2, keepdims=F...]
    all_to_all x4 -> x3, waiting for transfers between devices: 25.1 us -> 29.8 us  [exchange(): return lax.all_to_all(blocks, axis, 0, 0, tiled=True)]
    all_to_all x4 -> x3, starting transfers between devices: 30.4 us -> 34.4 us  [exchange(): return lax.all_to_all(blocks, axis, 0, 0, tiled=True)]
    dot_general x2 -> x0, matrix products: 3.75 us -> none  [shards(): dy = jnp.dot(full, weight, preferred_element_type=F32).astype(BF16)]
  transfers between devices with their start and end apart: 15 -> 10, of which waited for: 11 -> 7; matrix products, arithmetic and copies ran while one was open for 4% -> 15% of each run, Pallas kernels for 3% -> 2%
where the time goes in v3:
time: 143 us; the launch traced here: 142 us
  starting transfers between devices  57.9 us (40%)
  waiting for transfers between devices  45.9 us (32%)
  local copies, waits for them, and re-layouts  22 us (15%)
  other arithmetic  5.79 us (4%)
  Pallas kernels  4.84 us (3%)
  matrix products  4.17 us (3%)
    all_to_all x3, starting transfers between devices, exchange(): return lax.all_to_all(blocks, axis, 0, 0, tiled=True)  34.4 us
    all_to_all x3, waiting for transfers between devices, exchange(): return lax.all_to_all(blocks, axis, 0, 0, tiled=True)  29.8 us
    all_to_all x2, waiting for transfers between devices, broadcast_gather(): return lax.all_to_all(copies, axis, 0, 0, tiled=True)  10.5 us
    all_to_all x2, starting transfers between devices, broadcast_gather(): return lax.all_to_all(copies, axis, 0, 0, tiled=True)  10.5 us
    ppermute x3, starting transfers between devices, hand_on(): lax.ppermute(blocks[k], axis, shift(count, k))  9.21 us
    another operation x1, local copies, waits for them, and re-layouts, shards(): jnp.stack([lax.dynamic_index_in_dim(weight, index, 2, keepdims=False).res...  6.5 us
    reshape x1, local copies, waits for them, and re-layouts, shards(): weight = jnp.stack([lax.dynamic_index_in_dim(weight, index, 2, keepdims=F...  5.91 us
    unnamed x33, local copies, waits for them, and re-layouts  5.32 us
  transfers between devices with their start and end apart: 10, of which 7 were waited for; matrix products, arithmetic and copies ran while one was open for 15% of the time, Pallas kernels for 2%

profile of v3, /device:TPU:6, one launch (start us, length us, event | category | flops | bytes accessed | tf_op | source)
XLA Modules:
  0.0 141.6 jit_solution(8146210692864866389)
XLA Ops:
  0.6 1.0 copy.46
  2.7 1.1 broadcast_in_dim.18
  3.8 7.1 %all-to-all-start = ((bf16[8,2,128,256]{3,2,1,0:T(8,128)(2,1)}), bf16[8,2,128,256]{3,2,1,0:T(8,128)(2,1)S(1)}, u32[]{:S(2)}, u32[]{:S(2)}) async-start(bf16[8,2,128,256]{3,2,1,0:T(8,128)(2,1)} %broadcast_in_dim.18), calls=%async_computation | async-start | bytes 2097152 | tf_op jit(solution)/shard_map/all_to_all | solution.py:26
  11.0 1.9 %collective-permute-start = (bf16[256,528]{1,0:T(8,128)(2,1)S(1)}, bf16[256,528]{1,0:T(8,128)(2,1)S(1)}, u32[]{:S(2)}, u32[]{:S(2)}) collective-permute-start(bf16[256,528]{1,0:T(8,128)(2,1)S(1)} %pad_maximum_fusion.2.own_ref), channel_id=1, source_target_pairs={{0,1},{1,0},{2,3},{3,2},{4,5},{5,4},{6,7},{7,6},{8,9},{9,8},{10,11... | collective-permute-start | bytes 811016 | tf_op jit(solution)/shard_map/ppermute | solution.py:111
  13.5 1.7 %pad_maximum_fusion = bf16[2048,528]{1,0:T(8,128)(2,1)S(1)} fusion(bf16[2048,144]{1,0:T(8,128)(2,1)S(1)} %copy.48, bf16[2048,384]{1,0:T(8,128)(2,1)} %param.16), kind=kLoop, calls=%fused_computation | loop fusion | flops 4325376 | bytes 4325376 | tf_op jit(solution)/shard_map/concatenate | solution.py:112
  15.8 1.9 %pad_maximum_fusion.1 = bf16[8,2,128,528]{3,2,0,1:T(8,128)(2,1)} fusion(bf16[8,1,128,528]{3,2,0,1:T(8,128)(2,1)S(1)} %bitcast.64, bf16[8,1,128,528]{3,2,0,1:T(8,128)(2,1)S(1)} %bitcast.63), kind=kLoop, calls=%fused_computation.1 | loop fusion | flops 1081344 | bytes 4325376 | tf_op jit(solution)/shard_map/stack | solution.py:115
  17.8 6.5 %copy.51 = bf16[8,2,128,528]{2,1,0,3:T(2,128)(2,1)} copy(bf16[8,2,128,528]{3,2,0,1:T(8,128)(2,1)} %pad_maximum_fusion.1) | data formatting | bytes 4325376 | tf_op jit(solution)/shard_map/stack | solution.py:115
  24.3 5.9 %reshape.329 = bf16[2048,528]{0,1:T(8,128)(2,1)} reshape(bf16[8,2,128,528]{2,1,0,3:T(2,128)(2,1)} %copy.51) | data formatting | bytes 4325376 | tf_op jit(solution)/shard_map/reshape | solution.py:121
  30.4 9.3 %all-to-all-done.gathered_ref = bf16[8,2,128,256]{3,2,1,0:T(8,128)(2,1)S(1)} async-done(((bf16[8,2,128,256]{3,2,1,0:T(8,128)(2,1)}), bf16[8,2,128,256]{3,2,1,0:T(8,128)(2,1)S(1)}, u32[]{:S(2)}, u32[]{:S(2)}) %all-to-all-start) | async-done | bytes 1048608 | tf_op jit(solution)/shard_map/all_to_all | solution.py:26
  39.6 2.5 %convolution_convert_fusion.3 = bf16[256,528]{0,1:T(8,128)(2,1)S(1)} fusion(bf16[2048,528]{0,1:T(8,128)(2,1)} %reshape.329, bf16[2048,256]{1,0:T(8,128)(2,1)S(1)} %bitcast.61, s32[256]{0:T(256)S(1)} %add.142), kind=kOutput, calls=%fused_computation.5 | convolution fusion | flops 623190016 | bytes 3482624 | tf_op jit(solution)/shard_map/dot_general | solution.py:39
  42.2 0.9 copy.52
  43.1 4.8 %all-to-all-start.1 = ((bf16[4,64,528]{2,1,0:T(8,128)(2,1)}), bf16[4,64,528]{2,1,0:T(8,128)(2,1)S(1)}, u32[]{:S(2)}, u32[]{:S(2)}) async-start(bf16[4,64,528]{2,1,0:T(8,128)(2,1)} %bitcast.14), calls=%async_computation.1 | async-start | bytes 655360 | tf_op jit(solution)/shard_map/all_to_all | solution.py:30
  47.8 5.5 %all-to-all-done.1 = bf16[4,64,528]{2,1,0:T(8,128)(2,1)S(1)} async-done(((bf16[4,64,528]{2,1,0:T(8,128)(2,1)}), bf16[4,64,528]{2,1,0:T(8,128)(2,1)S(1)}, u32[]{:S(2)}, u32[]{:S(2)}) %all-to-all-start.1) | async-done | bytes 270368 | tf_op jit(solution)/shard_map/all_to_all | solution.py:30
  53.7 0.9 copy.53
  54.6 18.9 %all-to-all-start.2 = ((bf16[16,16,528]{2,1,0:T(8,128)(2,1)}), bf16[16,16,528]{2,1,0:T(8,128)(2,1)}, u32[]{:S(2)}, u32[]{:S(2)}) async-start(bf16[16,16,528]{2,1,0:T(8,128)(2,1)} %bitcast.16), calls=%async_computation.2 | async-start | bytes 655360 | tf_op jit(solution)/shard_map/all_to_all | solution.py:30
  73.6 1.9 %collective-permute-start.1 = (bf16[8,128,256]{2,1,0:T(8,128)(2,1)S(1)}, bf16[8,128,256]{2,1,0:T(8,128)(2,1)S(1)}, u32[]{:S(2)}, u32[]{:S(2)}) collective-permute-start(bf16[8,128,256]{2,1,0:T(8,128)(2,1)S(1)} %slice_bitcast_fusion), channel_id=1, source_target_pairs={{0,1},{1,0},{2,3},{3,2},{4,5},{5,4},{6,7},{7,6},{8,9},{9,8},{10,11... | collective-permute-start | bytes 1572872 | tf_op jit(solution)/shard_map/ppermute | solution.py:124
  75.9 1.5 %collective-permute-done.1.paired_ref = bf16[8,128,256]{2,1,0:T(8,128)(2,1)S(1)} collective-permute-done((bf16[8,128,256]{2,1,0:T(8,128)(2,1)S(1)}, bf16[8,128,256]{2,1,0:T(8,128)(2,1)S(1)}, u32[]{:S(2)}, u32[]{:S(2)}) %collective-permute-start.1) | collective-permute-done | bytes 524320 | tf_op jit(solution)/shard_map/ppermute | solution.py:124
  77.4 1.0 partial.1
  78.4 0.8 copy-done
  79.2 4.0 %collective-permute-start.2 = (bf16[256,528]{1,0:T(8,128)(2,1)S(1)}, bf16[256,528]{1,0:T(8,128)(2,1)S(1)}, u32[]{:S(2)}, u32[]{:S(2)}) collective-permute-start(bf16[256,528]{1,0:T(8,128)(2,1)S(1)} %get-tuple-element.19), channel_id=1, source_target_pairs={{0,32},{32,64},{64,96},{96,0},{1,33},{33,65},{65,97},{97,1},{2,34}... | collective-permute-start | bytes 811016 | tf_op jit(solution)/shard_map/ppermute | solution.py:35
  83.2 1.9 %collective-permute-start.3 = (bf16[256,528]{1,0:T(8,128)(2,1)S(1)}, bf16[256,528]{1,0:T(8,128)(2,1)S(1)}, u32[]{:S(2)}, u32[]{:S(2)}) collective-permute-start(bf16[256,528]{1,0:T(8,128)(2,1)S(1)} %get-tuple-element.20), channel_id=1, source_target_pairs={{0,64},{32,96},{64,0},{96,32},{1,65},{33,97},{65,1},{97,33},{2,66}... | collective-permute-start | bytes 811016 | tf_op jit(solution)/shard_map/ppermute | solution.py:35
  85.1 3.3 %collective-permute-start.4 = (bf16[256,528]{1,0:T(8,128)(2,1)S(1)}, bf16[256,528]{1,0:T(8,128)(2,1)S(1)}, u32[]{:S(2)}, u32[]{:S(2)}) collective-permute-start(bf16[256,528]{1,0:T(8,128)(2,1)S(1)} %get-tuple-element.21), channel_id=1, source_target_pairs={{0,96},{32,0},{64,32},{96,64},{1,97},{33,1},{65,33},{97,65},{2,98}... | collective-permute-start | bytes 811016 | tf_op jit(solution)/shard_map/ppermute | solution.py:35
  88.5 4.9 %all-to-all-done.2 = bf16[16,16,528]{2,1,0:T(8,128)(2,1)} async-done(((bf16[16,16,528]{2,1,0:T(8,128)(2,1)}), bf16[16,16,528]{2,1,0:T(8,128)(2,1)}, u32[]{:S(2)}, u32[]{:S(2)}) %all-to-all-start.2) | async-done | bytes 270368 | tf_op jit(solution)/shard_map/all_to_all | solution.py:30
  93.4 1.3 convolution_convert_fusion.1
  95.6 3.4 %all-to-all-start.3 = ((f32[8,8,256]{2,1,0:T(8,128)}), f32[8,8,256]{2,1,0:T(8,128)S(1)}, u32[]{:S(2)}, u32[]{:S(2)}) async-start(f32[8,8,256]{2,1,0:T(8,128)} %broadcast_in_dim.19), calls=%async_computation.3 | async-start | bytes 131072 | tf_op jit(solution)/shard_map/all_to_all | solution.py:26
  99.0 4.0 %collective-permute-done.4.refs_2_ = bf16[256,528]{1,0:T(8,128)(2,1)S(1)} collective-permute-done((bf16[256,528]{1,0:T(8,128)(2,1)S(1)}, bf16[256,528]{1,0:T(8,128)(2,1)S(1)}, u32[]{:S(2)}, u32[]{:S(2)}) %collective-permute-start.4) | collective-permute-done | bytes 270368 | tf_op jit(solution)/shard_map/ppermute | solution.py:35
  103.8 2.2 %sum_x.1 = bf16[256,528]{1,0:T(8,128)(2,1)} custom-call(f32[256,528]{1,0:T(8,128)} %copy-done, bf16[256,528]{1,0:T(8,128)(2,1)} %copy-done.3, bf16[256,528]{1,0:T(8,128)(2,1)} %copy-done.4, bf16[256,528]{1,0:T(8,128)(2,1)} %copy-done.5), custom_call_target="tpu_custom_call" | custom-call | tf_op jit(solution)/shard_map/sum_x/pallas_call | solution.py:163
  106.1 1.2 all-to-all-done.3
  107.3 10.7 %all-to-all-start.4 = ((bf16[16,16,528]{2,1,0:T(8,128)(2,1)}), bf16[16,16,528]{2,1,0:T(8,128)(2,1)S(1)}, u32[]{:S(2)}, u32[]{:S(2)}) async-start(bf16[16,16,528]{2,1,0:T(8,128)(2,1)} %bitcast.66), calls=%async_computation.4 | async-start | bytes 655360 | tf_op jit(solution)/shard_map/all_to_all | solution.py:30
  118.3 0.8 copy.56
  119.8 19.4 %all-to-all-done.4.parts_ref = bf16[16,16,528]{2,1,0:T(8,128)(2,1)S(1)} async-done(((bf16[16,16,528]{2,1,0:T(8,128)(2,1)}), bf16[16,16,528]{2,1,0:T(8,128)(2,1)S(1)}, u32[]{:S(2)}, u32[]{:S(2)}) %all-to-all-start.4) | async-done | bytes 270368 | tf_op jit(solution)/shard_map/all_to_all | solution.py:30
  140.0 1.6 %sum_z.1 = (f32[16,384]{1,0:T(8,128)}, f32[16,144]{1,0:T(8,128)}) custom-call(bf16[16,16,528]{2,1,0:T(8,128)(2,1)} %copy-done.1), custom_call_target="tpu_custom_call" | custom-call | tf_op jit(solution)/shard_map/sum_z/pallas_call | solution.py:191
  (60 shorter events, 6.5 us)
Async XLA Ops:
  0.6 10.2 %copy-start.9 = (bf16[256,144]{0,1:T(8,128)(2,1)S(1)}, bf16[256,144]{0,1:T(8,128)(2,1)}, u32[]{:S(2)}) copy-start(bf16[256,144]{0,1:T(8,128)(2,1)} %param.12) | copy-start | bytes 221188
  1.7 9.3 %copy-start.8 = (bf16[256,384]{1,0:T(8,128)(2,1)S(1)}, bf16[256,384]{1,0:T(8,128)(2,1)}, u32[]{:S(2)}) copy-start(bf16[256,384]{1,0:T(8,128)(2,1)} %param.13) | copy-start | bytes 589828
  2.6 10.3 %copy-start.2 = (bf16[2048,144]{0,1:T(8,128)(2,1)S(1)}, bf16[2048,144]{0,1:T(8,128)(2,1)}, u32[]{:S(2)}) copy-start(bf16[2048,144]{0,1:T(8,128)(2,1)} %param.15) | copy-start | bytes 1769476
  3.8 35.8 %all-to-all-start = ((bf16[8,2,128,256]{3,2,1,0:T(8,128)(2,1)}), bf16[8,2,128,256]{3,2,1,0:T(8,128)(2,1)S(1)}, u32[]{:S(2)}, u32[]{:S(2)}) async-start(bf16[8,2,128,256]{3,2,1,0:T(8,128)(2,1)} %broadcast_in_dim.18), calls=%async_computation | async-start | bytes 2097152 | tf_op jit(solution)/shard_map/all_to_all | solution.py:26
  11.0 19.3 %collective-permute-start = (bf16[256,528]{1,0:T(8,128)(2,1)S(1)}, bf16[256,528]{1,0:T(8,128)(2,1)S(1)}, u32[]{:S(2)}, u32[]{:S(2)}) collective-permute-start(bf16[256,528]{1,0:T(8,128)(2,1)S(1)} %pad_maximum_fusion.2.own_ref), channel_id=1, source_target_pairs={{0,1},{1,0},{2,3},{3,2},{4,5},{5,4},{6,7},{7,6},{8,9},{9,8},{10,11... | collective-permute-start | bytes 811016 | tf_op jit(solution)/shard_map/ppermute | solution.py:111
  15.2 0.7 copy-start.12
  42.1 33.4 %copy-start.13 = (s32[1,64]{1,0:T(1,128)S(1)}, s32[1,64]{1,0:T(1,128)}, u32[]{:S(2)}) copy-start(s32[1,64]{1,0:T(1,128)} %param.19) | copy-start | bytes 772
  42.1 33.6 %copy-start.7 = (bf16[256,384]{1,0:T(8,128)(2,1)S(1)}, bf16[256,384]{1,0:T(8,128)(2,1)}, u32[]{:S(2)}) copy-start(bf16[256,384]{1,0:T(8,128)(2,1)} %param.21) | copy-start | bytes 589828
  43.1 10.3 %all-to-all-start.1 = ((bf16[4,64,528]{2,1,0:T(8,128)(2,1)}), bf16[4,64,528]{2,1,0:T(8,128)(2,1)S(1)}, u32[]{:S(2)}, u32[]{:S(2)}) async-start(bf16[4,64,528]{2,1,0:T(8,128)(2,1)} %bitcast.14), calls=%async_computation.1 | async-start | bytes 655360 | tf_op jit(solution)/shard_map/all_to_all | solution.py:30
  54.6 38.8 %all-to-all-start.2 = ((bf16[16,16,528]{2,1,0:T(8,128)(2,1)}), bf16[16,16,528]{2,1,0:T(8,128)(2,1)}, u32[]{:S(2)}, u32[]{:S(2)}) async-start(bf16[16,16,528]{2,1,0:T(8,128)(2,1)} %bitcast.16), calls=%async_computation.2 | async-start | bytes 655360 | tf_op jit(solution)/shard_map/all_to_all | solution.py:30
  73.5 21.2 %copy-start.6 = (bf16[256,144]{0,1:T(8,128)(2,1)S(1)}, bf16[256,144]{0,1:T(8,128)(2,1)}, u32[]{:S(2)}) copy-start(bf16[256,144]{0,1:T(8,128)(2,1)} %param.20) | copy-start | bytes 221188
  73.5 21.2 %copy-start.11 = (f32[144]{0:T(256)S(1)}, f32[144]{0:T(256)}, u32[]{:S(2)}) copy-start(f32[144]{0:T(256)} %param.22) | copy-start | bytes 1732
  73.5 21.3 %copy-start.10 = (f32[384]{0:T(512)S(1)}, f32[384]{0:T(512)}, u32[]{:S(2)}) copy-start(f32[384]{0:T(512)} %param.23) | copy-start | bytes 4612
  73.6 3.8 %collective-permute-start.1 = (bf16[8,128,256]{2,1,0:T(8,128)(2,1)S(1)}, bf16[8,128,256]{2,1,0:T(8,128)(2,1)S(1)}, u32[]{:S(2)}, u32[]{:S(2)}) collective-permute-start(bf16[8,128,256]{2,1,0:T(8,128)(2,1)S(1)} %slice_bitcast_fusion), channel_id=1, source_target_pairs={{0,1},{1,0},{2,3},{3,2},{4,5},{5,4},{6,7},{7,6},{8,9},{9,8},{10,11... | collective-permute-start | bytes 1572872 | tf_op jit(solution)/shard_map/ppermute | solution.py:124
  78.4 0.8 copy-start
  79.2 19.8 %collective-permute-start.2 = (bf16[256,528]{1,0:T(8,128)(2,1)S(1)}, bf16[256,528]{1,0:T(8,128)(2,1)S(1)}, u32[]{:S(2)}, u32[]{:S(2)}) collective-permute-start(bf16[256,528]{1,0:T(8,128)(2,1)S(1)} %get-tuple-element.19), channel_id=1, source_target_pairs={{0,32},{32,64},{64,96},{96,0},{1,33},{33,65},{65,97},{97,1},{2,34}... | collective-permute-start | bytes 811016 | tf_op jit(solution)/shard_map/ppermute | solution.py:35
  83.2 15.8 %collective-permute-start.3 = (bf16[256,528]{1,0:T(8,128)(2,1)S(1)}, bf16[256,528]{1,0:T(8,128)(2,1)S(1)}, u32[]{:S(2)}, u32[]{:S(2)}) collective-permute-start(bf16[256,528]{1,0:T(8,128)(2,1)S(1)} %get-tuple-element.20), channel_id=1, source_target_pairs={{0,64},{32,96},{64,0},{96,32},{1,65},{33,97},{65,1},{97,33},{2,66}... | collective-permute-start | bytes 811016 | tf_op jit(solution)/shard_map/ppermute | solution.py:35
  85.1 18.0 %collective-permute-start.4 = (bf16[256,528]{1,0:T(8,128)(2,1)S(1)}, bf16[256,528]{1,0:T(8,128)(2,1)S(1)}, u32[]{:S(2)}, u32[]{:S(2)}) collective-permute-start(bf16[256,528]{1,0:T(8,128)(2,1)S(1)} %get-tuple-element.21), channel_id=1, source_target_pairs={{0,96},{32,0},{64,32},{96,64},{1,97},{33,1},{65,33},{97,65},{2,98}... | collective-permute-start | bytes 811016 | tf_op jit(solution)/shard_map/ppermute | solution.py:35
  95.6 11.7 %all-to-all-start.3 = ((f32[8,8,256]{2,1,0:T(8,128)}), f32[8,8,256]{2,1,0:T(8,128)S(1)}, u32[]{:S(2)}, u32[]{:S(2)}) async-start(f32[8,8,256]{2,1,0:T(8,128)} %broadcast_in_dim.19), calls=%async_computation.3 | async-start | bytes 131072 | tf_op jit(solution)/shard_map/all_to_all | solution.py:26
  99.0 4.1 %copy-start.3 = (bf16[256,528]{1,0:T(8,128)(2,1)}, bf16[256,528]{1,0:T(8,128)(2,1)S(1)}, u32[]{:S(2)}) copy-start(bf16[256,528]{1,0:T(8,128)(2,1)S(1)} %collective-permute-done.2.refs_0_) | copy-start | bytes 811012
  99.0 4.1 %copy-start.4 = (bf16[256,528]{1,0:T(8,128)(2,1)}, bf16[256,528]{1,0:T(8,128)(2,1)S(1)}, u32[]{:S(2)}) copy-start(bf16[256,528]{1,0:T(8,128)(2,1)S(1)} %collective-permute-done.3.refs_1_) | copy-start | bytes 811012
  103.1 0.7 copy-start.5
  107.3 31.9 %all-to-all-start.4 = ((bf16[16,16,528]{2,1,0:T(8,128)(2,1)}), bf16[16,16,528]{2,1,0:T(8,128)(2,1)S(1)}, u32[]{:S(2)}, u32[]{:S(2)}) async-start(bf16[16,16,528]{2,1,0:T(8,128)(2,1)} %bitcast.66), calls=%async_computation.4 | async-start | bytes 655360 | tf_op jit(solution)/shard_map/all_to_all | solution.py:30
  139.2 0.7 copy-start.1

commit v4 on v3

--- a/solution.py
+++ b/solution.py
@@ -53,20 +53,19 @@
             ).astype(out.dtype)
 
 
-def sum_x_kernel(own_ref, *refs):
-    total = own_ref[...]
-    for ref in refs[:-1]:
-        total += ref[...].astype(F32)
-    refs[-1][...] = total.astype(BF16)
-
-
-def sum_z_kernel(scale, split, parts_ref, cnx_ref, sig_ref):
-    total = parts_ref[0].astype(F32)
-    for k in range(1, parts_ref.shape[0]):
-        total += parts_ref[k].astype(F32)
-    total *= scale
-    cnx_ref[...] = total[:, :split]
-    sig_ref[...] = total[:, split:]
+def norm_kernel(channels, sums_ref, dy_ref, gain_ref, cnx_ref, sig_ref, cnx_out, sig_out):
+    sums = sums_ref[...].T
+    start = 0
+    for index, (pre, out) in enumerate(((cnx_ref, cnx_out), (sig_ref, sig_out))):
+        means = sums[:, index * 4 : index * 4 + 4] * (1.0 / channels[index])
+        mean, grad_mean = means[:, 0:1], means[:, 2:3]
+        inverse = lax.rsqrt(means[:, 1:2] - mean * mean + EPS)
+        product = inverse * inverse * (means[:, 3:4] - mean * grad_mean)
+        at = slice(start, start + pre.shape[1])
+        scaled = dy_ref[:, at].astype(F32) * gain_ref[:, at]
+        height = pre[...].astype(F32)
+        out[...] = (inverse * (scaled - grad_mean - (height - mean) * product)).astype(BF16)
+        start += pre.shape[1]
 
 
 def shards(
@@ -123,26 +122,6 @@
 
     paired = lax.ppermute(gathered[:, 1], "rep", swap)
 
-    row = lax.broadcasted_iota(jnp.int32, (rows, rows), 0)
-    column = lax.broadcasted_iota(jnp.int32, (rows, rows), 1)
-    line = lax.broadcasted_iota(jnp.int32, (rows, 1), 0)
-    back = lax.dot_general(
-        gathered.reshape(enc_count * cols, rows),
-        weight,
-        (((0,), (0,)), ((), ())),
-        preferred_element_type=F32,
-    ).astype(BF16)
-    goal = ((enc_of[0] * depth)[:, None] + token).reshape(1, rows)
-    held = pick(row == goal, back)
-    held = exchange(held.reshape(nx, rows // nx, width), "x").reshape(rows, width)
-    unit = line // depth
-    unit = unit % nx * nz + unit // nx
-    held = pick(column == unit * depth + line % depth, held)
-    held = exchange(held.reshape(nz, rows // nz, width), "z").reshape(rows, width)
-    sender = owner_of[0]
-    place = (((sender % nz * nx + sender // nz) * depth)[:, None] + token).reshape(rows, 1)
-    routed = pick(column == place, held)
-
     block = enc_count * half // nx
     parts = pl.pallas_call(
         partial_kernel,
@@ -159,58 +138,64 @@
         ),
         name="partial",
     )(hx.reshape(1), gathered, features, paired, other_features)
+
+    row = lax.broadcasted_iota(jnp.int32, (rows, rows), 0)
+    column = lax.broadcasted_iota(jnp.int32, (rows, rows), 1)
+    line = lax.broadcasted_iota(jnp.int32, (rows, 1), 0)
+    back = lax.dot_general(
+        gathered.reshape(enc_count * cols, rows),
+        weight,
+        (((0,), (0,)), ((), ())),
+        preferred_element_type=F32,
+    ).astype(BF16)
+    goal = ((enc_of[0] * depth)[:, None] + token).reshape(1, rows)
+    held = pick(row == goal, back)
+    held = exchange(held.reshape(nx, rows // nx, width), "x").reshape(rows, width)
+    unit = line // depth
+    unit = unit % nx * nz + unit // nx
+    held = pick(column == unit * depth + line % depth, held)
+    held, parts = lax.optimization_barrier((held, parts))
+    held = exchange(held.reshape(nz, rows // nz, width), "z").reshape(rows, width)
+    sender = owner_of[0]
+    place = (((sender % nz * nx + sender // nz) * depth)[:, None] + token).reshape(rows, 1)
+    routed = pick(column == place, held)
+
     parts = hand_on(parts, "x")
-    total = pl.pallas_call(
-        sum_x_kernel,
-        out_shape=jax.ShapeDtypeStruct((block, width), BF16),
-        in_specs=[VMEM] * nx,
-        out_specs=VMEM,
-        name="sum_x",
-    )(*parts)
+    total = sum((part.astype(F32) for part in parts[1:]), parts[0]).astype(BF16)
     split = feat_cnx.shape[1]
 
     sums = []
-    kept = []
     for dy, gain, pre in (
+        (routed[:, :split], gain_cnx, pre_cnx),
         (routed[:, split:], gain_sig, pre_sig),
-        (routed[:, :split], gain_cnx, pre_cnx),
     ):
         height = pre.astype(F32)
         scaled = dy.astype(F32) * gain
-        kept.append((height, scaled, gain.shape[0] * enc_count))
         sums += [
             jnp.sum(height, axis=1),
             jnp.sum(height * height, axis=1),
             jnp.sum(scaled, axis=1),
             jnp.sum(scaled * height, axis=1),
         ]
-    sums = broadcast_gather(jnp.stack(sums), "enc")
-    sums, total = lax.optimization_barrier((sums, total))
-    sums = jnp.sum(sums.reshape(enc_count, 8, rows), axis=0)
+    sums, total = lax.optimization_barrier((jnp.stack(sums), total))
     total = exchange(total.reshape(nz, block // nz, width), "z")
-    grad_cnx, grad_sig = pl.pallas_call(
-        functools.partial(sum_z_kernel, 1.0 / math.sqrt(rows * nx * nz * rep_count), split),
+    sums = lax.psum(sums, "enc")
+    before_cnx, before_sig = pl.pallas_call(
+        functools.partial(
+            norm_kernel, (gain_cnx.shape[0] * enc_count, gain_sig.shape[0] * enc_count)
+        ),
         out_shape=[
-            jax.ShapeDtypeStruct((block // nz, split), F32),
-            jax.ShapeDtypeStruct((block // nz, width - split), F32),
+            jax.ShapeDtypeStruct(pre_cnx.shape, BF16),
+            jax.ShapeDtypeStruct(pre_sig.shape, BF16),
         ],
-        in_specs=[VMEM],
-        out_specs=[VMEM, VMEM],
-        name="sum_z",
-    )(total)
-    grads = []
-    for index, (height, scaled, channels) in enumerate(kept):
-        means = sums[index * 4 : index * 4 + 4] / channels
-        mean = means[0]
-        inverse = lax.rsqrt(means[1] - mean * mean + EPS)
-        product = inverse * (means[3] - mean * means[2])
-        grads.append(
-            (
-                inverse[:, None]
-                * (scaled - means[2][:, None] - (height - mean[:, None]) * inverse[:, None] * product[:, None])
-            ).astype(BF16)
-        )
-    return (grad_sig, grad_cnx, grads[0], grads[1])
+        in_specs=[VMEM] * 5,
+        out_specs=[VMEM] * 2,
+        cost_estimate=pl.CostEstimate(flops=1, bytes_accessed=1, transcendentals=0),
+        name="norm",
+    )(sums, routed, jnp.concatenate([gain_cnx, gain_sig])[None, :], pre_cnx, pre_sig)
+    total = jnp.sum(total.astype(F32), axis=0) * (1.0 / math.sqrt(rows * nx * nz * rep_count))
+    grad_cnx, grad_sig = total[:, :split], total[:, split:]
+    return (grad_sig, grad_cnx, before_sig, before_cnx)
 
 
 def solution(mesh):

time: 143 us -> 139 us (0.972)
  waiting for transfers between devices: 45.9 us -> 28.3 us
  blocking collectives: 0 us -> 15.5 us
  starting transfers between devices: 57.9 us -> 55.5 us
  local copies, waits for them, and re-layouts: 22 us -> 24.1 us
    all_to_all x3, waiting for transfers between devices: 29.8 us -> 6.63 us  [exchange(): return lax.all_to_all(blocks, axis, 0, 0, tiled=True)]
    psum x0 -> x1, blocking collectives: none -> 15.5 us  [shards(): sums = lax.psum(sums, 'enc')]
    ppermute x3, waiting for transfers between devices: 4.05 us -> 12.4 us  [hand_on(): lax.ppermute(blocks[k], axis, shift(count, k))]
    all_to_all x2 -> x1, starting transfers between devices: 10.5 us -> 7.1 us  [broadcast_gather(): return lax.all_to_all(copies, axis, 0, 0, tiled=True)]
    optimization_barrier x0 -> x1, local copies, waits for them, and re-layouts: none -> 1.9 us  [shards(): held, parts = lax.optimization_barrier((held, parts))]
    ppermute x1, waiting for transfers between devices: 1.5 us -> 0.01 us  [shards(): paired = lax.ppermute(gathered[:, 1], 'rep', swap)]
    all_to_all x2 -> x1, waiting for transfers between devices: 10.5 us -> 9.29 us  [broadcast_gather(): return lax.all_to_all(copies, axis, 0, 0, tiled=True)]
    pallas_call x2 -> x1, Pallas kernels: 3.86 us -> 2.74 us  [shards(): pl.pallas_call(functools.partial(norm_kernel, (gain_cnx.shape[0] * enc_co...]
  transfers between devices with their start and end apart: 10 -> 9, of which waited for: 7 -> 6; matrix products, arithmetic and copies ran while one was open for 15% -> 19% of each run, Pallas kernels for 2% -> 2%
where the time goes in v4:
time: 139 us; the launch traced here: 138 us
  starting transfers between devices  55.5 us (40%)
  waiting for transfers between devices  28.3 us (20%)
  local copies, waits for them, and re-layouts  24.1 us (17%)
  blocking collectives  15.5 us (11%)
  other arithmetic  6.02 us (4%)
  matrix products  3.89 us (3%)
  Pallas kernels  3.73 us (3%)
    all_to_all x3, starting transfers between devices, exchange(): return lax.all_to_all(blocks, axis, 0, 0, tiled=True)  35.4 us
    psum x1, blocking collectives, shards(): sums = lax.psum(sums, 'enc')  15.5 us
    ppermute x3, waiting for transfers between devices, hand_on(): lax.ppermute(blocks[k], axis, shift(count, k))  12.4 us
    all_to_all x1, waiting for transfers between devices, broadcast_gather(): return lax.all_to_all(copies, axis, 0, 0, tiled=True)  9.29 us
    ppermute x3, starting transfers between devices, hand_on(): lax.ppermute(blocks[k], axis, shift(count, k))  9.21 us
    all_to_all x1, starting transfers between devices, broadcast_gather(): return lax.all_to_all(copies, axis, 0, 0, tiled=True)  7.1 us
    all_to_all x3, waiting for transfers between devices, exchange(): return lax.all_to_all(blocks, axis, 0, 0, tiled=True)  6.63 us
    another operation x1, local copies, waits for them, and re-layouts, shards(): jnp.stack([lax.dynamic_index_in_dim(weight, index, 2, keepdims=False).res...  6.49 us
  transfers between devices with their start and end apart: 9, of which 6 were waited for; matrix products, arithmetic and copies ran while one was open for 19% of the time, Pallas kernels for 2%

profile of v4, /device:TPU:6, one launch (start us, length us, event | category | flops | bytes accessed | tf_op | source)
XLA Modules:
  0.0 138.1 jit_solution(7992665142189726708)
XLA Ops:
  0.6 1.0 copy.52
  1.7 0.8 iota_compare_fusion.6
  2.7 1.1 broadcast_in_dim.27
  3.8 7.1 %all-to-all-start = ((bf16[8,2,128,256]{3,2,1,0:T(8,128)(2,1)}), bf16[8,2,128,256]{3,2,1,0:T(8,128)(2,1)S(1)}, u32[]{:S(2)}, u32[]{:S(2)}) async-start(bf16[8,2,128,256]{3,2,1,0:T(8,128)(2,1)} %broadcast_in_dim.27), calls=%async_computation | async-start | bytes 2097152 | tf_op jit(solution)/shard_map/all_to_all | solution.py:26
  11.1 1.9 %collective-permute-start = (bf16[256,528]{1,0:T(8,128)(2,1)S(1)}, bf16[256,528]{1,0:T(8,128)(2,1)S(1)}, u32[]{:S(2)}, u32[]{:S(2)}) collective-permute-start(bf16[256,528]{1,0:T(8,128)(2,1)S(1)} %pad_maximum_fusion.2.own_ref), channel_id=1, source_target_pairs={{0,1},{1,0},{2,3},{3,2},{4,5},{5,4},{6,7},{7,6},{8,9},{9,8},{10,11... | collective-permute-start | bytes 811016 | tf_op jit(solution)/shard_map/ppermute | solution.py:110
  13.5 1.7 %pad_maximum_fusion = bf16[2048,528]{1,0:T(8,128)(2,1)S(1)} fusion(bf16[2048,144]{1,0:T(8,128)(2,1)S(1)} %copy.54, bf16[2048,384]{1,0:T(8,128)(2,1)} %param.16), kind=kLoop, calls=%fused_computation | loop fusion | flops 4325376 | bytes 4325376 | tf_op jit(solution)/shard_map/concatenate | solution.py:111
  15.9 1.9 %pad_maximum_fusion.1 = bf16[8,2,128,528]{3,2,0,1:T(8,128)(2,1)} fusion(bf16[8,1,128,528]{3,2,0,1:T(8,128)(2,1)S(1)} %bitcast.56, bf16[8,1,128,528]{3,2,0,1:T(8,128)(2,1)S(1)} %bitcast.55), kind=kLoop, calls=%fused_computation.1 | loop fusion | flops 1081344 | bytes 4325376 | tf_op jit(solution)/shard_map/stack | solution.py:114
  17.8 6.5 %copy.57 = bf16[8,2,128,528]{2,1,0,3:T(2,128)(2,1)} copy(bf16[8,2,128,528]{3,2,0,1:T(8,128)(2,1)} %pad_maximum_fusion.1) | data formatting | bytes 4325376 | tf_op jit(solution)/shard_map/stack | solution.py:114
  24.3 5.9 %reshape.260 = bf16[2048,528]{0,1:T(8,128)(2,1)} reshape(bf16[8,2,128,528]{2,1,0,3:T(2,128)(2,1)} %copy.57) | data formatting | bytes 4325376 | tf_op jit(solution)/shard_map/reshape | solution.py:120
  30.4 9.3 %all-to-all-done.gathered_ref = bf16[8,2,128,256]{3,2,1,0:T(8,128)(2,1)S(1)} async-done(((bf16[8,2,128,256]{3,2,1,0:T(8,128)(2,1)}), bf16[8,2,128,256]{3,2,1,0:T(8,128)(2,1)S(1)}, u32[]{:S(2)}, u32[]{:S(2)}) %all-to-all-start) | async-done | bytes 1048608 | tf_op jit(solution)/shard_map/all_to_all | solution.py:26
  39.7 1.9 %collective-permute-start.1 = (bf16[8,128,256]{2,1,0:T(8,128)(2,1)S(1)}, bf16[8,128,256]{2,1,0:T(8,128)(2,1)S(1)}, u32[]{:S(2)}, u32[]{:S(2)}) collective-permute-start(bf16[8,128,256]{2,1,0:T(8,128)(2,1)S(1)} %slice_bitcast_fusion), channel_id=1, source_target_pairs={{0,1},{1,0},{2,3},{3,2},{4,5},{5,4},{6,7},{7,6},{8,9},{9,8},{10,11... | collective-permute-start | bytes 1572872 | tf_op jit(solution)/shard_map/ppermute | solution.py:123
  41.6 2.5 %convolution_convert_fusion.3 = bf16[256,528]{0,1:T(8,128)(2,1)S(1)} fusion(bf16[2048,528]{0,1:T(8,128)(2,1)} %reshape.260, bf16[2048,256]{1,0:T(8,128)(2,1)S(1)} %bitcast.53, s32[256]{0:T(256)S(1)} %add.133), kind=kOutput, calls=%fused_computation.5 | convolution fusion | flops 623190016 | bytes 3482624 | tf_op jit(solution)/shard_map/dot_general | solution.py:39
  44.1 0.9 copy.58
  45.0 4.8 %all-to-all-start.1 = ((bf16[4,64,528]{2,1,0:T(8,128)(2,1)}), bf16[4,64,528]{2,1,0:T(8,128)(2,1)S(1)}, u32[]{:S(2)}, u32[]{:S(2)}) async-start(bf16[4,64,528]{2,1,0:T(8,128)(2,1)} %bitcast.14), calls=%async_computation.1 | async-start | bytes 655360 | tf_op jit(solution)/shard_map/all_to_all | solution.py:30
  49.8 6.0 %all-to-all-done.1 = bf16[4,64,528]{2,1,0:T(8,128)(2,1)S(1)} async-done(((bf16[4,64,528]{2,1,0:T(8,128)(2,1)}), bf16[4,64,528]{2,1,0:T(8,128)(2,1)S(1)}, u32[]{:S(2)}, u32[]{:S(2)}) %all-to-all-start.1) | async-done | bytes 270368 | tf_op jit(solution)/shard_map/all_to_all | solution.py:30
  55.8 1.1 convolution_convert_fusion.2
  56.8 1.0 partial.1
  57.8 0.7 copy-done
  58.5 1.9 %copy.60 = bf16[256,528]{1,0:T(8,128)(2,1)} copy(bf16[256,528]{0,1:T(8,128)(2,1)} %convolution_convert_fusion.2) | data formatting | bytes 540672 | tf_op jit(solution)/shard_map/optimization_barrier | solution.py:157
  60.4 18.9 %all-to-all-start.2 = ((bf16[16,16,528]{2,1,0:T(8,128)(2,1)}), bf16[16,16,528]{2,1,0:T(8,128)(2,1)S(1)}, u32[]{:S(2)}, u32[]{:S(2)}) async-start(bf16[16,16,528]{2,1,0:T(8,128)(2,1)} %bitcast.18), calls=%async_computation.2 | async-start | bytes 655360 | tf_op jit(solution)/shard_map/all_to_all | solution.py:30
  79.3 4.0 %collective-permute-start.2 = (bf16[256,528]{1,0:T(8,128)(2,1)}, bf16[256,528]{1,0:T(8,128)(2,1)S(1)}, u32[]{:S(2)}, u32[]{:S(2)}) collective-permute-start(bf16[256,528]{1,0:T(8,128)(2,1)} %copy-done), channel_id=1, source_target_pairs={{0,32},{32,64},{64,96},{96,0},{1,33},{33,65},{65,97},{97,1},{2,34}... | collective-permute-start | bytes 811016 | tf_op jit(solution)/shard_map/ppermute | solution.py:35
  83.3 1.9 %collective-permute-start.3 = (bf16[256,528]{1,0:T(8,128)(2,1)S(1)}, bf16[256,528]{1,0:T(8,128)(2,1)S(1)}, u32[]{:S(2)}, u32[]{:S(2)}) collective-permute-start(bf16[256,528]{1,0:T(8,128)(2,1)S(1)} %get-tuple-element.30), channel_id=1, source_target_pairs={{0,64},{32,96},{64,0},{96,32},{1,65},{33,97},{65,1},{97,33},{2,66}... | collective-permute-start | bytes 811016 | tf_op jit(solution)/shard_map/ppermute | solution.py:35
  85.2 3.3 %collective-permute-start.4 = (bf16[256,528]{1,0:T(8,128)(2,1)S(1)}, bf16[256,528]{1,0:T(8,128)(2,1)S(1)}, u32[]{:S(2)}, u32[]{:S(2)}) collective-permute-start(bf16[256,528]{1,0:T(8,128)(2,1)S(1)} %get-tuple-element.31), channel_id=1, source_target_pairs={{0,96},{32,0},{64,32},{96,64},{1,97},{33,1},{65,33},{97,65},{2,98}... | collective-permute-start | bytes 811016 | tf_op jit(solution)/shard_map/ppermute | solution.py:35
  88.8 1.0 copy.62.sig_ref
  89.8 7.1 %collective-permute-done.2 = bf16[256,528]{1,0:T(8,128)(2,1)S(1)} collective-permute-done((bf16[256,528]{1,0:T(8,128)(2,1)}, bf16[256,528]{1,0:T(8,128)(2,1)S(1)}, u32[]{:S(2)}, u32[]{:S(2)}) %collective-permute-start.2) | collective-permute-done | bytes 270368 | tf_op jit(solution)/shard_map/ppermute | solution.py:35
  97.4 4.8 %collective-permute-done.4 = bf16[256,528]{1,0:T(8,128)(2,1)S(1)} collective-permute-done((bf16[256,528]{1,0:T(8,128)(2,1)S(1)}, bf16[256,528]{1,0:T(8,128)(2,1)S(1)}, u32[]{:S(2)}, u32[]{:S(2)}) %collective-permute-start.4) | collective-permute-done | bytes 270368 | tf_op jit(solution)/shard_map/ppermute | solution.py:35
  102.2 0.9 add_convert_fusion
  103.9 11.7 %all-to-all-start.3 = ((bf16[16,16,528]{2,1,0:T(8,128)(2,1)}), bf16[16,16,528]{2,1,0:T(8,128)(2,1)S(1)}, u32[]{:S(2)}, u32[]{:S(2)}) async-start(bf16[16,16,528]{2,1,0:T(8,128)(2,1)} %bitcast.26), calls=%async_computation.3 | async-start | bytes 655360 | tf_op jit(solution)/shard_map/all_to_all | solution.py:30
  116.3 15.5 %psum.7.sums_ref = f32[8,256]{1,0:T(8,128)} all-reduce(f32[8,256]{1,0:T(8,128)S(1)} %stack.43), channel_id=1, replica_groups=mesh['enc'=8,'x'=4,'z'=16,'rep'=2] {'enc'}, use_global_device_ids=true, to_apply=%region_9.10 | all-reduce | flops 2048 | bytes 16384 | tf_op jit(solution)/shard_map/psum | solution.py:182
  131.8 2.7 %norm.1 = (bf16[256,384]{1,0:T(8,128)(2,1)}, bf16[256,144]{1,0:T(8,128)(2,1)}) custom-call(f32[8,256]{1,0:T(8,128)} %psum.7.sums_ref, bf16[256,528]{1,0:T(8,128)(2,1)} %copy-done.1, f32[1,528]{1,0:T(1,128)} %broadcast_in_dim.28.gain_ref, bf16[256,384]{1,0:T(8,128)(2,1)} %cnx_ref.1, bf16[256,144]{1,0:T(8,128)(2,1)} %copy-done.2), custom_call_target="tpu_custom_call" | custom-call | flops 1 | bytes 1 | tf_op jit(solution)/shard_map/norm/pallas_call | solution.py:183
  134.5 1.6 %copy.64 = bf16[256,144]{0,1:T(8,128)(2,1)} copy(bf16[256,144]{1,0:T(8,128)(2,1)} %get-tuple-element.50) | data formatting | bytes 147456
  136.1 0.7 all-to-all-done.3
  (51 shorter events, 5.1 us)
Async XLA Ops:
  0.6 10.3 %copy-start.6 = (bf16[256,144]{0,1:T(8,128)(2,1)S(1)}, bf16[256,144]{0,1:T(8,128)(2,1)}, u32[]{:S(2)}) copy-start(bf16[256,144]{0,1:T(8,128)(2,1)} %param.12) | copy-start | bytes 221188
  1.7 9.3 %copy-start.5 = (bf16[256,384]{1,0:T(8,128)(2,1)S(1)}, bf16[256,384]{1,0:T(8,128)(2,1)}, u32[]{:S(2)}) copy-start(bf16[256,384]{1,0:T(8,128)(2,1)} %param.13) | copy-start | bytes 589828
  2.6 10.4 %copy-start.4 = (bf16[2048,144]{0,1:T(8,128)(2,1)S(1)}, bf16[2048,144]{0,1:T(8,128)(2,1)}, u32[]{:S(2)}) copy-start(bf16[2048,144]{0,1:T(8,128)(2,1)} %param.15) | copy-start | bytes 1769476
  3.8 35.8 %all-to-all-start = ((bf16[8,2,128,256]{3,2,1,0:T(8,128)(2,1)}), bf16[8,2,128,256]{3,2,1,0:T(8,128)(2,1)S(1)}, u32[]{:S(2)}, u32[]{:S(2)}) async-start(bf16[8,2,128,256]{3,2,1,0:T(8,128)(2,1)} %broadcast_in_dim.27), calls=%async_computation | async-start | bytes 2097152 | tf_op jit(solution)/shard_map/all_to_all | solution.py:26
  11.1 19.3 %collective-permute-start = (bf16[256,528]{1,0:T(8,128)(2,1)S(1)}, bf16[256,528]{1,0:T(8,128)(2,1)S(1)}, u32[]{:S(2)}, u32[]{:S(2)}) collective-permute-start(bf16[256,528]{1,0:T(8,128)(2,1)S(1)} %pad_maximum_fusion.2.own_ref), channel_id=1, source_target_pairs={{0,1},{1,0},{2,3},{3,2},{4,5},{5,4},{6,7},{7,6},{8,9},{9,8},{10,11... | collective-permute-start | bytes 811016 | tf_op jit(solution)/shard_map/ppermute | solution.py:110
  15.2 0.7 copy-start.9
  39.7 17.1 %collective-permute-start.1 = (bf16[8,128,256]{2,1,0:T(8,128)(2,1)S(1)}, bf16[8,128,256]{2,1,0:T(8,128)(2,1)S(1)}, u32[]{:S(2)}, u32[]{:S(2)}) collective-permute-start(bf16[8,128,256]{2,1,0:T(8,128)(2,1)S(1)} %slice_bitcast_fusion), channel_id=1, source_target_pairs={{0,1},{1,0},{2,3},{3,2},{4,5},{5,4},{6,7},{7,6},{8,9},{9,8},{10,11... | collective-permute-start | bytes 1572872 | tf_op jit(solution)/shard_map/ppermute | solution.py:123
  45.0 10.7 %all-to-all-start.1 = ((bf16[4,64,528]{2,1,0:T(8,128)(2,1)}), bf16[4,64,528]{2,1,0:T(8,128)(2,1)S(1)}, u32[]{:S(2)}, u32[]{:S(2)}) async-start(bf16[4,64,528]{2,1,0:T(8,128)(2,1)} %bitcast.14), calls=%async_computation.1 | async-start | bytes 655360 | tf_op jit(solution)/shard_map/all_to_all | solution.py:30
  49.8 38.7 %copy-start.10 = (s32[1,64]{1,0:T(1,128)S(1)}, s32[1,64]{1,0:T(1,128)}, u32[]{:S(2)}) copy-start(s32[1,64]{1,0:T(1,128)} %param.19) | copy-start | bytes 772
  57.8 0.7 copy-start
  58.5 44.8 %copy-start.8 = (f32[144]{0:T(256)S(1)}, f32[144]{0:T(256)}, u32[]{:S(2)}) copy-start(f32[144]{0:T(256)} %param.22) | copy-start | bytes 1732
  58.5 45.1 %copy-start.3 = (bf16[256,384]{1,0:T(8,128)(2,1)S(1)}, bf16[256,384]{1,0:T(8,128)(2,1)}, u32[]{:S(2)}) copy-start(bf16[256,384]{1,0:T(8,128)(2,1)} %cnx_ref.1) | copy-start | bytes 589828
  58.5 45.1 %copy-start.7 = (f32[384]{0:T(512)S(1)}, f32[384]{0:T(512)}, u32[]{:S(2)}) copy-start(f32[384]{0:T(512)} %param.23) | copy-start | bytes 4612
  60.4 42.6 %all-to-all-start.2 = ((bf16[16,16,528]{2,1,0:T(8,128)(2,1)}), bf16[16,16,528]{2,1,0:T(8,128)(2,1)S(1)}, u32[]{:S(2)}, u32[]{:S(2)}) async-start(bf16[16,16,528]{2,1,0:T(8,128)(2,1)} %bitcast.18), calls=%async_computation.2 | async-start | bytes 655360 | tf_op jit(solution)/shard_map/all_to_all | solution.py:30
  79.3 17.6 %collective-permute-start.2 = (bf16[256,528]{1,0:T(8,128)(2,1)}, bf16[256,528]{1,0:T(8,128)(2,1)S(1)}, u32[]{:S(2)}, u32[]{:S(2)}) collective-permute-start(bf16[256,528]{1,0:T(8,128)(2,1)} %copy-done), channel_id=1, source_target_pairs={{0,32},{32,64},{64,96},{96,0},{1,33},{33,65},{65,97},{97,1},{2,34}... | collective-permute-start | bytes 811016 | tf_op jit(solution)/shard_map/ppermute | solution.py:35
  83.3 14.1 %collective-permute-start.3 = (bf16[256,528]{1,0:T(8,128)(2,1)S(1)}, bf16[256,528]{1,0:T(8,128)(2,1)S(1)}, u32[]{:S(2)}, u32[]{:S(2)}) collective-permute-start(bf16[256,528]{1,0:T(8,128)(2,1)S(1)} %get-tuple-element.30), channel_id=1, source_target_pairs={{0,64},{32,96},{64,0},{96,32},{1,65},{33,97},{65,1},{97,33},{2,66}... | collective-permute-start | bytes 811016 | tf_op jit(solution)/shard_map/ppermute | solution.py:35
  85.2 17.0 %collective-permute-start.4 = (bf16[256,528]{1,0:T(8,128)(2,1)S(1)}, bf16[256,528]{1,0:T(8,128)(2,1)S(1)}, u32[]{:S(2)}, u32[]{:S(2)}) collective-permute-start(bf16[256,528]{1,0:T(8,128)(2,1)S(1)} %get-tuple-element.31), channel_id=1, source_target_pairs={{0,96},{32,0},{64,32},{96,64},{1,97},{33,1},{65,33},{97,65},{2,98}... | collective-permute-start | bytes 811016 | tf_op jit(solution)/shard_map/ppermute | solution.py:35
  89.8 42.0 %copy-start.2 = (bf16[256,144]{1,0:T(8,128)(2,1)}, bf16[256,144]{1,0:T(8,128)(2,1)S(1)}, u32[]{:S(2)}) copy-start(bf16[256,144]{1,0:T(8,128)(2,1)S(1)} %copy.62.sig_ref) | copy-start | bytes 221188
  103.4 28.4 %copy-start.1 = (bf16[256,528]{1,0:T(8,128)(2,1)}, bf16[256,528]{1,0:T(8,128)(2,1)S(1)}, u32[]{:S(2)}) copy-start(bf16[256,528]{1,0:T(8,128)(2,1)S(1)} %convolution_convert_fusion.dy_ref) | copy-start | bytes 811012
  103.9 32.9 %all-to-all-start.3 = ((bf16[16,16,528]{2,1,0:T(8,128)(2,1)}), bf16[16,16,528]{2,1,0:T(8,128)(2,1)S(1)}, u32[]{:S(2)}, u32[]{:S(2)}) async-start(bf16[16,16,528]{2,1,0:T(8,128)(2,1)} %bitcast.26), calls=%async_computation.3 | async-start | bytes 655360 | tf_op jit(solution)/shard_map/all_to_all | solution.py:30

commit v5 on v4

--- a/solution.py
+++ b/solution.py
@@ -20,12 +20,6 @@
     return [(i, (i + step) % count) for i in range(count)]
 
 
-def broadcast_gather(block, axis):
-    count = lax.axis_size(axis)
-    copies = jnp.broadcast_to(block[None], (count,) + block.shape)
-    return lax.all_to_all(copies, axis, 0, 0, tiled=True)
-
-
 def exchange(blocks, axis):
     return lax.all_to_all(blocks, axis, 0, 0, tiled=True)
 
@@ -37,6 +31,29 @@
 
 def pick(chosen, source):
     return jnp.dot(chosen.astype(BF16), source, preferred_element_type=F32).astype(BF16)
+
+
+def turn_kernel(pieces, core_ref, lengths_ref, cotangent_ref, out_ref, turned_ref):
+    rows = cotangent_ref.shape[0]
+    slots = lengths_ref.shape[1]
+    depth = rows // slots
+    lane = lax.broadcasted_iota(jnp.int32, (slots, rows), 1)
+    slot = lax.broadcasted_iota(jnp.int32, (slots, rows), 0)
+    spread = (lane >= slot * depth) & (lane < slot * depth + depth)
+    first = jnp.broadcast_to(lengths_ref[...].astype(F32), (8, slots))
+    limit = jnp.dot(first, spread.astype(F32), preferred_element_type=F32)[:1]
+    token = lax.rem(lax.broadcasted_iota(jnp.int32, (1, rows), 1), depth).astype(F32)
+    turned = cotangent_ref[...].astype(F32).T
+    turned_ref[...] = jnp.where(token < limit, turned, 0.0).astype(BF16)
+    halves = out_ref.shape[1]
+    piece = out_ref.shape[2] // pieces
+    for half in range(halves):
+        source = lax.rem(core_ref[0] + half, halves)
+        for k in range(pieces):
+            start = pl.multiple_of((k * halves + source) * piece, piece)
+            block = turned_ref[pl.ds(start, piece), :]
+            for copy in range(out_ref.shape[0]):
+                out_ref[copy, half, pl.ds(k * piece, piece), :] = block
 
 
 def partial_kernel(here_ref, gathered_ref, own_ref, paired_ref, other_ref, *outs):
@@ -61,10 +78,13 @@
         mean, grad_mean = means[:, 0:1], means[:, 2:3]
         inverse = lax.rsqrt(means[:, 1:2] - mean * mean + EPS)
         product = inverse * inverse * (means[:, 3:4] - mean * grad_mean)
-        at = slice(start, start + pre.shape[1])
+        at = slice(start, start + pre.shape[1 - index])
         scaled = dy_ref[:, at].astype(F32) * gain_ref[:, at]
         height = pre[...].astype(F32)
-        out[...] = (inverse * (scaled - grad_mean - (height - mean) * product)).astype(BF16)
+        if index:
+            height = height.T
+        grad = inverse * (scaled - grad_mean - (height - mean) * product)
+        out[...] = (grad.T if index else grad).astype(BF16)
         start += pre.shape[1]
 
 
@@ -93,19 +113,18 @@
     swap = shift(rep_count, 1)
 
     token = lax.broadcasted_iota(jnp.int32, (slots, depth), 1)
-    live = (token < lengths[0][:, None]).reshape(1, rows)
-    turned = jnp.where(live, cotangent.T, jnp.zeros((), BF16))
     chips = slots // enc_count
     piece = cols // chips // rep_count
     half = cols // rep_count
-    turned = turned.reshape(chips, rep_count, piece, rows)
-    turned = jnp.stack(
-        [
-            lax.dynamic_index_in_dim(turned, index, 1, keepdims=False).reshape(half, rows)
-            for index in (core, 1 - core)
-        ]
-    )
-    gathered = broadcast_gather(turned, "enc").reshape(enc_count, rep_count, half, rows)
+    copies = pl.pallas_call(
+        functools.partial(turn_kernel, chips),
+        out_shape=jax.ShapeDtypeStruct((enc_count, rep_count, half, rows), BF16),
+        in_specs=[SMEM, VMEM, VMEM],
+        out_specs=VMEM,
+        scratch_shapes=[pltpu.VMEM((cols, rows), BF16)],
+        name="turn",
+    )(core.reshape(1), lengths, cotangent)
+    gathered = exchange(copies, "enc")
     features = jnp.concatenate([feat_cnx, feat_sig], axis=1)
     other_features = lax.ppermute(features, "rep", swap)
     weight = jnp.concatenate([w_cnx, w_sig], axis=1)
@@ -141,7 +160,6 @@
 
     row = lax.broadcasted_iota(jnp.int32, (rows, rows), 0)
     column = lax.broadcasted_iota(jnp.int32, (rows, rows), 1)
-    line = lax.broadcasted_iota(jnp.int32, (rows, 1), 0)
     back = lax.dot_general(
         gathered.reshape(enc_count * cols, rows),
         weight,
@@ -149,15 +167,9 @@
         preferred_element_type=F32,
     ).astype(BF16)
     goal = ((enc_of[0] * depth)[:, None] + token).reshape(1, rows)
-    held = pick(row == goal, back)
-    held = exchange(held.reshape(nx, rows // nx, width), "x").reshape(rows, width)
-    unit = line // depth
-    unit = unit % nx * nz + unit // nx
-    held = pick(column == unit * depth + line % depth, held)
-    held, parts = lax.optimization_barrier((held, parts))
-    held = exchange(held.reshape(nz, rows // nz, width), "z").reshape(rows, width)
-    sender = owner_of[0]
-    place = (((sender % nz * nx + sender // nz) * depth)[:, None] + token).reshape(rows, 1)
+    held = pick(row == goal, back).reshape(slots, depth, width)
+    held = exchange(held, ("x", "z")).reshape(rows, width)
+    place = ((owner_of[0] * depth)[:, None] + token).reshape(rows, 1)
     routed = pick(column == place, held)
 
     parts = hand_on(parts, "x")
@@ -186,16 +198,17 @@
         ),
         out_shape=[
             jax.ShapeDtypeStruct(pre_cnx.shape, BF16),
-            jax.ShapeDtypeStruct(pre_sig.shape, BF16),
+            jax.ShapeDtypeStruct(pre_sig.shape[::-1], BF16),
         ],
         in_specs=[VMEM] * 5,
         out_specs=[VMEM] * 2,
         cost_estimate=pl.CostEstimate(flops=1, bytes_accessed=1, transcendentals=0),
         name="norm",
-    )(sums, routed, jnp.concatenate([gain_cnx, gain_sig])[None, :], pre_cnx, pre_sig)
-    total = jnp.sum(total.astype(F32), axis=0) * (1.0 / math.sqrt(rows * nx * nz * rep_count))
-    grad_cnx, grad_sig = total[:, :split], total[:, split:]
-    return (grad_sig, grad_cnx, before_sig, before_cnx)
+    )(sums, routed, jnp.concatenate([gain_cnx, gain_sig])[None, :], pre_cnx, pre_sig.T)
+    scale = 1.0 / math.sqrt(rows * nx * nz * rep_count)
+    grad_cnx = jnp.sum(total[:, :, :split].astype(F32), axis=0) * scale
+    grad_sig = jnp.sum(total[:, :, split:].astype(F32), axis=0) * scale
+    return (grad_sig, grad_cnx, before_sig.T, before_cnx)
 
 
 def solution(mesh):

time: 139 us -> 131 us (0.942)
  local copies, waits for them, and re-layouts: 24.1 us -> 17.6 us
  Pallas kernels: 3.73 us -> 6.58 us
  starting transfers between devices: 55.5 us -> 53 us
  waiting for transfers between devices: 28.3 us -> 26.2 us
    all_to_all x1 -> x0, waiting for transfers between devices: 9.29 us -> none  [broadcast_gather(): return lax.all_to_all(copies, axis, 0, 0, tiled=True)]
    all_to_all x1 -> x0, starting transfers between devices: 7.1 us -> none  [broadcast_gather(): return lax.all_to_all(copies, axis, 0, 0, tiled=True)]
    all_to_all x3, starting transfers between devices: 35.4 us -> 40.5 us  [exchange(): return lax.all_to_all(blocks, axis, 0, 0, tiled=True)]
    all_to_all x3, waiting for transfers between devices: 6.63 us -> 11.5 us  [exchange(): return lax.all_to_all(blocks, axis, 0, 0, tiled=True)]
    unnamed x27 -> x21, local copies, waits for them, and re-layouts: 5.4 us -> 2.01 us
    ppermute x3, waiting for transfers between devices: 12.4 us -> 14.7 us  [hand_on(): lax.ppermute(blocks[k], axis, shift(count, k))]
    pallas_call x0 -> x1, Pallas kernels: none -> 2.27 us  [shards(): pl.pallas_call(functools.partial(turn_kernel, chips), out_shape=jax.Shape...]
    reshape x0 -> x2, local copies, waits for them, and re-layouts: none -> 1.95 us  [the longest x1 1.12 us: shards(): held = exchange(held, ('x', 'z')).reshape(rows, width)]
  transfers between devices with their start and end apart: 9 -> 8, of which waited for: 6 -> 5; matrix products, arithmetic and copies ran while one was open for 19% -> 18% of each run, Pallas kernels for 2% -> 3%
where the time goes in v5:
time: 131 us; the launch traced here: 129 us
  starting transfers between devices  53 us (40%)
  waiting for transfers between devices  26.2 us (20%)
  local copies, waits for them, and re-layouts  17.6 us (13%)
  blocking collectives  15.5 us (12%)
  Pallas kernels  6.58 us (5%)
  other arithmetic  6.42 us (5%)
  matrix products  2.84 us (2%)
    all_to_all x3, starting transfers between devices, exchange(): return lax.all_to_all(blocks, axis, 0, 0, tiled=True)  40.5 us
    psum x1, blocking collectives, shards(): sums = lax.psum(sums, 'enc')  15.5 us
    ppermute x3, waiting for transfers between devices, hand_on(): lax.ppermute(blocks[k], axis, shift(count, k))  14.7 us
    all_to_all x3, waiting for transfers between devices, exchange(): return lax.all_to_all(blocks, axis, 0, 0, tiled=True)  11.5 us
    ppermute x3, starting transfers between devices, hand_on(): lax.ppermute(blocks[k], axis, shift(count, k))  8.67 us
    another operation x1, local copies, waits for them, and re-layouts, shards(): jnp.stack([lax.dynamic_index_in_dim(weight, index, 2, keepdims=False).res...  6.49 us
    reshape x1, local copies, waits for them, and re-layouts, shards(): weight = jnp.stack([lax.dynamic_index_in_dim(weight, index, 2, keepdims=F...  5.87 us
    dot_general x2, matrix products, pick(): jnp.dot(chosen.astype(BF16), source, preferred_element_type=F32)  2.84 us
  transfers between devices with their start and end apart: 8, of which 5 were waited for; matrix products, arithmetic and copies ran while one was open for 18% of the time, Pallas kernels for 3%

profile of v5, /device:TPU:6, one launch (start us, length us, event | category | flops | bytes accessed | tf_op | source)
XLA Modules:
  0.0 129.2 jit_solution(459068033547474184)
XLA Ops:
  0.7 2.3 %turn.1 = bf16[8,2,128,256]{3,2,1,0:T(8,128)(2,1)} custom-call(s32[1]{0:T(128)} %bitcast.4.core_ref, s32[1,64]{1,0:T(1,128)} %lengths_ref.1, bf16[256,256]{1,0:T(8,128)(2,1)} %cotangent_ref.1), custom_call_target="tpu_custom_call" | custom-call | tf_op jit(solution)/shard_map/turn/pallas_call | solution.py:119
  2.9 7.1 %all-to-all-start = ((bf16[8,2,128,256]{3,2,1,0:T(8,128)(2,1)}), bf16[8,2,128,256]{3,2,1,0:T(8,128)(2,1)S(1)}, u32[]{:S(2)}, u32[]{:S(2)}) async-start(bf16[8,2,128,256]{3,2,1,0:T(8,128)(2,1)} %turn.1), calls=%async_computation | async-start | bytes 2097152 | tf_op jit(solution)/shard_map/all_to_all | solution.py:24
  10.2 1.9 %collective-permute-start = (bf16[256,528]{1,0:T(8,128)(2,1)S(1)}, bf16[256,528]{1,0:T(8,128)(2,1)S(1)}, u32[]{:S(2)}, u32[]{:S(2)}) collective-permute-start(bf16[256,528]{1,0:T(8,128)(2,1)S(1)} %pad_maximum_fusion.2.own_ref), channel_id=1, source_target_pairs={{0,1},{1,0},{2,3},{3,2},{4,5},{5,4},{6,7},{7,6},{8,9},{9,8},{10,11... | collective-permute-start | bytes 811016 | tf_op jit(solution)/shard_map/ppermute | solution.py:129
  12.1 0.5 copy.44
  12.6 1.7 %pad_maximum_fusion = bf16[2048,528]{1,0:T(8,128)(2,1)S(1)} fusion(bf16[2048,144]{1,0:T(8,128)(2,1)S(1)} %copy.44, bf16[2048,384]{1,0:T(8,128)(2,1)} %param.16), kind=kLoop, calls=%fused_computation | loop fusion | flops 4325376 | bytes 4325376 | tf_op jit(solution)/shard_map/concatenate | solution.py:130
  14.6 0.4 copy-done.7
  15.0 1.9 %pad_maximum_fusion.1 = bf16[8,2,128,528]{3,2,0,1:T(8,128)(2,1)} fusion(bf16[8,1,128,528]{3,2,0,1:T(8,128)(2,1)S(1)} %bitcast.35, bf16[8,1,128,528]{3,2,0,1:T(8,128)(2,1)S(1)} %bitcast.34), kind=kLoop, calls=%fused_computation.1 | loop fusion | flops 1081344 | bytes 4325376 | tf_op jit(solution)/shard_map/stack | solution.py:133
  16.9 6.5 %copy.47 = bf16[8,2,128,528]{2,1,0,3:T(2,128)(2,1)} copy(bf16[8,2,128,528]{3,2,0,1:T(8,128)(2,1)} %pad_maximum_fusion.1) | data formatting | bytes 4325376 | tf_op jit(solution)/shard_map/stack | solution.py:133
  23.4 5.9 %reshape.82 = bf16[2048,528]{0,1:T(8,128)(2,1)} reshape(bf16[8,2,128,528]{2,1,0,3:T(2,128)(2,1)} %copy.47) | data formatting | bytes 4325376 | tf_op jit(solution)/shard_map/reshape | solution.py:139
  29.5 9.3 %all-to-all-done.gathered_ref = bf16[8,2,128,256]{3,2,1,0:T(8,128)(2,1)S(1)} async-done(((bf16[8,2,128,256]{3,2,1,0:T(8,128)(2,1)}), bf16[8,2,128,256]{3,2,1,0:T(8,128)(2,1)S(1)}, u32[]{:S(2)}, u32[]{:S(2)}) %all-to-all-start) | async-done | bytes 1048608 | tf_op jit(solution)/shard_map/all_to_all | solution.py:24
  38.8 1.9 %collective-permute-start.1 = (bf16[8,128,256]{2,1,0:T(8,128)(2,1)S(1)}, bf16[8,128,256]{2,1,0:T(8,128)(2,1)S(1)}, u32[]{:S(2)}, u32[]{:S(2)}) collective-permute-start(bf16[8,128,256]{2,1,0:T(8,128)(2,1)S(1)} %slice_bitcast_fusion), channel_id=1, source_target_pairs={{0,1},{1,0},{2,3},{3,2},{4,5},{5,4},{6,7},{7,6},{8,9},{9,8},{10,11... | collective-permute-start | bytes 1572872 | tf_op jit(solution)/shard_map/ppermute | solution.py:142
  40.7 2.5 %convolution_convert_fusion.2 = bf16[256,528]{0,1:T(8,128)(2,1)S(1)} fusion(bf16[2048,528]{0,1:T(8,128)(2,1)} %reshape.82, bf16[2048,256]{1,0:T(8,128)(2,1)S(1)} %bitcast.32, s32[256]{0:T(256)S(1)} %add.54), kind=kOutput, calls=%fused_computation.4 | convolution fusion | flops 623190016 | bytes 3482624 | tf_op jit(solution)/shard_map/dot_general | solution.py:33
  43.5 0.8 reshape.84
  44.3 22.6 %all-to-all-start.1 = ((bf16[64,4,528]{2,1,0:T(4,128)(2,1)}), bf16[64,4,528]{2,1,0:T(4,128)(2,1)}, u32[]{:S(2)}, u32[]{:S(2)}) async-start(bf16[64,4,528]{2,1,0:T(4,128)(2,1)} %reshape.84), calls=%async_computation.1 | async-start | bytes 655360 | tf_op jit(solution)/shard_map/all_to_all | solution.py:24
  67.0 1.5 %partial.1 = (f32[256,528]{1,0:T(8,128)S(1)}, bf16[256,528]{1,0:T(8,128)(2,1)}, bf16[256,528]{1,0:T(8,128)(2,1)S(1)}, bf16[256,528]{1,0:T(8,128)(2,1)S(1)}) custom-call(s32[1]{0:T(128)} %bitcast.15.here_ref, bf16[8,2,128,256]{3,2,1,0:T(8,128)(2,1)S(1)} %all-to-all-done.gathered_ref, bf16[256,528]{1,0:T(8,128)(2,1)S(1)} %pad_maximum_fusion.2.own_ref, ...), custom_call_target="tpu_custom_call" | custom-call | flops 553648128 | bytes 2162688 | tf_op jit(solution)/shard_map/partial/pallas_call | solution.py:145
  68.5 2.3 %collective-permute-start.2 = (bf16[256,528]{1,0:T(8,128)(2,1)}, bf16[256,528]{1,0:T(8,128)(2,1)S(1)}, u32[]{:S(2)}, u32[]{:S(2)}) collective-permute-start(bf16[256,528]{1,0:T(8,128)(2,1)} %get-tuple-element.19), channel_id=1, source_target_pairs={{0,32},{32,64},{64,96},{96,0},{1,33},{33,65},{65,97},{97,1},{2,34}... | collective-permute-start | bytes 811016 | tf_op jit(solution)/shard_map/ppermute | solution.py:29
  70.8 4.4 %collective-permute-start.3 = (bf16[256,528]{1,0:T(8,128)(2,1)S(1)}, bf16[256,528]{1,0:T(8,128)(2,1)S(1)}, u32[]{:S(2)}, u32[]{:S(2)}) collective-permute-start(bf16[256,528]{1,0:T(8,128)(2,1)S(1)} %get-tuple-element.20), channel_id=1, source_target_pairs={{0,64},{32,96},{64,0},{96,32},{1,65},{33,97},{65,1},{97,33},{2,66}... | collective-permute-start | bytes 811016 | tf_op jit(solution)/shard_map/ppermute | solution.py:29
  75.3 1.9 %collective-permute-start.4 = (bf16[256,528]{1,0:T(8,128)(2,1)S(1)}, bf16[256,528]{1,0:T(8,128)(2,1)S(1)}, u32[]{:S(2)}, u32[]{:S(2)}) collective-permute-start(bf16[256,528]{1,0:T(8,128)(2,1)S(1)} %get-tuple-element.21), channel_id=1, source_target_pairs={{0,96},{32,0},{64,32},{96,64},{1,97},{33,1},{65,33},{97,65},{2,98}... | collective-permute-start | bytes 811016 | tf_op jit(solution)/shard_map/ppermute | solution.py:29
  77.4 1.0 copy.50
  78.4 5.6 %collective-permute-done.2 = bf16[256,528]{1,0:T(8,128)(2,1)S(1)} collective-permute-done((bf16[256,528]{1,0:T(8,128)(2,1)}, bf16[256,528]{1,0:T(8,128)(2,1)S(1)}, u32[]{:S(2)}, u32[]{:S(2)}) %collective-permute-start.2) | collective-permute-done | bytes 270368 | tf_op jit(solution)/shard_map/ppermute | solution.py:29
  84.0 2.7 %collective-permute-done.3 = bf16[256,528]{1,0:T(8,128)(2,1)S(1)} collective-permute-done((bf16[256,528]{1,0:T(8,128)(2,1)S(1)}, bf16[256,528]{1,0:T(8,128)(2,1)S(1)}, u32[]{:S(2)}, u32[]{:S(2)}) %collective-permute-start.3) | collective-permute-done | bytes 270368 | tf_op jit(solution)/shard_map/ppermute | solution.py:29
  86.7 6.4 %collective-permute-done.4 = bf16[256,528]{1,0:T(8,128)(2,1)S(1)} collective-permute-done((bf16[256,528]{1,0:T(8,128)(2,1)S(1)}, bf16[256,528]{1,0:T(8,128)(2,1)S(1)}, u32[]{:S(2)}, u32[]{:S(2)}) %collective-permute-start.4) | collective-permute-done | bytes 270368 | tf_op jit(solution)/shard_map/ppermute | solution.py:29
  93.1 0.9 add_convert_fusion
  93.9 1.1 reshape.85
  95.1 0.3 convolution_convert_fusion.dy_ref
  95.9 10.8 %all-to-all-start.2 = ((bf16[16,16,528]{2,1,0:T(8,128)(2,1)}), bf16[16,16,528]{2,1,0:T(8,128)(2,1)S(1)}, u32[]{:S(2)}, u32[]{:S(2)}) async-start(bf16[16,16,528]{2,1,0:T(8,128)(2,1)} %bitcast.17), calls=%async_computation.2 | async-start | bytes 655360 | tf_op jit(solution)/shard_map/all_to_all | solution.py:24
  106.7 0.6 broadcast_in_dim.2.gain_ref
  107.3 15.5 %psum.7.sums_ref = f32[8,256]{1,0:T(8,128)} all-reduce(f32[8,256]{1,0:T(8,128)S(1)} %stack.39), channel_id=1, replica_groups=mesh['enc'=8,'x'=4,'z'=16,'rep'=2] {'enc'}, use_global_device_ids=true, to_apply=%region_10.11 | all-reduce | flops 2048 | bytes 16384 | tf_op jit(solution)/shard_map/psum | solution.py:194
  122.8 2.8 %norm.1 = (bf16[256,384]{1,0:T(8,128)(2,1)}, bf16[144,256]{1,0:T(8,128)(2,1)}) custom-call(f32[8,256]{1,0:T(8,128)} %psum.7.sums_ref, bf16[256,528]{1,0:T(8,128)(2,1)} %copy-done, f32[1,528]{1,0:T(1,128)} %broadcast_in_dim.2.gain_ref, bf16[256,384]{1,0:T(8,128)(2,1)} %cnx_ref.1, bf16[144,256]{1,0:T(8,128)(2,1)} %bitcast.36), custom_call_target="tpu_custom_call" | custom-call | flops 1 | bytes 1 | tf_op jit(solution)/shard_map/norm/pallas_call | solution.py:195
  125.6 2.2 %all-to-all-done.2 = bf16[16,16,528]{2,1,0:T(8,128)(2,1)S(1)} async-done(((bf16[16,16,528]{2,1,0:T(8,128)(2,1)}), bf16[16,16,528]{2,1,0:T(8,128)(2,1)S(1)}, u32[]{:S(2)}, u32[]{:S(2)}) %all-to-all-start.2) | async-done | bytes 270368 | tf_op jit(solution)/shard_map/all_to_all | solution.py:24
  127.9 0.6 broadcast_multiply_fusion
  128.6 0.6 broadcast_multiply_fusion.1
  (37 shorter events, 1.6 us)
Async XLA Ops:
  0.6 9.4 %copy-start.4 = (bf16[256,144]{0,1:T(8,128)(2,1)S(1)}, bf16[256,144]{0,1:T(8,128)(2,1)}, u32[]{:S(2)}) copy-start(bf16[256,144]{0,1:T(8,128)(2,1)} %param.12) | copy-start | bytes 221188
  0.6 9.5 %copy-start.3 = (bf16[256,384]{1,0:T(8,128)(2,1)S(1)}, bf16[256,384]{1,0:T(8,128)(2,1)}, u32[]{:S(2)}) copy-start(bf16[256,384]{1,0:T(8,128)(2,1)} %param.13) | copy-start | bytes 589828
  0.7 11.5 %copy-start.2 = (bf16[2048,144]{0,1:T(8,128)(2,1)S(1)}, bf16[2048,144]{0,1:T(8,128)(2,1)}, u32[]{:S(2)}) copy-start(bf16[2048,144]{0,1:T(8,128)(2,1)} %param.15) | copy-start | bytes 1769476
  2.9 35.8 %all-to-all-start = ((bf16[8,2,128,256]{3,2,1,0:T(8,128)(2,1)}), bf16[8,2,128,256]{3,2,1,0:T(8,128)(2,1)S(1)}, u32[]{:S(2)}, u32[]{:S(2)}) async-start(bf16[8,2,128,256]{3,2,1,0:T(8,128)(2,1)} %turn.1), calls=%async_computation | async-start | bytes 2097152 | tf_op jit(solution)/shard_map/all_to_all | solution.py:24
  10.2 19.3 %collective-permute-start = (bf16[256,528]{1,0:T(8,128)(2,1)S(1)}, bf16[256,528]{1,0:T(8,128)(2,1)S(1)}, u32[]{:S(2)}, u32[]{:S(2)}) collective-permute-start(bf16[256,528]{1,0:T(8,128)(2,1)S(1)} %pad_maximum_fusion.2.own_ref), channel_id=1, source_target_pairs={{0,1},{1,0},{2,3},{3,2},{4,5},{5,4},{6,7},{7,6},{8,9},{9,8},{10,11... | collective-permute-start | bytes 811016 | tf_op jit(solution)/shard_map/ppermute | solution.py:129
  14.3 0.7 copy-start.7
  38.8 28.1 %collective-permute-start.1 = (bf16[8,128,256]{2,1,0:T(8,128)(2,1)S(1)}, bf16[8,128,256]{2,1,0:T(8,128)(2,1)S(1)}, u32[]{:S(2)}, u32[]{:S(2)}) collective-permute-start(bf16[8,128,256]{2,1,0:T(8,128)(2,1)S(1)} %slice_bitcast_fusion), channel_id=1, source_target_pairs={{0,1},{1,0},{2,3},{3,2},{4,5},{5,4},{6,7},{7,6},{8,9},{9,8},{10,11... | collective-permute-start | bytes 1572872 | tf_op jit(solution)/shard_map/ppermute | solution.py:142
  43.3 33.9 %copy-start.8 = (s32[1,64]{1,0:T(1,128)S(1)}, s32[1,64]{1,0:T(1,128)}, u32[]{:S(2)}) copy-start(s32[1,64]{1,0:T(1,128)} %param.19) | copy-start | bytes 772
  44.3 49.6 %all-to-all-start.1 = ((bf16[64,4,528]{2,1,0:T(4,128)(2,1)}), bf16[64,4,528]{2,1,0:T(4,128)(2,1)}, u32[]{:S(2)}, u32[]{:S(2)}) async-start(bf16[64,4,528]{2,1,0:T(4,128)(2,1)} %reshape.84), calls=%async_computation.1 | async-start | bytes 655360 | tf_op jit(solution)/shard_map/all_to_all | solution.py:24
  68.5 26.9 %copy-start.6 = (f32[144]{0:T(256)S(1)}, f32[144]{0:T(256)}, u32[]{:S(2)}) copy-start(f32[144]{0:T(256)} %param.22) | copy-start | bytes 1732
  68.5 27.2 %copy-start.1 = (bf16[256,384]{1,0:T(8,128)(2,1)S(1)}, bf16[256,384]{1,0:T(8,128)(2,1)}, u32[]{:S(2)}) copy-start(bf16[256,384]{1,0:T(8,128)(2,1)} %cnx_ref.1) | copy-start | bytes 589828
  68.5 27.2 %copy-start.5 = (f32[384]{0:T(512)S(1)}, f32[384]{0:T(512)}, u32[]{:S(2)}) copy-start(f32[384]{0:T(512)} %param.23) | copy-start | bytes 4612
  68.5 15.5 %collective-permute-start.2 = (bf16[256,528]{1,0:T(8,128)(2,1)}, bf16[256,528]{1,0:T(8,128)(2,1)S(1)}, u32[]{:S(2)}, u32[]{:S(2)}) collective-permute-start(bf16[256,528]{1,0:T(8,128)(2,1)} %get-tuple-element.19), channel_id=1, source_target_pairs={{0,32},{32,64},{64,96},{96,0},{1,33},{33,65},{65,97},{97,1},{2,34}... | collective-permute-start | bytes 811016 | tf_op jit(solution)/shard_map/ppermute | solution.py:29
  70.8 15.9 %collective-permute-start.3 = (bf16[256,528]{1,0:T(8,128)(2,1)S(1)}, bf16[256,528]{1,0:T(8,128)(2,1)S(1)}, u32[]{:S(2)}, u32[]{:S(2)}) collective-permute-start(bf16[256,528]{1,0:T(8,128)(2,1)S(1)} %get-tuple-element.20), channel_id=1, source_target_pairs={{0,64},{32,96},{64,0},{96,32},{1,65},{33,97},{65,1},{97,33},{2,66}... | collective-permute-start | bytes 811016 | tf_op jit(solution)/shard_map/ppermute | solution.py:29
  75.3 17.8 %collective-permute-start.4 = (bf16[256,528]{1,0:T(8,128)(2,1)S(1)}, bf16[256,528]{1,0:T(8,128)(2,1)S(1)}, u32[]{:S(2)}, u32[]{:S(2)}) collective-permute-start(bf16[256,528]{1,0:T(8,128)(2,1)S(1)} %get-tuple-element.21), channel_id=1, source_target_pairs={{0,96},{32,0},{64,32},{96,64},{1,97},{33,1},{65,33},{97,65},{2,98}... | collective-permute-start | bytes 811016 | tf_op jit(solution)/shard_map/ppermute | solution.py:29
  95.4 27.4 %copy-start = (bf16[256,528]{1,0:T(8,128)(2,1)}, bf16[256,528]{1,0:T(8,128)(2,1)S(1)}, u32[]{:S(2)}) copy-start(bf16[256,528]{1,0:T(8,128)(2,1)S(1)} %convolution_convert_fusion.dy_ref) | copy-start | bytes 811012
  95.9 31.9 %all-to-all-start.2 = ((bf16[16,16,528]{2,1,0:T(8,128)(2,1)}), bf16[16,16,528]{2,1,0:T(8,128)(2,1)S(1)}, u32[]{:S(2)}, u32[]{:S(2)}) async-start(bf16[16,16,528]{2,1,0:T(8,128)(2,1)} %bitcast.17), calls=%async_computation.2 | async-start | bytes 655360 | tf_op jit(solution)/shard_map/all_to_all | solution.py:24

commit v6 on v5

--- a/solution.py
+++ b/solution.py
@@ -26,7 +26,9 @@
 
 def hand_on(blocks, axis):
     count = lax.axis_size(axis)
-    return [blocks[0]] + [lax.ppermute(blocks[k], axis, shift(count, k)) for k in range(1, count)]
+    order = sorted(range(1, count), key=lambda k: -min(k, count - k))
+    got = {k: lax.ppermute(blocks[k], axis, shift(count, k)) for k in order}
+    return [blocks[0]] + [got[k] for k in range(1, count)]
 
 
 def pick(chosen, source):
@@ -60,14 +62,40 @@
     count = len(outs)
     each = gathered_ref.shape[0] // count
     piece = gathered_ref.shape[2]
+    main = outs[0].shape[1]
+    rest = own_ref.shape[1] - main
+    block = each * piece
+    turned = (((0,), (1,)), ((), ()))
+    own_rest = own_ref[:, main:]
+    other_rest = other_ref[:, main:]
     for k, out in enumerate(outs):
         target = lax.rem(here_ref[0] + k, count)
         for j in range(each):
             at = target * each + j
+            mine = gathered_ref[at, 0]
+            theirs = paired_ref[at]
             out[pl.ds(j * piece, piece), :] = (
-                jnp.dot(gathered_ref[at, 0], own_ref[...], preferred_element_type=F32)
-                + jnp.dot(paired_ref[at], other_ref[...], preferred_element_type=F32)
+                jnp.dot(mine, own_ref[:, :main], preferred_element_type=F32)
+                + jnp.dot(theirs, other_ref[:, :main], preferred_element_type=F32)
             ).astype(out.dtype)
+            out[pl.ds(block, rest), pl.ds(j * piece, piece)] = (
+                lax.dot_general(own_rest, mine, turned, preferred_element_type=F32)
+                + lax.dot_general(other_rest, theirs, turned, preferred_element_type=F32)
+            ).astype(out.dtype)
+        out[pl.ds(block, rest), pl.ds(block, main - block)] = jnp.zeros(
+            (rest, main - block), out.dtype
+        )
+
+
+def sum_x_kernel(own_ref, *refs):
+    out = refs[-1]
+    block = out.shape[0]
+    main = own_ref.shape[1]
+    total = own_ref[...]
+    for ref in refs[:-1]:
+        total += ref[...].astype(F32)
+    out[:, :main] = total[:block].astype(BF16)
+    out[:, main:] = total[block:, :block].T.astype(BF16)
 
 
 def norm_kernel(channels, sums_ref, dy_ref, gain_ref, cnx_ref, sig_ref, cnx_out, sig_out):
@@ -141,11 +169,28 @@
 
     paired = lax.ppermute(gathered[:, 1], "rep", swap)
 
+    row = lax.broadcasted_iota(jnp.int32, (rows, rows), 0)
+    column = lax.broadcasted_iota(jnp.int32, (rows, rows), 1)
+    back = lax.dot_general(
+        gathered.reshape(enc_count * cols, rows),
+        weight,
+        (((0,), (0,)), ((), ())),
+        preferred_element_type=F32,
+    ).astype(BF16)
+    goal = ((enc_of[0] * depth)[:, None] + token).reshape(1, rows)
+    held = pick(row == goal, back).reshape(slots, depth, width)
+    held, paired = lax.optimization_barrier((held, paired))
+    held = exchange(held, ("x", "z")).reshape(rows, width)
+    place = ((owner_of[0] * depth)[:, None] + token).reshape(rows, 1)
+    routed = pick(column == place, held)
+
     block = enc_count * half // nx
+    main = width // 128 * 128
+    tall = block + width - main
     parts = pl.pallas_call(
         partial_kernel,
         out_shape=[
-            jax.ShapeDtypeStruct((block, width), F32 if k == 0 else BF16) for k in range(nx)
+            jax.ShapeDtypeStruct((tall, main), F32 if k == 0 else BF16) for k in range(nx)
         ],
         in_specs=[SMEM, VMEM, VMEM, VMEM, VMEM],
         out_specs=[VMEM] * nx,
@@ -157,23 +202,14 @@
         ),
         name="partial",
     )(hx.reshape(1), gathered, features, paired, other_features)
-
-    row = lax.broadcasted_iota(jnp.int32, (rows, rows), 0)
-    column = lax.broadcasted_iota(jnp.int32, (rows, rows), 1)
-    back = lax.dot_general(
-        gathered.reshape(enc_count * cols, rows),
-        weight,
-        (((0,), (0,)), ((), ())),
-        preferred_element_type=F32,
-    ).astype(BF16)
-    goal = ((enc_of[0] * depth)[:, None] + token).reshape(1, rows)
-    held = pick(row == goal, back).reshape(slots, depth, width)
-    held = exchange(held, ("x", "z")).reshape(rows, width)
-    place = ((owner_of[0] * depth)[:, None] + token).reshape(rows, 1)
-    routed = pick(column == place, held)
-
     parts = hand_on(parts, "x")
-    total = sum((part.astype(F32) for part in parts[1:]), parts[0]).astype(BF16)
+    total = pl.pallas_call(
+        sum_x_kernel,
+        out_shape=jax.ShapeDtypeStruct((block, width), BF16),
+        in_specs=[VMEM] * nx,
+        out_specs=VMEM,
+        name="sum_x",
+    )(*parts)
     split = feat_cnx.shape[1]
 
     sums = []

time: 131 us -> 130 us (level)
  Pallas kernels: 6.58 us -> 8.32 us
    pallas_call x1 -> x2, Pallas kernels: 1.52 us -> 3.25 us  [the longest x1 2.25 us: shards(): pl.pallas_call(sum_x_kernel, out_shape=jax.ShapeDtypeStruct((block, width...]
    ppermute x3, waiting for transfers between devices: 14.7 us -> 13.4 us  [hand_on(): got = {k: lax.ppermute(blocks[k], axis, shift(count, k)) for k in order}]
  transfers between devices with their start and end apart: 8 -> 8, of which waited for: 5 -> 5; matrix products, arithmetic and copies ran while one was open for 18% -> 17% of each run, Pallas kernels for 3% -> 5%
where the time goes in v6:
time: 130 us; the launch traced here: 128 us
  starting transfers between devices  52.9 us (41%)
  waiting for transfers between devices  25.5 us (20%)
  local copies, waits for them, and re-layouts  16.9 us (13%)
  blocking collectives  15.5 us (12%)
  Pallas kernels  8.32 us (6%)
  other arithmetic  5.55 us (4%)
  matrix products  2.84 us (2%)
    all_to_all x3, starting transfers between devices, exchange(): return lax.all_to_all(blocks, axis, 0, 0, tiled=True)  40.4 us
    psum x1, blocking collectives, shards(): sums = lax.psum(sums, 'enc')  15.5 us
    ppermute x3, waiting for transfers between devices, hand_on(): got = {k: lax.ppermute(blocks[k], axis, shift(count, k)) for k in order}  13.4 us
    all_to_all x3, waiting for transfers between devices, exchange(): return lax.all_to_all(blocks, axis, 0, 0, tiled=True)  12.1 us
    ppermute x3, starting transfers between devices, hand_on(): got = {k: lax.ppermute(blocks[k], axis, shift(count, k)) for k in order}  8.67 us
    another operation x1, local copies, waits for them, and re-layouts, shards(): jnp.stack([lax.dynamic_index_in_dim(weight, index, 2, keepdims=False).res...  6.49 us
    reshape x1, local copies, waits for them, and re-layouts, shards(): weight = jnp.stack([lax.dynamic_index_in_dim(weight, index, 2, keepdims=F...  5.89 us
    dot_general x2, matrix products, pick(): jnp.dot(chosen.astype(BF16), source, preferred_element_type=F32)  2.84 us
  transfers between devices with their start and end apart: 8, of which 5 were waited for; matrix products, arithmetic and copies ran while one was open for 17% of the time, Pallas kernels for 5%

profile of v6, /device:TPU:6, one launch (start us, length us, event | category | flops | bytes accessed | tf_op | source)
XLA Modules:
  0.0 128.5 jit_solution(11816958998592248115)
XLA Ops:
  0.7 2.3 %turn.1 = bf16[8,2,128,256]{3,2,1,0:T(8,128)(2,1)} custom-call(s32[1]{0:T(128)} %bitcast.4.core_ref, s32[1,64]{1,0:T(1,128)} %lengths_ref.1, bf16[256,256]{1,0:T(8,128)(2,1)} %cotangent_ref.1), custom_call_target="tpu_custom_call" | custom-call | tf_op jit(solution)/shard_map/turn/pallas_call | solution.py:147
  2.9 7.1 %all-to-all-start = ((bf16[8,2,128,256]{3,2,1,0:T(8,128)(2,1)}), bf16[8,2,128,256]{3,2,1,0:T(8,128)(2,1)S(1)}, u32[]{:S(2)}, u32[]{:S(2)}) async-start(bf16[8,2,128,256]{3,2,1,0:T(8,128)(2,1)} %turn.1), calls=%async_computation | async-start | bytes 2097152 | tf_op jit(solution)/shard_map/all_to_all | solution.py:24
  10.2 1.9 %collective-permute-start = (bf16[256,528]{1,0:T(8,128)(2,1)S(1)}, bf16[256,528]{1,0:T(8,128)(2,1)S(1)}, u32[]{:S(2)}, u32[]{:S(2)}) collective-permute-start(bf16[256,528]{1,0:T(8,128)(2,1)S(1)} %pad_maximum_fusion.2.own_ref), channel_id=1, source_target_pairs={{0,1},{1,0},{2,3},{3,2},{4,5},{5,4},{6,7},{7,6},{8,9},{9,8},{10,11... | collective-permute-start | bytes 811016 | tf_op jit(solution)/shard_map/ppermute | solution.py:157
  12.1 0.5 copy.44
  12.6 1.7 %pad_maximum_fusion = bf16[2048,528]{1,0:T(8,128)(2,1)S(1)} fusion(bf16[2048,144]{1,0:T(8,128)(2,1)S(1)} %copy.44, bf16[2048,384]{1,0:T(8,128)(2,1)} %param.16), kind=kLoop, calls=%fused_computation | loop fusion | flops 4325376 | bytes 4325376 | tf_op jit(solution)/shard_map/concatenate | solution.py:158
  14.3 0.2 constant_dynamic-slice_fusion.1
  14.6 1.9 %pad_maximum_fusion.1 = bf16[8,2,128,528]{3,2,0,1:T(8,128)(2,1)} fusion(bf16[8,1,128,528]{3,2,0,1:T(8,128)(2,1)S(1)} %bitcast.35, bf16[8,1,128,528]{3,2,0,1:T(8,128)(2,1)S(1)} %bitcast.34), kind=kLoop, calls=%fused_computation.1 | loop fusion | flops 1081344 | bytes 4325376 | tf_op jit(solution)/shard_map/stack | solution.py:161
  16.5 6.5 %copy.47 = bf16[8,2,128,528]{2,1,0,3:T(2,128)(2,1)} copy(bf16[8,2,128,528]{3,2,0,1:T(8,128)(2,1)} %pad_maximum_fusion.1) | data formatting | bytes 4325376 | tf_op jit(solution)/shard_map/stack | solution.py:161
  23.0 5.9 %reshape.82 = bf16[2048,528]{0,1:T(8,128)(2,1)} reshape(bf16[8,2,128,528]{2,1,0,3:T(2,128)(2,1)} %copy.47) | data formatting | bytes 4325376 | tf_op jit(solution)/shard_map/reshape | solution.py:167
  28.9 9.9 %all-to-all-done.gathered_ref = bf16[8,2,128,256]{3,2,1,0:T(8,128)(2,1)S(1)} async-done(((bf16[8,2,128,256]{3,2,1,0:T(8,128)(2,1)}), bf16[8,2,128,256]{3,2,1,0:T(8,128)(2,1)S(1)}, u32[]{:S(2)}, u32[]{:S(2)}) %all-to-all-start) | async-done | bytes 1048608 | tf_op jit(solution)/shard_map/all_to_all | solution.py:24
  38.8 1.9 %collective-permute-start.1 = (bf16[8,128,256]{2,1,0:T(8,128)(2,1)S(1)}, bf16[8,128,256]{2,1,0:T(8,128)(2,1)S(1)}, u32[]{:S(2)}, u32[]{:S(2)}) collective-permute-start(bf16[8,128,256]{2,1,0:T(8,128)(2,1)S(1)} %slice_bitcast_fusion), channel_id=1, source_target_pairs={{0,1},{1,0},{2,3},{3,2},{4,5},{5,4},{6,7},{7,6},{8,9},{9,8},{10,11... | collective-permute-start | bytes 1572872 | tf_op jit(solution)/shard_map/ppermute | solution.py:170
  40.9 2.5 %convolution_convert_fusion.2 = bf16[256,528]{0,1:T(8,128)(2,1)S(1)} fusion(bf16[2048,528]{0,1:T(8,128)(2,1)} %reshape.82, bf16[2048,256]{1,0:T(8,128)(2,1)S(1)} %bitcast.32, s32[256]{0:T(256)S(1)} %add.45), kind=kOutput, calls=%fused_computation.4 | convolution fusion | flops 623190016 | bytes 3482624 | tf_op jit(solution)/shard_map/dot_general | solution.py:35
  43.7 0.8 reshape.84
  44.5 22.5 %all-to-all-start.1 = ((bf16[64,4,528]{2,1,0:T(4,128)(2,1)}), bf16[64,4,528]{2,1,0:T(4,128)(2,1)S(1)}, u32[]{:S(2)}, u32[]{:S(2)}) async-start(bf16[64,4,528]{2,1,0:T(4,128)(2,1)} %reshape.84), calls=%async_computation.1 | async-start | bytes 655360 | tf_op jit(solution)/shard_map/all_to_all | solution.py:24
  67.0 1.0 partial.1
  68.0 0.8 copy-done
  68.8 2.3 %collective-permute-start.2 = (bf16[272,512]{1,0:T(8,128)(2,1)S(1)}, bf16[272,512]{1,0:T(8,128)(2,1)S(1)}, u32[]{:S(2)}, u32[]{:S(2)}) collective-permute-start(bf16[272,512]{1,0:T(8,128)(2,1)S(1)} %get-tuple-element.23), channel_id=1, source_target_pairs={{0,32},{32,64},{64,96},{96,0},{1,33},{33,65},{65,97},{97,1},{2,34}... | collective-permute-start | bytes 835592 | tf_op jit(solution)/shard_map/ppermute | solution.py:30
  71.1 4.5 %collective-permute-start.3 = (bf16[272,512]{1,0:T(8,128)(2,1)S(1)}, bf16[272,512]{1,0:T(8,128)(2,1)S(1)}, u32[]{:S(2)}, u32[]{:S(2)}) collective-permute-start(bf16[272,512]{1,0:T(8,128)(2,1)S(1)} %get-tuple-element.24), channel_id=1, source_target_pairs={{0,64},{32,96},{64,0},{96,32},{1,65},{33,97},{65,1},{97,33},{2,66}... | collective-permute-start | bytes 835592 | tf_op jit(solution)/shard_map/ppermute | solution.py:30
  75.5 1.9 %collective-permute-start.4 = (bf16[272,512]{1,0:T(8,128)(2,1)S(1)}, bf16[272,512]{1,0:T(8,128)(2,1)S(1)}, u32[]{:S(2)}, u32[]{:S(2)}) collective-permute-start(bf16[272,512]{1,0:T(8,128)(2,1)S(1)} %get-tuple-element.25), channel_id=1, source_target_pairs={{0,96},{32,0},{64,32},{96,64},{1,97},{33,1},{65,33},{97,65},{2,98}... | collective-permute-start | bytes 835592 | tf_op jit(solution)/shard_map/ppermute | solution.py:30
  77.8 4.9 %collective-permute-done.2.refs_0_ = bf16[272,512]{1,0:T(8,128)(2,1)S(1)} collective-permute-done((bf16[272,512]{1,0:T(8,128)(2,1)S(1)}, bf16[272,512]{1,0:T(8,128)(2,1)S(1)}, u32[]{:S(2)}, u32[]{:S(2)}) %collective-permute-start.2) | collective-permute-done | bytes 278560 | tf_op jit(solution)/shard_map/ppermute | solution.py:30
  82.7 3.1 %collective-permute-done.3.refs_1_ = bf16[272,512]{1,0:T(8,128)(2,1)S(1)} collective-permute-done((bf16[272,512]{1,0:T(8,128)(2,1)S(1)}, bf16[272,512]{1,0:T(8,128)(2,1)S(1)}, u32[]{:S(2)}, u32[]{:S(2)}) %collective-permute-start.3) | collective-permute-done | bytes 278560 | tf_op jit(solution)/shard_map/ppermute | solution.py:30
  85.8 5.4 %collective-permute-done.4.refs_2_ = bf16[272,512]{1,0:T(8,128)(2,1)S(1)} collective-permute-done((bf16[272,512]{1,0:T(8,128)(2,1)S(1)}, bf16[272,512]{1,0:T(8,128)(2,1)S(1)}, u32[]{:S(2)}, u32[]{:S(2)}) %collective-permute-start.4) | collective-permute-done | bytes 278560 | tf_op jit(solution)/shard_map/ppermute | solution.py:30
  91.2 0.7 copy-done.7
  91.9 2.3 %sum_x.1 = bf16[256,528]{1,0:T(8,128)(2,1)} custom-call(f32[272,512]{1,0:T(8,128)} %copy-done, bf16[272,512]{1,0:T(8,128)(2,1)} %copy-done.5, bf16[272,512]{1,0:T(8,128)(2,1)} %copy-done.6, bf16[272,512]{1,0:T(8,128)(2,1)} %copy-done.7), custom_call_target="tpu_custom_call" | custom-call | tf_op jit(solution)/shard_map/sum_x/pallas_call | solution.py:206
  94.3 0.3 convolution_convert_fusion.dy_ref
  95.2 10.8 %all-to-all-start.2 = ((bf16[16,16,528]{2,1,0:T(8,128)(2,1)}), bf16[16,16,528]{2,1,0:T(8,128)(2,1)S(1)}, u32[]{:S(2)}, u32[]{:S(2)}) async-start(bf16[16,16,528]{2,1,0:T(8,128)(2,1)} %bitcast.36), calls=%async_computation.2 | async-start | bytes 655360 | tf_op jit(solution)/shard_map/all_to_all | solution.py:24
  106.0 0.6 broadcast_in_dim.2.gain_ref
  106.6 15.5 %psum.7.sums_ref = f32[8,256]{1,0:T(8,128)} all-reduce(f32[8,256]{1,0:T(8,128)S(1)} %stack.39), channel_id=1, replica_groups=mesh['enc'=8,'x'=4,'z'=16,'rep'=2] {'enc'}, use_global_device_ids=true, to_apply=%region_10.11 | all-reduce | flops 2048 | bytes 16384 | tf_op jit(solution)/shard_map/psum | solution.py:230
  122.1 2.8 %norm.1 = (bf16[256,384]{1,0:T(8,128)(2,1)}, bf16[144,256]{1,0:T(8,128)(2,1)}) custom-call(f32[8,256]{1,0:T(8,128)} %psum.7.sums_ref, bf16[256,528]{1,0:T(8,128)(2,1)} %copy-done.1, f32[1,528]{1,0:T(1,128)} %broadcast_in_dim.2.gain_ref, bf16[256,384]{1,0:T(8,128)(2,1)} %cnx_ref.1, bf16[144,256]{1,0:T(8,128)(2,1)} %bitcast.37), custom_call_target="tpu_custom_call" | custom-call | flops 1 | bytes 1 | tf_op jit(solution)/shard_map/norm/pallas_call | solution.py:231
  124.9 2.3 %all-to-all-done.2 = bf16[16,16,528]{2,1,0:T(8,128)(2,1)S(1)} async-done(((bf16[16,16,528]{2,1,0:T(8,128)(2,1)}), bf16[16,16,528]{2,1,0:T(8,128)(2,1)S(1)}, u32[]{:S(2)}, u32[]{:S(2)}) %all-to-all-start.2) | async-done | bytes 270368 | tf_op jit(solution)/shard_map/all_to_all | solution.py:24
  127.2 0.6 broadcast_multiply_fusion
  127.9 0.6 broadcast_multiply_fusion.1
  (47 shorter events, 1.6 us)
Async XLA Ops:
  0.6 9.4 %copy-start.9 = (bf16[256,144]{0,1:T(8,128)(2,1)S(1)}, bf16[256,144]{0,1:T(8,128)(2,1)}, u32[]{:S(2)}) copy-start(bf16[256,144]{0,1:T(8,128)(2,1)} %param.12) | copy-start | bytes 221188
  0.6 9.5 %copy-start.8 = (bf16[256,384]{1,0:T(8,128)(2,1)S(1)}, bf16[256,384]{1,0:T(8,128)(2,1)}, u32[]{:S(2)}) copy-start(bf16[256,384]{1,0:T(8,128)(2,1)} %param.13) | copy-start | bytes 589828
  0.7 11.5 %copy-start.3 = (bf16[2048,144]{0,1:T(8,128)(2,1)S(1)}, bf16[2048,144]{0,1:T(8,128)(2,1)}, u32[]{:S(2)}) copy-start(bf16[2048,144]{0,1:T(8,128)(2,1)} %param.15) | copy-start | bytes 1769476
  2.9 35.8 %all-to-all-start = ((bf16[8,2,128,256]{3,2,1,0:T(8,128)(2,1)}), bf16[8,2,128,256]{3,2,1,0:T(8,128)(2,1)S(1)}, u32[]{:S(2)}, u32[]{:S(2)}) async-start(bf16[8,2,128,256]{3,2,1,0:T(8,128)(2,1)} %turn.1), calls=%async_computation | async-start | bytes 2097152 | tf_op jit(solution)/shard_map/all_to_all | solution.py:24
  10.2 18.7 %collective-permute-start = (bf16[256,528]{1,0:T(8,128)(2,1)S(1)}, bf16[256,528]{1,0:T(8,128)(2,1)S(1)}, u32[]{:S(2)}, u32[]{:S(2)}) collective-permute-start(bf16[256,528]{1,0:T(8,128)(2,1)S(1)} %pad_maximum_fusion.2.own_ref), channel_id=1, source_target_pairs={{0,1},{1,0},{2,3},{3,2},{4,5},{5,4},{6,7},{7,6},{8,9},{9,8},{10,11... | collective-permute-start | bytes 811016 | tf_op jit(solution)/shard_map/ppermute | solution.py:157
  23.0 5.9 %copy-start.12 = (s32[1,64]{1,0:T(1,128)S(1)}, s32[1,64]{1,0:T(1,128)}, u32[]{:S(2)}) copy-start(s32[1,64]{1,0:T(1,128)} %param.18) | copy-start | bytes 772
  38.8 5.7 %collective-permute-start.1 = (bf16[8,128,256]{2,1,0:T(8,128)(2,1)S(1)}, bf16[8,128,256]{2,1,0:T(8,128)(2,1)S(1)}, u32[]{:S(2)}, u32[]{:S(2)}) collective-permute-start(bf16[8,128,256]{2,1,0:T(8,128)(2,1)S(1)} %slice_bitcast_fusion), channel_id=1, source_target_pairs={{0,1},{1,0},{2,3},{3,2},{4,5},{5,4},{6,7},{7,6},{8,9},{9,8},{10,11... | collective-permute-start | bytes 1572872 | tf_op jit(solution)/shard_map/ppermute | solution.py:170
  43.5 34.0 %copy-start.13 = (s32[1,64]{1,0:T(1,128)S(1)}, s32[1,64]{1,0:T(1,128)}, u32[]{:S(2)}) copy-start(s32[1,64]{1,0:T(1,128)} %param.19) | copy-start | bytes 772
  43.5 34.2 %copy-start.4 = (bf16[256,144]{0,1:T(8,128)(2,1)S(1)}, bf16[256,144]{0,1:T(8,128)(2,1)}, u32[]{:S(2)}) copy-start(bf16[256,144]{0,1:T(8,128)(2,1)} %param.20) | copy-start | bytes 221188
  44.5 49.6 %all-to-all-start.1 = ((bf16[64,4,528]{2,1,0:T(4,128)(2,1)}), bf16[64,4,528]{2,1,0:T(4,128)(2,1)S(1)}, u32[]{:S(2)}, u32[]{:S(2)}) async-start(bf16[64,4,528]{2,1,0:T(4,128)(2,1)} %reshape.84), calls=%async_computation.1 | async-start | bytes 655360 | tf_op jit(solution)/shard_map/all_to_all | solution.py:24
  68.0 0.8 copy-start
  68.8 25.8 %copy-start.11 = (f32[144]{0:T(256)S(1)}, f32[144]{0:T(256)}, u32[]{:S(2)}) copy-start(f32[144]{0:T(256)} %param.22) | copy-start | bytes 1732
  68.8 26.1 %copy-start.2 = (bf16[256,384]{1,0:T(8,128)(2,1)S(1)}, bf16[256,384]{1,0:T(8,128)(2,1)}, u32[]{:S(2)}) copy-start(bf16[256,384]{1,0:T(8,128)(2,1)} %cnx_ref.1) | copy-start | bytes 589828
  68.8 26.1 %copy-start.10 = (f32[384]{0:T(512)S(1)}, f32[384]{0:T(512)}, u32[]{:S(2)}) copy-start(f32[384]{0:T(512)} %param.23) | copy-start | bytes 4612
  68.8 13.9 %collective-permute-start.2 = (bf16[272,512]{1,0:T(8,128)(2,1)S(1)}, bf16[272,512]{1,0:T(8,128)(2,1)S(1)}, u32[]{:S(2)}, u32[]{:S(2)}) collective-permute-start(bf16[272,512]{1,0:T(8,128)(2,1)S(1)} %get-tuple-element.23), channel_id=1, source_target_pairs={{0,32},{32,64},{64,96},{96,0},{1,33},{33,65},{65,97},{97,1},{2,34}... | collective-permute-start | bytes 835592 | tf_op jit(solution)/shard_map/ppermute | solution.py:30
  71.1 14.7 %collective-permute-start.3 = (bf16[272,512]{1,0:T(8,128)(2,1)S(1)}, bf16[272,512]{1,0:T(8,128)(2,1)S(1)}, u32[]{:S(2)}, u32[]{:S(2)}) collective-permute-start(bf16[272,512]{1,0:T(8,128)(2,1)S(1)} %get-tuple-element.24), channel_id=1, source_target_pairs={{0,64},{32,96},{64,0},{96,32},{1,65},{33,97},{65,1},{97,33},{2,66}... | collective-permute-start | bytes 835592 | tf_op jit(solution)/shard_map/ppermute | solution.py:30
  75.5 15.6 %collective-permute-start.4 = (bf16[272,512]{1,0:T(8,128)(2,1)S(1)}, bf16[272,512]{1,0:T(8,128)(2,1)S(1)}, u32[]{:S(2)}, u32[]{:S(2)}) collective-permute-start(bf16[272,512]{1,0:T(8,128)(2,1)S(1)} %get-tuple-element.25), channel_id=1, source_target_pairs={{0,96},{32,0},{64,32},{96,64},{1,97},{33,1},{65,33},{97,65},{2,98}... | collective-permute-start | bytes 835592 | tf_op jit(solution)/shard_map/ppermute | solution.py:30
  82.7 8.5 %copy-start.5 = (bf16[272,512]{1,0:T(8,128)(2,1)}, bf16[272,512]{1,0:T(8,128)(2,1)S(1)}, u32[]{:S(2)}) copy-start(bf16[272,512]{1,0:T(8,128)(2,1)S(1)} %collective-permute-done.2.refs_0_) | copy-start | bytes 835588
  85.8 5.4 %copy-start.6 = (bf16[272,512]{1,0:T(8,128)(2,1)}, bf16[272,512]{1,0:T(8,128)(2,1)S(1)}, u32[]{:S(2)}) copy-start(bf16[272,512]{1,0:T(8,128)(2,1)S(1)} %collective-permute-done.3.refs_1_) | copy-start | bytes 835588
  91.2 0.7 copy-start.7
  94.6 27.5 %copy-start.1 = (bf16[256,528]{1,0:T(8,128)(2,1)}, bf16[256,528]{1,0:T(8,128)(2,1)S(1)}, u32[]{:S(2)}) copy-start(bf16[256,528]{1,0:T(8,128)(2,1)S(1)} %convolution_convert_fusion.dy_ref) | copy-start | bytes 811012
  95.2 32.0 %all-to-all-start.2 = ((bf16[16,16,528]{2,1,0:T(8,128)(2,1)}), bf16[16,16,528]{2,1,0:T(8,128)(2,1)S(1)}, u32[]{:S(2)}, u32[]{:S(2)}) async-start(bf16[16,16,528]{2,1,0:T(8,128)(2,1)} %bitcast.36), calls=%async_computation.2 | async-start | bytes 655360 | tf_op jit(solution)/shard_map/all_to_all | solution.py:24

commit v7 on v5

--- a/solution.py
+++ b/solution.py
@@ -22,11 +22,6 @@
 
 def exchange(blocks, axis):
     return lax.all_to_all(blocks, axis, 0, 0, tiled=True)
-
-
-def hand_on(blocks, axis):
-    count = lax.axis_size(axis)
-    return [blocks[0]] + [lax.ppermute(blocks[k], axis, shift(count, k)) for k in range(1, count)]
 
 
 def pick(chosen, source):
@@ -56,18 +51,32 @@
                 out_ref[copy, half, pl.ds(k * piece, piece), :] = block
 
 
-def partial_kernel(here_ref, gathered_ref, own_ref, paired_ref, other_ref, *outs):
-    count = len(outs)
+def partial_kernel(count, steps, here_ref, gathered_ref, own_ref, paired_ref, other_ref, *outs):
     each = gathered_ref.shape[0] // count
     piece = gathered_ref.shape[2]
-    for k, out in enumerate(outs):
+    main = outs[0].shape[1]
+    rest = own_ref.shape[1] - main
+    block = each * piece
+    turned = (((0,), (1,)), ((), ()))
+    own_rest = own_ref[:, main:]
+    other_rest = other_ref[:, main:]
+    for k, out in zip(steps, outs):
         target = lax.rem(here_ref[0] + k, count)
         for j in range(each):
             at = target * each + j
+            mine = gathered_ref[at, 0]
+            theirs = paired_ref[at]
             out[pl.ds(j * piece, piece), :] = (
-                jnp.dot(gathered_ref[at, 0], own_ref[...], preferred_element_type=F32)
-                + jnp.dot(paired_ref[at], other_ref[...], preferred_element_type=F32)
+                jnp.dot(mine, own_ref[:, :main], preferred_element_type=F32)
+                + jnp.dot(theirs, other_ref[:, :main], preferred_element_type=F32)
             ).astype(out.dtype)
+            out[pl.ds(block, rest), pl.ds(j * piece, piece)] = (
+                lax.dot_general(own_rest, mine, turned, preferred_element_type=F32)
+                + lax.dot_general(other_rest, theirs, turned, preferred_element_type=F32)
+            ).astype(out.dtype)
+        out[pl.ds(block, rest), pl.ds(block, main - block)] = jnp.zeros(
+            (rest, main - block), out.dtype
+        )
 
 
 def norm_kernel(channels, sums_ref, dy_ref, gain_ref, cnx_ref, sig_ref, cnx_out, sig_out):
@@ -137,26 +146,39 @@
         ],
         axis=1,
     ).reshape(enc_count * cols, width)
-    gathered, other_features, weight = lax.optimization_barrier((gathered, other_features, weight))
+    gains = jnp.concatenate([gain_cnx, gain_sig])[None, :]
+    gathered, other_features, weight, gains = lax.optimization_barrier(
+        (gathered, other_features, weight, gains)
+    )
 
     paired = lax.ppermute(gathered[:, 1], "rep", swap)
 
     block = enc_count * half // nx
-    parts = pl.pallas_call(
-        partial_kernel,
-        out_shape=[
-            jax.ShapeDtypeStruct((block, width), F32 if k == 0 else BF16) for k in range(nx)
-        ],
-        in_specs=[SMEM, VMEM, VMEM, VMEM, VMEM],
-        out_specs=[VMEM] * nx,
-        compiler_params=pltpu.CompilerParams(vmem_limit_bytes=32 * 2**20),
-        cost_estimate=pl.CostEstimate(
-            flops=4 * enc_count * half * rows * width,
-            bytes_accessed=4 * enc_count * half * width,
-            transcendentals=0,
-        ),
-        name="partial",
-    )(hx.reshape(1), gathered, features, paired, other_features)
+    main = width // 128 * 128
+    tall = block + width - main
+
+    def multiply(steps):
+        return list(
+            pl.pallas_call(
+                functools.partial(partial_kernel, nx, steps),
+                out_shape=[
+                    jax.ShapeDtypeStruct((tall, main), BF16 if k else F32) for k in steps
+                ],
+                in_specs=[SMEM, VMEM, VMEM, VMEM, VMEM],
+                out_specs=[VMEM] * len(steps),
+                compiler_params=pltpu.CompilerParams(vmem_limit_bytes=32 * 2**20),
+                cost_estimate=pl.CostEstimate(
+                    flops=4 * block * len(steps) * rows * width,
+                    bytes_accessed=4 * block * len(steps) * width,
+                    transcendentals=0,
+                ),
+                name="partial",
+            )(hx.reshape(1), gathered, features, paired, other_features)
+        )
+
+    far = nx // 2
+    (far_part,) = multiply([far])
+    far_got = lax.ppermute(far_part, "x", shift(nx, far))
 
     row = lax.broadcasted_iota(jnp.int32, (rows, rows), 0)
     column = lax.broadcasted_iota(jnp.int32, (rows, rows), 1)
@@ -168,12 +190,19 @@
     ).astype(BF16)
     goal = ((enc_of[0] * depth)[:, None] + token).reshape(1, rows)
     held = pick(row == goal, back).reshape(slots, depth, width)
+    held, far_part = lax.optimization_barrier((held, far_part))
     held = exchange(held, ("x", "z")).reshape(rows, width)
     place = ((owner_of[0] * depth)[:, None] + token).reshape(rows, 1)
     routed = pick(column == place, held)
 
-    parts = hand_on(parts, "x")
+    parts = multiply([k for k in range(nx) if k != far])
+    parts.insert(far, far_part)
+    parts = [
+        far_got if k == far else lax.ppermute(part, "x", shift(nx, k)) if k else part
+        for k, part in enumerate(parts)
+    ]
     total = sum((part.astype(F32) for part in parts[1:]), parts[0]).astype(BF16)
+    total = jnp.concatenate([total[:block], total[block:, :block].T], axis=1)
     split = feat_cnx.shape[1]
 
     sums = []
@@ -204,7 +233,7 @@
         out_specs=[VMEM] * 2,
         cost_estimate=pl.CostEstimate(flops=1, bytes_accessed=1, transcendentals=0),
         name="norm",
-    )(sums, routed, jnp.concatenate([gain_cnx, gain_sig])[None, :], pre_cnx, pre_sig.T)
+    )(sums, routed, gains, pre_cnx, pre_sig.T)
     scale = 1.0 / math.sqrt(rows * nx * nz * rep_count)
     grad_cnx = jnp.sum(total[:, :, :split].astype(F32), axis=0) * scale
     grad_sig = jnp.sum(total[:, :, split:].astype(F32), axis=0) * scale

time: 131 us -> 125 us (0.954)
  starting transfers between devices: 53 us -> 48.7 us
    ppermute x3, waiting for transfers between devices: 14.7 us -> 8.94 us  [the longest x2 8.93 us: shards(): lax.ppermute(part, 'x', shift(nx, k))]
    all_to_all x3, waiting for transfers between devices: 11.5 us -> 16.5 us  [exchange(): return lax.all_to_all(blocks, axis, 0, 0, tiled=True)]
    all_to_all x3, starting transfers between devices: 40.5 us -> 35.7 us  [exchange(): return lax.all_to_all(blocks, axis, 0, 0, tiled=True)]
  transfers between devices with their start and end apart: 8 -> 8, of which waited for: 5 -> 5; matrix products, arithmetic and copies ran while one was open for 18% -> 19% of each run, Pallas kernels for 3% -> 3%
where the time goes in v7:
time: 125 us; the launch traced here: 124 us
  starting transfers between devices  48.7 us (39%)
  waiting for transfers between devices  25.5 us (20%)
  local copies, waits for them, and re-layouts  16.5 us (13%)
  blocking collectives  15.5 us (12%)
  other arithmetic  7.46 us (6%)
  Pallas kernels  6.81 us (5%)
  matrix products  2.84 us (2%)
    all_to_all x3, starting transfers between devices, exchange(): return lax.all_to_all(blocks, axis, 0, 0, tiled=True)  35.7 us
    all_to_all x3, waiting for transfers between devices, exchange(): return lax.all_to_all(blocks, axis, 0, 0, tiled=True)  16.5 us
    psum x1, blocking collectives, shards(): sums = lax.psum(sums, 'enc')  15.5 us
    ppermute x2, waiting for transfers between devices, shards(): lax.ppermute(part, 'x', shift(nx, k))  8.93 us
    another operation x1, local copies, waits for them, and re-layouts, shards(): jnp.stack([lax.dynamic_index_in_dim(weight, index, 2, keepdims=False).res...  6.5 us
    reshape x1, local copies, waits for them, and re-layouts, shards(): weight = jnp.stack([lax.dynamic_index_in_dim(weight, index, 2, keepdims=F...  5.89 us
    ppermute x2, starting transfers between devices, shards(): lax.ppermute(part, 'x', shift(nx, k))  5.83 us
    ppermute x1, starting transfers between devices, shards(): far_got = lax.ppermute(far_part, 'x', shift(nx, far))  3.31 us
  transfers between devices with their start and end apart: 8, of which 5 were waited for; matrix products, arithmetic and copies ran while one was open for 19% of the time, Pallas kernels for 3%

profile of v7, /device:TPU:6, one launch (start us, length us, event | category | flops | bytes accessed | tf_op | source)
XLA Modules:
  0.0 124.2 jit_solution(13235987769363221520)
XLA Ops:
  0.7 2.3 %turn.1 = bf16[8,2,128,256]{3,2,1,0:T(8,128)(2,1)} custom-call(s32[1]{0:T(128)} %bitcast.4.core_ref, s32[1,64]{1,0:T(1,128)} %lengths_ref.1, bf16[256,256]{1,0:T(8,128)(2,1)} %cotangent_ref.1), custom_call_target="tpu_custom_call" | custom-call | tf_op jit(solution)/shard_map/turn/pallas_call | solution.py:128
  2.9 7.1 %all-to-all-start = ((bf16[8,2,128,256]{3,2,1,0:T(8,128)(2,1)}), bf16[8,2,128,256]{3,2,1,0:T(8,128)(2,1)S(1)}, u32[]{:S(2)}, u32[]{:S(2)}) async-start(bf16[8,2,128,256]{3,2,1,0:T(8,128)(2,1)} %turn.1), calls=%async_computation | async-start | bytes 2097152 | tf_op jit(solution)/shard_map/all_to_all | solution.py:24
  10.2 1.9 %collective-permute-start = (bf16[256,528]{1,0:T(8,128)(2,1)S(1)}, bf16[256,528]{1,0:T(8,128)(2,1)S(1)}, u32[]{:S(2)}, u32[]{:S(2)}) collective-permute-start(bf16[256,528]{1,0:T(8,128)(2,1)S(1)} %pad_maximum_fusion.2.own_ref), channel_id=1, source_target_pairs={{0,1},{1,0},{2,3},{3,2},{4,5},{5,4},{6,7},{7,6},{8,9},{9,8},{10,11... | collective-permute-start | bytes 811016 | tf_op jit(solution)/shard_map/ppermute | solution.py:138
  12.1 0.5 copy.50
  12.6 1.7 %pad_maximum_fusion = bf16[2048,528]{1,0:T(8,128)(2,1)S(1)} fusion(bf16[2048,144]{1,0:T(8,128)(2,1)S(1)} %copy.50, bf16[2048,384]{1,0:T(8,128)(2,1)} %param.16), kind=kLoop, calls=%fused_computation | loop fusion | flops 4325376 | bytes 4325376 | tf_op jit(solution)/shard_map/concatenate | solution.py:139
  14.6 1.9 %pad_maximum_fusion.1 = bf16[8,2,128,528]{3,2,0,1:T(8,128)(2,1)} fusion(bf16[8,1,128,528]{3,2,0,1:T(8,128)(2,1)S(1)} %bitcast.37, bf16[8,1,128,528]{3,2,0,1:T(8,128)(2,1)S(1)} %bitcast.36), kind=kLoop, calls=%fused_computation.1 | loop fusion | flops 1081344 | bytes 4325376 | tf_op jit(solution)/shard_map/stack | solution.py:142
  16.5 6.5 %copy.53 = bf16[8,2,128,528]{2,1,0,3:T(2,128)(2,1)} copy(bf16[8,2,128,528]{3,2,0,1:T(8,128)(2,1)} %pad_maximum_fusion.1) | data formatting | bytes 4325376 | tf_op jit(solution)/shard_map/stack | solution.py:142
  23.0 5.9 %reshape.83 = bf16[2048,528]{0,1:T(8,128)(2,1)} reshape(bf16[8,2,128,528]{2,1,0,3:T(2,128)(2,1)} %copy.53) | data formatting | bytes 4325376 | tf_op jit(solution)/shard_map/reshape | solution.py:148
  28.9 0.6 broadcast_in_dim.2.gain_ref
  29.5 9.2 %all-to-all-done.gathered_ref = bf16[8,2,128,256]{3,2,1,0:T(8,128)(2,1)S(1)} async-done(((bf16[8,2,128,256]{3,2,1,0:T(8,128)(2,1)}), bf16[8,2,128,256]{3,2,1,0:T(8,128)(2,1)S(1)}, u32[]{:S(2)}, u32[]{:S(2)}) %all-to-all-start) | async-done | bytes 1048608 | tf_op jit(solution)/shard_map/all_to_all | solution.py:24
  38.8 1.9 %collective-permute-start.1 = (bf16[8,128,256]{2,1,0:T(8,128)(2,1)S(1)}, bf16[8,128,256]{2,1,0:T(8,128)(2,1)S(1)}, u32[]{:S(2)}, u32[]{:S(2)}) collective-permute-start(bf16[8,128,256]{2,1,0:T(8,128)(2,1)S(1)} %slice_bitcast_fusion), channel_id=1, source_target_pairs={{0,1},{1,0},{2,3},{3,2},{4,5},{5,4},{6,7},{7,6},{8,9},{9,8},{10,11... | collective-permute-start | bytes 1572872 | tf_op jit(solution)/shard_map/ppermute | solution.py:154
  40.9 2.5 %convolution_convert_fusion.2 = bf16[256,528]{0,1:T(8,128)(2,1)S(1)} fusion(bf16[2048,528]{0,1:T(8,128)(2,1)} %reshape.83, bf16[2048,256]{1,0:T(8,128)(2,1)S(1)} %bitcast.34, s32[256]{0:T(256)S(1)} %add.54), kind=kOutput, calls=%fused_computation.4 | convolution fusion | flops 623190016 | bytes 3482624 | tf_op jit(solution)/shard_map/dot_general | solution.py:28
  43.7 0.8 reshape.85
  44.5 0.4 partial.2
  44.9 3.3 %collective-permute-start.3 = (bf16[272,512]{1,0:T(8,128)(2,1)S(1)}, bf16[272,512]{1,0:T(8,128)(2,1)}, u32[]{:S(2)}, u32[]{:S(2)}) collective-permute-start(bf16[272,512]{1,0:T(8,128)(2,1)S(1)} %partial.2), channel_id=1, source_target_pairs={{0,64},{32,96},{64,0},{96,32},{1,65},{33,97},{65,1},{97,33},{2,66}... | collective-permute-start | bytes 835592 | tf_op jit(solution)/shard_map/ppermute | solution.py:181
  48.2 22.4 %all-to-all-start.1 = ((bf16[64,4,528]{2,1,0:T(4,128)(2,1)}), bf16[64,4,528]{2,1,0:T(4,128)(2,1)}, u32[]{:S(2)}, u32[]{:S(2)}) async-start(bf16[64,4,528]{2,1,0:T(4,128)(2,1)} %reshape.85), calls=%async_computation.1 | async-start | bytes 655360 | tf_op jit(solution)/shard_map/all_to_all | solution.py:24
  70.6 1.4 %partial.3 = (f32[272,512]{1,0:T(8,128)S(1)}, bf16[272,512]{1,0:T(8,128)(2,1)}, bf16[272,512]{1,0:T(8,128)(2,1)S(1)}) custom-call(s32[1]{0:T(128)} %bitcast.9.here_ref, bf16[8,2,128,256]{3,2,1,0:T(8,128)(2,1)S(1)} %all-to-all-done.gathered_ref, bf16[256,528]{1,0:T(8,128)(2,1)S(1)} %pad_maximum_fusion.2.own_ref, ...), custom_call_target="tpu_custom_call" | custom-call | flops 415236096 | bytes 1622016 | tf_op jit(solution)/shard_map/partial/pallas_call | solution.py:162
  71.9 2.2 %collective-permute-start.2 = (bf16[272,512]{1,0:T(8,128)(2,1)}, bf16[272,512]{1,0:T(8,128)(2,1)S(1)}, u32[]{:S(2)}, u32[]{:S(2)}) collective-permute-start(bf16[272,512]{1,0:T(8,128)(2,1)} %get-tuple-element.21), channel_id=1, source_target_pairs={{0,32},{32,64},{64,96},{96,0},{1,33},{33,65},{65,97},{97,1},{2,34}... | collective-permute-start | bytes 835592 | tf_op jit(solution)/shard_map/ppermute | solution.py:201
  74.2 3.6 %collective-permute-start.4 = (bf16[272,512]{1,0:T(8,128)(2,1)S(1)}, bf16[272,512]{1,0:T(8,128)(2,1)S(1)}, u32[]{:S(2)}, u32[]{:S(2)}) collective-permute-start(bf16[272,512]{1,0:T(8,128)(2,1)S(1)} %get-tuple-element.22), channel_id=1, source_target_pairs={{0,96},{32,0},{64,32},{96,64},{1,97},{33,1},{65,33},{97,65},{2,98}... | collective-permute-start | bytes 835592 | tf_op jit(solution)/shard_map/ppermute | solution.py:201
  78.1 6.4 %collective-permute-done.2 = bf16[272,512]{1,0:T(8,128)(2,1)S(1)} collective-permute-done((bf16[272,512]{1,0:T(8,128)(2,1)}, bf16[272,512]{1,0:T(8,128)(2,1)S(1)}, u32[]{:S(2)}, u32[]{:S(2)}) %collective-permute-start.2) | collective-permute-done | bytes 278560 | tf_op jit(solution)/shard_map/ppermute | solution.py:201
  84.5 2.5 %collective-permute-done.4 = bf16[272,512]{1,0:T(8,128)(2,1)S(1)} collective-permute-done((bf16[272,512]{1,0:T(8,128)(2,1)S(1)}, bf16[272,512]{1,0:T(8,128)(2,1)S(1)}, u32[]{:S(2)}, u32[]{:S(2)}) %collective-permute-start.4) | collective-permute-done | bytes 278560 | tf_op jit(solution)/shard_map/ppermute | solution.py:201
  87.0 1.1 add_convert_fusion
  88.4 0.8 pad_maximum_fusion.3
  89.1 5.4 %all-to-all-done.1 = bf16[64,4,528]{2,1,0:T(4,128)(2,1)} async-done(((bf16[64,4,528]{2,1,0:T(4,128)(2,1)}), bf16[64,4,528]{2,1,0:T(4,128)(2,1)}, u32[]{:S(2)}, u32[]{:S(2)}) %all-to-all-start.1) | async-done | bytes 270368 | tf_op jit(solution)/shard_map/all_to_all | solution.py:24
  94.5 1.1 reshape.87
  95.6 0.3 convolution_convert_fusion.dy_ref
  96.4 6.2 %all-to-all-start.2 = ((bf16[16,16,528]{2,1,0:T(8,128)(2,1)}), bf16[16,16,528]{2,1,0:T(8,128)(2,1)S(1)}, u32[]{:S(2)}, u32[]{:S(2)}) async-start(bf16[16,16,528]{2,1,0:T(8,128)(2,1)} %bitcast.18), calls=%async_computation.2 | async-start | bytes 655360 | tf_op jit(solution)/shard_map/all_to_all | solution.py:24
  102.7 15.5 %psum.7.sums_ref = f32[8,256]{1,0:T(8,128)} all-reduce(f32[8,256]{1,0:T(8,128)S(1)} %stack.39), channel_id=1, replica_groups=mesh['enc'=8,'x'=4,'z'=16,'rep'=2] {'enc'}, use_global_device_ids=true, to_apply=%region_10.11 | all-reduce | flops 2048 | bytes 16384 | tf_op jit(solution)/shard_map/psum | solution.py:223
  118.2 2.8 %norm.1 = (bf16[256,384]{1,0:T(8,128)(2,1)}, bf16[144,256]{1,0:T(8,128)(2,1)}) custom-call(f32[8,256]{1,0:T(8,128)} %psum.7.sums_ref, bf16[256,528]{1,0:T(8,128)(2,1)} %copy-done, f32[1,528]{1,0:T(1,128)} %broadcast_in_dim.2.gain_ref, bf16[256,384]{1,0:T(8,128)(2,1)} %cnx_ref.1, bf16[144,256]{1,0:T(8,128)(2,1)} %bitcast.38), custom_call_target="tpu_custom_call" | custom-call | flops 1 | bytes 1 | tf_op jit(solution)/shard_map/norm/pallas_call | solution.py:224
  121.0 1.9 %all-to-all-done.2 = bf16[16,16,528]{2,1,0:T(8,128)(2,1)S(1)} async-done(((bf16[16,16,528]{2,1,0:T(8,128)(2,1)}), bf16[16,16,528]{2,1,0:T(8,128)(2,1)S(1)}, u32[]{:S(2)}, u32[]{:S(2)}) %all-to-all-start.2) | async-done | bytes 270368 | tf_op jit(solution)/shard_map/all_to_all | solution.py:24
  123.0 0.6 broadcast_multiply_fusion
  123.6 0.6 broadcast_multiply_fusion.1
  (44 shorter events, 1.9 us)
Async XLA Ops:
  0.6 9.4 %copy-start.5 = (bf16[256,144]{0,1:T(8,128)(2,1)S(1)}, bf16[256,144]{0,1:T(8,128)(2,1)}, u32[]{:S(2)}) copy-start(bf16[256,144]{0,1:T(8,128)(2,1)} %param.12) | copy-start | bytes 221188
  0.6 9.5 %copy-start.4 = (bf16[256,384]{1,0:T(8,128)(2,1)S(1)}, bf16[256,384]{1,0:T(8,128)(2,1)}, u32[]{:S(2)}) copy-start(bf16[256,384]{1,0:T(8,128)(2,1)} %param.13) | copy-start | bytes 589828
  0.7 11.5 %copy-start.2 = (bf16[2048,144]{0,1:T(8,128)(2,1)S(1)}, bf16[2048,144]{0,1:T(8,128)(2,1)}, u32[]{:S(2)}) copy-start(bf16[2048,144]{0,1:T(8,128)(2,1)} %param.15) | copy-start | bytes 1769476
  2.9 35.8 %all-to-all-start = ((bf16[8,2,128,256]{3,2,1,0:T(8,128)(2,1)}), bf16[8,2,128,256]{3,2,1,0:T(8,128)(2,1)S(1)}, u32[]{:S(2)}, u32[]{:S(2)}) async-start(bf16[8,2,128,256]{3,2,1,0:T(8,128)(2,1)} %turn.1), calls=%async_computation | async-start | bytes 2097152 | tf_op jit(solution)/shard_map/all_to_all | solution.py:24
  10.2 19.3 %collective-permute-start = (bf16[256,528]{1,0:T(8,128)(2,1)S(1)}, bf16[256,528]{1,0:T(8,128)(2,1)S(1)}, u32[]{:S(2)}, u32[]{:S(2)}) collective-permute-start(bf16[256,528]{1,0:T(8,128)(2,1)S(1)} %pad_maximum_fusion.2.own_ref), channel_id=1, source_target_pairs={{0,1},{1,0},{2,3},{3,2},{4,5},{5,4},{6,7},{7,6},{8,9},{9,8},{10,11... | collective-permute-start | bytes 811016 | tf_op jit(solution)/shard_map/ppermute | solution.py:138
  14.6 1.9 %copy-start.6 = (f32[384]{0:T(512)S(1)}, f32[384]{0:T(512)}, u32[]{:S(2)}) copy-start(f32[384]{0:T(512)} %param.23) | copy-start | bytes 4612
  14.6 1.9 %copy-start.7 = (f32[144]{0:T(256)S(1)}, f32[144]{0:T(256)}, u32[]{:S(2)}) copy-start(f32[144]{0:T(256)} %param.22) | copy-start | bytes 1732
  23.0 6.5 %copy-start.8 = (s32[1,64]{1,0:T(1,128)S(1)}, s32[1,64]{1,0:T(1,128)}, u32[]{:S(2)}) copy-start(s32[1,64]{1,0:T(1,128)} %param.18) | copy-start | bytes 772
  38.8 5.7 %collective-permute-start.1 = (bf16[8,128,256]{2,1,0:T(8,128)(2,1)S(1)}, bf16[8,128,256]{2,1,0:T(8,128)(2,1)S(1)}, u32[]{:S(2)}, u32[]{:S(2)}) collective-permute-start(bf16[8,128,256]{2,1,0:T(8,128)(2,1)S(1)} %slice_bitcast_fusion), channel_id=1, source_target_pairs={{0,1},{1,0},{2,3},{3,2},{4,5},{5,4},{6,7},{7,6},{8,9},{9,8},{10,11... | collective-permute-start | bytes 1572872 | tf_op jit(solution)/shard_map/ppermute | solution.py:154
  44.5 33.3 %copy-start.9 = (s32[1,64]{1,0:T(1,128)S(1)}, s32[1,64]{1,0:T(1,128)}, u32[]{:S(2)}) copy-start(s32[1,64]{1,0:T(1,128)} %param.19) | copy-start | bytes 772
  44.5 33.5 %copy-start.3 = (bf16[256,144]{0,1:T(8,128)(2,1)S(1)}, bf16[256,144]{0,1:T(8,128)(2,1)}, u32[]{:S(2)}) copy-start(bf16[256,144]{0,1:T(8,128)(2,1)} %param.20) | copy-start | bytes 221188
  44.9 42.2 %collective-permute-start.3 = (bf16[272,512]{1,0:T(8,128)(2,1)S(1)}, bf16[272,512]{1,0:T(8,128)(2,1)}, u32[]{:S(2)}, u32[]{:S(2)}) collective-permute-start(bf16[272,512]{1,0:T(8,128)(2,1)S(1)} %partial.2), channel_id=1, source_target_pairs={{0,64},{32,96},{64,0},{96,32},{1,65},{33,97},{65,1},{97,33},{2,66}... | collective-permute-start | bytes 835592 | tf_op jit(solution)/shard_map/ppermute | solution.py:181
  48.2 46.3 %all-to-all-start.1 = ((bf16[64,4,528]{2,1,0:T(4,128)(2,1)}), bf16[64,4,528]{2,1,0:T(4,128)(2,1)}, u32[]{:S(2)}, u32[]{:S(2)}) async-start(bf16[64,4,528]{2,1,0:T(4,128)(2,1)} %reshape.85), calls=%async_computation.1 | async-start | bytes 655360 | tf_op jit(solution)/shard_map/all_to_all | solution.py:24
  71.9 12.6 %collective-permute-start.2 = (bf16[272,512]{1,0:T(8,128)(2,1)}, bf16[272,512]{1,0:T(8,128)(2,1)S(1)}, u32[]{:S(2)}, u32[]{:S(2)}) collective-permute-start(bf16[272,512]{1,0:T(8,128)(2,1)} %get-tuple-element.21), channel_id=1, source_target_pairs={{0,32},{32,64},{64,96},{96,0},{1,33},{33,65},{65,97},{97,1},{2,34}... | collective-permute-start | bytes 835592 | tf_op jit(solution)/shard_map/ppermute | solution.py:201
  74.2 12.9 %collective-permute-start.4 = (bf16[272,512]{1,0:T(8,128)(2,1)S(1)}, bf16[272,512]{1,0:T(8,128)(2,1)S(1)}, u32[]{:S(2)}, u32[]{:S(2)}) collective-permute-start(bf16[272,512]{1,0:T(8,128)(2,1)S(1)} %get-tuple-element.22), channel_id=1, source_target_pairs={{0,96},{32,0},{64,32},{96,64},{1,97},{33,1},{65,33},{97,65},{2,98}... | collective-permute-start | bytes 835592 | tf_op jit(solution)/shard_map/ppermute | solution.py:201
  87.0 9.1 %copy-start.1 = (bf16[256,384]{1,0:T(8,128)(2,1)S(1)}, bf16[256,384]{1,0:T(8,128)(2,1)}, u32[]{:S(2)}) copy-start(bf16[256,384]{1,0:T(8,128)(2,1)} %cnx_ref.1) | copy-start | bytes 589828
  95.9 22.3 %copy-start = (bf16[256,528]{1,0:T(8,128)(2,1)}, bf16[256,528]{1,0:T(8,128)(2,1)S(1)}, u32[]{:S(2)}) copy-start(bf16[256,528]{1,0:T(8,128)(2,1)S(1)} %convolution_convert_fusion.dy_ref) | copy-start | bytes 811012
  96.4 26.5 %all-to-all-start.2 = ((bf16[16,16,528]{2,1,0:T(8,128)(2,1)}), bf16[16,16,528]{2,1,0:T(8,128)(2,1)S(1)}, u32[]{:S(2)}, u32[]{:S(2)}) async-start(bf16[16,16,528]{2,1,0:T(8,128)(2,1)} %bitcast.18), calls=%async_computation.2 | async-start | bytes 655360 | tf_op jit(solution)/shard_map/all_to_all | solution.py:24

commit v8 on v7

--- a/solution.py
+++ b/solution.py
@@ -176,9 +176,9 @@
             )(hx.reshape(1), gathered, features, paired, other_features)
         )
 
-    far = nx // 2
-    (far_part,) = multiply([far])
-    far_got = lax.ppermute(far_part, "x", shift(nx, far))
+    first = 1
+    (first_part,) = multiply([first])
+    first_got = lax.ppermute(first_part, "x", shift(nx, first))
 
     row = lax.broadcasted_iota(jnp.int32, (rows, rows), 0)
     column = lax.broadcasted_iota(jnp.int32, (rows, rows), 1)
@@ -190,15 +190,15 @@
     ).astype(BF16)
     goal = ((enc_of[0] * depth)[:, None] + token).reshape(1, rows)
     held = pick(row == goal, back).reshape(slots, depth, width)
-    held, far_part = lax.optimization_barrier((held, far_part))
+    held, first_part = lax.optimization_barrier((held, first_part))
     held = exchange(held, ("x", "z")).reshape(rows, width)
     place = ((owner_of[0] * depth)[:, None] + token).reshape(rows, 1)
     routed = pick(column == place, held)
 
-    parts = multiply([k for k in range(nx) if k != far])
-    parts.insert(far, far_part)
+    parts = multiply([k for k in range(nx) if k != first])
+    parts.insert(first, first_part)
     parts = [
-        far_got if k == far else lax.ppermute(part, "x", shift(nx, k)) if k else part
+        first_got if k == first else lax.ppermute(part, "x", shift(nx, k)) if k else part
         for k, part in enumerate(parts)
     ]
     total = sum((part.astype(F32) for part in parts[1:]), parts[0]).astype(BF16)

time: 125 us -> 131 us (1.048)
  starting transfers between devices: 48.7 us -> 52.8 us
  waiting for transfers between devices: 25.5 us -> 27.2 us
    ppermute x2, waiting for transfers between devices: 8.93 us -> 15 us  [shards(): lax.ppermute(part, 'x', shift(nx, k))]
    all_to_all x3, starting transfers between devices: 35.7 us -> 41.2 us  [exchange(): return lax.all_to_all(blocks, axis, 0, 0, tiled=True)]
    all_to_all x3, waiting for transfers between devices: 16.5 us -> 12.1 us  [exchange(): return lax.all_to_all(blocks, axis, 0, 0, tiled=True)]
  transfers between devices with their start and end apart: 8 -> 8, of which waited for: 5 -> 4; matrix products, arithmetic and copies ran while one was open for 19% -> 18% of each run, Pallas kernels for 3% -> 3%
where the time goes in v8:
time: 131 us; the launch traced here: 130 us
  starting transfers between devices  52.8 us (40%)
  waiting for transfers between devices  27.2 us (21%)
  local copies, waits for them, and re-layouts  16.5 us (13%)
  blocking collectives  15.6 us (12%)
  other arithmetic  7.46 us (6%)
  Pallas kernels  6.81 us (5%)
  matrix products  2.85 us (2%)
    all_to_all x3, starting transfers between devices, exchange(): return lax.all_to_all(blocks, axis, 0, 0, tiled=True)  41.2 us
    psum x1, blocking collectives, shards(): sums = lax.psum(sums, 'enc')  15.6 us
    ppermute x2, waiting for transfers between devices, shards(): lax.ppermute(part, 'x', shift(nx, k))  15 us
    all_to_all x3, waiting for transfers between devices, exchange(): return lax.all_to_all(blocks, axis, 0, 0, tiled=True)  12.1 us
    another operation x1, local copies, waits for them, and re-layouts, shards(): jnp.stack([lax.dynamic_index_in_dim(weight, index, 2, keepdims=False).res...  6.5 us
    reshape x1, local copies, waits for them, and re-layouts, shards(): weight = jnp.stack([lax.dynamic_index_in_dim(weight, index, 2, keepdims=F...  5.89 us
    ppermute x2, starting transfers between devices, shards(): lax.ppermute(part, 'x', shift(nx, k))  5.08 us
    dot_general x2, matrix products, pick(): jnp.dot(chosen.astype(BF16), source, preferred_element_type=F32)  2.85 us
  transfers between devices with their start and end apart: 8, of which 4 were waited for; matrix products, arithmetic and copies ran while one was open for 18% of the time, Pallas kernels for 3%

profile of v8, /device:TPU:6, one launch (start us, length us, event | category | flops | bytes accessed | tf_op | source)
XLA Modules:
  0.0 130.1 jit_solution(7280599953606746662)
XLA Ops:
  0.7 2.3 %turn.1 = bf16[8,2,128,256]{3,2,1,0:T(8,128)(2,1)} custom-call(s32[1]{0:T(128)} %bitcast.4.core_ref, s32[1,64]{1,0:T(1,128)} %lengths_ref.1, bf16[256,256]{1,0:T(8,128)(2,1)} %cotangent_ref.1), custom_call_target="tpu_custom_call" | custom-call | tf_op jit(solution)/shard_map/turn/pallas_call | solution.py:128
  2.9 7.1 %all-to-all-start = ((bf16[8,2,128,256]{3,2,1,0:T(8,128)(2,1)}), bf16[8,2,128,256]{3,2,1,0:T(8,128)(2,1)S(1)}, u32[]{:S(2)}, u32[]{:S(2)}) async-start(bf16[8,2,128,256]{3,2,1,0:T(8,128)(2,1)} %turn.1), calls=%async_computation | async-start | bytes 2097152 | tf_op jit(solution)/shard_map/all_to_all | solution.py:24
  10.2 1.9 %collective-permute-start = (bf16[256,528]{1,0:T(8,128)(2,1)S(1)}, bf16[256,528]{1,0:T(8,128)(2,1)S(1)}, u32[]{:S(2)}, u32[]{:S(2)}) collective-permute-start(bf16[256,528]{1,0:T(8,128)(2,1)S(1)} %pad_maximum_fusion.2.own_ref), channel_id=1, source_target_pairs={{0,1},{1,0},{2,3},{3,2},{4,5},{5,4},{6,7},{7,6},{8,9},{9,8},{10,11... | collective-permute-start | bytes 811016 | tf_op jit(solution)/shard_map/ppermute | solution.py:138
  12.1 0.5 copy.50
  12.6 1.7 %pad_maximum_fusion = bf16[2048,528]{1,0:T(8,128)(2,1)S(1)} fusion(bf16[2048,144]{1,0:T(8,128)(2,1)S(1)} %copy.50, bf16[2048,384]{1,0:T(8,128)(2,1)} %param.16), kind=kLoop, calls=%fused_computation | loop fusion | flops 4325376 | bytes 4325376 | tf_op jit(solution)/shard_map/concatenate | solution.py:139
  14.3 0.2 constant_dynamic-slice_fusion.1
  14.6 1.9 %pad_maximum_fusion.1 = bf16[8,2,128,528]{3,2,0,1:T(8,128)(2,1)} fusion(bf16[8,1,128,528]{3,2,0,1:T(8,128)(2,1)S(1)} %bitcast.37, bf16[8,1,128,528]{3,2,0,1:T(8,128)(2,1)S(1)} %bitcast.36), kind=kLoop, calls=%fused_computation.1 | loop fusion | flops 1081344 | bytes 4325376 | tf_op jit(solution)/shard_map/stack | solution.py:142
  16.5 6.5 %copy.53 = bf16[8,2,128,528]{2,1,0,3:T(2,128)(2,1)} copy(bf16[8,2,128,528]{3,2,0,1:T(8,128)(2,1)} %pad_maximum_fusion.1) | data formatting | bytes 4325376 | tf_op jit(solution)/shard_map/stack | solution.py:142
  23.0 5.9 %reshape.83 = bf16[2048,528]{0,1:T(8,128)(2,1)} reshape(bf16[8,2,128,528]{2,1,0,3:T(2,128)(2,1)} %copy.53) | data formatting | bytes 4325376 | tf_op jit(solution)/shard_map/reshape | solution.py:148
  28.9 0.6 broadcast_in_dim.2.gain_ref
  29.5 9.2 %all-to-all-done.gathered_ref = bf16[8,2,128,256]{3,2,1,0:T(8,128)(2,1)S(1)} async-done(((bf16[8,2,128,256]{3,2,1,0:T(8,128)(2,1)}), bf16[8,2,128,256]{3,2,1,0:T(8,128)(2,1)S(1)}, u32[]{:S(2)}, u32[]{:S(2)}) %all-to-all-start) | async-done | bytes 1048608 | tf_op jit(solution)/shard_map/all_to_all | solution.py:24
  38.8 1.9 %collective-permute-start.1 = (bf16[8,128,256]{2,1,0:T(8,128)(2,1)S(1)}, bf16[8,128,256]{2,1,0:T(8,128)(2,1)S(1)}, u32[]{:S(2)}, u32[]{:S(2)}) collective-permute-start(bf16[8,128,256]{2,1,0:T(8,128)(2,1)S(1)} %slice_bitcast_fusion), channel_id=1, source_target_pairs={{0,1},{1,0},{2,3},{3,2},{4,5},{5,4},{6,7},{7,6},{8,9},{9,8},{10,11... | collective-permute-start | bytes 1572872 | tf_op jit(solution)/shard_map/ppermute | solution.py:154
  40.9 2.5 %convolution_convert_fusion.2 = bf16[256,528]{0,1:T(8,128)(2,1)S(1)} fusion(bf16[2048,528]{0,1:T(8,128)(2,1)} %reshape.83, bf16[2048,256]{1,0:T(8,128)(2,1)S(1)} %bitcast.34, s32[256]{0:T(256)S(1)} %add.54), kind=kOutput, calls=%fused_computation.4 | convolution fusion | flops 623190016 | bytes 3482624 | tf_op jit(solution)/shard_map/dot_general | solution.py:28
  43.7 0.8 reshape.85
  44.5 0.4 partial.2
  44.9 2.8 %collective-permute-start.2 = (bf16[272,512]{1,0:T(8,128)(2,1)S(1)}, bf16[272,512]{1,0:T(8,128)(2,1)}, u32[]{:S(2)}, u32[]{:S(2)}) collective-permute-start(bf16[272,512]{1,0:T(8,128)(2,1)S(1)} %partial.2), channel_id=1, source_target_pairs={{0,32},{32,64},{64,96},{96,0},{1,33},{33,65},{65,97},{97,1},{2,34}... | collective-permute-start | bytes 835592 | tf_op jit(solution)/shard_map/ppermute | solution.py:181
  47.6 23.0 %all-to-all-start.1 = ((bf16[64,4,528]{2,1,0:T(4,128)(2,1)}), bf16[64,4,528]{2,1,0:T(4,128)(2,1)}, u32[]{:S(2)}, u32[]{:S(2)}) async-start(bf16[64,4,528]{2,1,0:T(4,128)(2,1)} %reshape.85), calls=%async_computation.1 | async-start | bytes 655360 | tf_op jit(solution)/shard_map/all_to_all | solution.py:24
  70.6 1.4 %partial.3 = (f32[272,512]{1,0:T(8,128)S(1)}, bf16[272,512]{1,0:T(8,128)(2,1)}, bf16[272,512]{1,0:T(8,128)(2,1)S(1)}) custom-call(s32[1]{0:T(128)} %bitcast.9.here_ref, bf16[8,2,128,256]{3,2,1,0:T(8,128)(2,1)S(1)} %all-to-all-done.gathered_ref, bf16[256,528]{1,0:T(8,128)(2,1)S(1)} %pad_maximum_fusion.2.own_ref, ...), custom_call_target="tpu_custom_call" | custom-call | flops 415236096 | bytes 1622016 | tf_op jit(solution)/shard_map/partial/pallas_call | solution.py:162
  72.0 3.2 %collective-permute-start.3 = (bf16[272,512]{1,0:T(8,128)(2,1)}, bf16[272,512]{1,0:T(8,128)(2,1)S(1)}, u32[]{:S(2)}, u32[]{:S(2)}) collective-permute-start(bf16[272,512]{1,0:T(8,128)(2,1)} %get-tuple-element.21), channel_id=1, source_target_pairs={{0,64},{32,96},{64,0},{96,32},{1,65},{33,97},{65,1},{97,33},{2,66}... | collective-permute-start | bytes 835592 | tf_op jit(solution)/shard_map/ppermute | solution.py:201
  75.2 1.9 %collective-permute-start.4 = (bf16[272,512]{1,0:T(8,128)(2,1)S(1)}, bf16[272,512]{1,0:T(8,128)(2,1)S(1)}, u32[]{:S(2)}, u32[]{:S(2)}) collective-permute-start(bf16[272,512]{1,0:T(8,128)(2,1)S(1)} %get-tuple-element.22), channel_id=1, source_target_pairs={{0,96},{32,0},{64,32},{96,64},{1,97},{33,1},{65,33},{97,65},{2,98}... | collective-permute-start | bytes 835592 | tf_op jit(solution)/shard_map/ppermute | solution.py:201
  77.4 9.5 %collective-permute-done.3 = bf16[272,512]{1,0:T(8,128)(2,1)S(1)} collective-permute-done((bf16[272,512]{1,0:T(8,128)(2,1)}, bf16[272,512]{1,0:T(8,128)(2,1)S(1)}, u32[]{:S(2)}, u32[]{:S(2)}) %collective-permute-start.3) | collective-permute-done | bytes 278560 | tf_op jit(solution)/shard_map/ppermute | solution.py:201
  87.0 5.5 %collective-permute-done.4 = bf16[272,512]{1,0:T(8,128)(2,1)S(1)} collective-permute-done((bf16[272,512]{1,0:T(8,128)(2,1)S(1)}, bf16[272,512]{1,0:T(8,128)(2,1)S(1)}, u32[]{:S(2)}, u32[]{:S(2)}) %collective-permute-start.4) | collective-permute-done | bytes 278560 | tf_op jit(solution)/shard_map/ppermute | solution.py:201
  92.4 1.1 add_convert_fusion
  93.7 0.8 pad_maximum_fusion.3
  94.5 1.1 reshape.87
  95.7 0.3 convolution_convert_fusion.dy_ref
  96.5 11.1 %all-to-all-start.2 = ((bf16[16,16,528]{2,1,0:T(8,128)(2,1)}), bf16[16,16,528]{2,1,0:T(8,128)(2,1)S(1)}, u32[]{:S(2)}, u32[]{:S(2)}) async-start(bf16[16,16,528]{2,1,0:T(8,128)(2,1)} %bitcast.18), calls=%async_computation.2 | async-start | bytes 655360 | tf_op jit(solution)/shard_map/all_to_all | solution.py:24
  107.6 15.6 %psum.7.sums_ref = f32[8,256]{1,0:T(8,128)} all-reduce(f32[8,256]{1,0:T(8,128)S(1)} %stack.39), channel_id=1, replica_groups=mesh['enc'=8,'x'=4,'z'=16,'rep'=2] {'enc'}, use_global_device_ids=true, to_apply=%region_10.11 | all-reduce | flops 2048 | bytes 16384 | tf_op jit(solution)/shard_map/psum | solution.py:223
  123.1 2.8 %norm.1 = (bf16[256,384]{1,0:T(8,128)(2,1)}, bf16[144,256]{1,0:T(8,128)(2,1)}) custom-call(f32[8,256]{1,0:T(8,128)} %psum.7.sums_ref, bf16[256,528]{1,0:T(8,128)(2,1)} %copy-done, f32[1,528]{1,0:T(1,128)} %broadcast_in_dim.2.gain_ref, bf16[256,384]{1,0:T(8,128)(2,1)} %cnx_ref.1, bf16[144,256]{1,0:T(8,128)(2,1)} %bitcast.38), custom_call_target="tpu_custom_call" | custom-call | flops 1 | bytes 1 | tf_op jit(solution)/shard_map/norm/pallas_call | solution.py:224
  125.9 2.9 %all-to-all-done.2 = bf16[16,16,528]{2,1,0:T(8,128)(2,1)S(1)} async-done(((bf16[16,16,528]{2,1,0:T(8,128)(2,1)}), bf16[16,16,528]{2,1,0:T(8,128)(2,1)S(1)}, u32[]{:S(2)}, u32[]{:S(2)}) %all-to-all-start.2) | async-done | bytes 270368 | tf_op jit(solution)/shard_map/all_to_all | solution.py:24
  128.8 0.6 broadcast_multiply_fusion
  129.5 0.6 broadcast_multiply_fusion.1
  (44 shorter events, 1.7 us)
Async XLA Ops:
  0.6 9.4 %copy-start.5 = (bf16[256,144]{0,1:T(8,128)(2,1)S(1)}, bf16[256,144]{0,1:T(8,128)(2,1)}, u32[]{:S(2)}) copy-start(bf16[256,144]{0,1:T(8,128)(2,1)} %param.12) | copy-start | bytes 221188
  0.6 9.5 %copy-start.4 = (bf16[256,384]{1,0:T(8,128)(2,1)S(1)}, bf16[256,384]{1,0:T(8,128)(2,1)}, u32[]{:S(2)}) copy-start(bf16[256,384]{1,0:T(8,128)(2,1)} %param.13) | copy-start | bytes 589828
  0.7 11.5 %copy-start.2 = (bf16[2048,144]{0,1:T(8,128)(2,1)S(1)}, bf16[2048,144]{0,1:T(8,128)(2,1)}, u32[]{:S(2)}) copy-start(bf16[2048,144]{0,1:T(8,128)(2,1)} %param.15) | copy-start | bytes 1769476
  2.9 35.8 %all-to-all-start = ((bf16[8,2,128,256]{3,2,1,0:T(8,128)(2,1)}), bf16[8,2,128,256]{3,2,1,0:T(8,128)(2,1)S(1)}, u32[]{:S(2)}, u32[]{:S(2)}) async-start(bf16[8,2,128,256]{3,2,1,0:T(8,128)(2,1)} %turn.1), calls=%async_computation | async-start | bytes 2097152 | tf_op jit(solution)/shard_map/all_to_all | solution.py:24
  10.2 19.3 %collective-permute-start = (bf16[256,528]{1,0:T(8,128)(2,1)S(1)}, bf16[256,528]{1,0:T(8,128)(2,1)S(1)}, u32[]{:S(2)}, u32[]{:S(2)}) collective-permute-start(bf16[256,528]{1,0:T(8,128)(2,1)S(1)} %pad_maximum_fusion.2.own_ref), channel_id=1, source_target_pairs={{0,1},{1,0},{2,3},{3,2},{4,5},{5,4},{6,7},{7,6},{8,9},{9,8},{10,11... | collective-permute-start | bytes 811016 | tf_op jit(solution)/shard_map/ppermute | solution.py:138
  14.6 1.9 %copy-start.6 = (f32[384]{0:T(512)S(1)}, f32[384]{0:T(512)}, u32[]{:S(2)}) copy-start(f32[384]{0:T(512)} %param.23) | copy-start | bytes 4612
  14.6 1.9 %copy-start.7 = (f32[144]{0:T(256)S(1)}, f32[144]{0:T(256)}, u32[]{:S(2)}) copy-start(f32[144]{0:T(256)} %param.22) | copy-start | bytes 1732
  23.0 6.5 %copy-start.8 = (s32[1,64]{1,0:T(1,128)S(1)}, s32[1,64]{1,0:T(1,128)}, u32[]{:S(2)}) copy-start(s32[1,64]{1,0:T(1,128)} %param.18) | copy-start | bytes 772
  38.8 5.7 %collective-permute-start.1 = (bf16[8,128,256]{2,1,0:T(8,128)(2,1)S(1)}, bf16[8,128,256]{2,1,0:T(8,128)(2,1)S(1)}, u32[]{:S(2)}, u32[]{:S(2)}) collective-permute-start(bf16[8,128,256]{2,1,0:T(8,128)(2,1)S(1)} %slice_bitcast_fusion), channel_id=1, source_target_pairs={{0,1},{1,0},{2,3},{3,2},{4,5},{5,4},{6,7},{7,6},{8,9},{9,8},{10,11... | collective-permute-start | bytes 1572872 | tf_op jit(solution)/shard_map/ppermute | solution.py:154
  44.5 32.6 %copy-start.9 = (s32[1,64]{1,0:T(1,128)S(1)}, s32[1,64]{1,0:T(1,128)}, u32[]{:S(2)}) copy-start(s32[1,64]{1,0:T(1,128)} %param.19) | copy-start | bytes 772
  44.5 32.8 %copy-start.3 = (bf16[256,144]{0,1:T(8,128)(2,1)S(1)}, bf16[256,144]{0,1:T(8,128)(2,1)}, u32[]{:S(2)}) copy-start(bf16[256,144]{0,1:T(8,128)(2,1)} %param.20) | copy-start | bytes 221188
  44.9 47.5 %collective-permute-start.2 = (bf16[272,512]{1,0:T(8,128)(2,1)S(1)}, bf16[272,512]{1,0:T(8,128)(2,1)}, u32[]{:S(2)}, u32[]{:S(2)}) collective-permute-start(bf16[272,512]{1,0:T(8,128)(2,1)S(1)} %partial.2), channel_id=1, source_target_pairs={{0,32},{32,64},{64,96},{96,0},{1,33},{33,65},{65,97},{97,1},{2,34}... | collective-permute-start | bytes 835592 | tf_op jit(solution)/shard_map/ppermute | solution.py:181
  47.6 46.9 %all-to-all-start.1 = ((bf16[64,4,528]{2,1,0:T(4,128)(2,1)}), bf16[64,4,528]{2,1,0:T(4,128)(2,1)}, u32[]{:S(2)}, u32[]{:S(2)}) async-start(bf16[64,4,528]{2,1,0:T(4,128)(2,1)} %reshape.85), calls=%async_computation.1 | async-start | bytes 655360 | tf_op jit(solution)/shard_map/all_to_all | solution.py:24
  72.0 15.0 %collective-permute-start.3 = (bf16[272,512]{1,0:T(8,128)(2,1)}, bf16[272,512]{1,0:T(8,128)(2,1)S(1)}, u32[]{:S(2)}, u32[]{:S(2)}) collective-permute-start(bf16[272,512]{1,0:T(8,128)(2,1)} %get-tuple-element.21), channel_id=1, source_target_pairs={{0,64},{32,96},{64,0},{96,32},{1,65},{33,97},{65,1},{97,33},{2,66}... | collective-permute-start | bytes 835592 | tf_op jit(solution)/shard_map/ppermute | solution.py:201
  75.2 17.2 %collective-permute-start.4 = (bf16[272,512]{1,0:T(8,128)(2,1)S(1)}, bf16[272,512]{1,0:T(8,128)(2,1)S(1)}, u32[]{:S(2)}, u32[]{:S(2)}) collective-permute-start(bf16[272,512]{1,0:T(8,128)(2,1)S(1)} %get-tuple-element.22), channel_id=1, source_target_pairs={{0,96},{32,0},{64,32},{96,64},{1,97},{33,1},{65,33},{97,65},{2,98}... | collective-permute-start | bytes 835592 | tf_op jit(solution)/shard_map/ppermute | solution.py:201
  92.4 3.8 %copy-start.1 = (bf16[256,384]{1,0:T(8,128)(2,1)S(1)}, bf16[256,384]{1,0:T(8,128)(2,1)}, u32[]{:S(2)}) copy-start(bf16[256,384]{1,0:T(8,128)(2,1)} %cnx_ref.1) | copy-start | bytes 589828
  96.0 27.2 %copy-start = (bf16[256,528]{1,0:T(8,128)(2,1)}, bf16[256,528]{1,0:T(8,128)(2,1)S(1)}, u32[]{:S(2)}) copy-start(bf16[256,528]{1,0:T(8,128)(2,1)S(1)} %convolution_convert_fusion.dy_ref) | copy-start | bytes 811012
  96.5 32.3 %all-to-all-start.2 = ((bf16[16,16,528]{2,1,0:T(8,128)(2,1)}), bf16[16,16,528]{2,1,0:T(8,128)(2,1)S(1)}, u32[]{:S(2)}, u32[]{:S(2)}) async-start(bf16[16,16,528]{2,1,0:T(8,128)(2,1)} %bitcast.18), calls=%async_computation.2 | async-start | bytes 655360 | tf_op jit(solution)/shard_map/all_to_all | solution.py:24

commit v9 on v7

--- a/solution.py
+++ b/solution.py
@@ -79,22 +79,21 @@
         )
 
 
-def norm_kernel(channels, sums_ref, dy_ref, gain_ref, cnx_ref, sig_ref, cnx_out, sig_out):
+def norm_kernel(channels, sums_ref, dy_ref, gain_ref, pre_ref, cnx_out, sig_out):
     sums = sums_ref[...].T
-    start = 0
-    for index, (pre, out) in enumerate(((cnx_ref, cnx_out), (sig_ref, sig_out))):
+    split = cnx_out.shape[1]
+    for index, at in enumerate((slice(0, split), slice(split, pre_ref.shape[1]))):
         means = sums[:, index * 4 : index * 4 + 4] * (1.0 / channels[index])
         mean, grad_mean = means[:, 0:1], means[:, 2:3]
         inverse = lax.rsqrt(means[:, 1:2] - mean * mean + EPS)
         product = inverse * inverse * (means[:, 3:4] - mean * grad_mean)
-        at = slice(start, start + pre.shape[1 - index])
         scaled = dy_ref[:, at].astype(F32) * gain_ref[:, at]
-        height = pre[...].astype(F32)
+        height = pre_ref[:, at].astype(F32)
+        grad = inverse * (scaled - grad_mean - (height - mean) * product)
         if index:
-            height = height.T
-        grad = inverse * (scaled - grad_mean - (height - mean) * product)
-        out[...] = (grad.T if index else grad).astype(BF16)
-        start += pre.shape[1]
+            sig_out[...] = grad.T.astype(BF16)
+        else:
+            cnx_out[...] = grad.astype(BF16)
 
 
 def shards(
@@ -192,8 +191,6 @@
     held = pick(row == goal, back).reshape(slots, depth, width)
     held, far_part = lax.optimization_barrier((held, far_part))
     held = exchange(held, ("x", "z")).reshape(rows, width)
-    place = ((owner_of[0] * depth)[:, None] + token).reshape(rows, 1)
-    routed = pick(column == place, held)
 
     parts = multiply([k for k in range(nx) if k != far])
     parts.insert(far, far_part)
@@ -205,10 +202,15 @@
     total = jnp.concatenate([total[:block], total[block:, :block].T], axis=1)
     split = feat_cnx.shape[1]
 
+    heights = jnp.concatenate([pre_cnx, pre_sig], axis=1)
+    place = ((owner_of[0] * depth)[:, None] + token).reshape(rows, 1)
+    held, total, heights, place = lax.optimization_barrier((held, total, heights, place))
+    total = exchange(total.reshape(nz, block // nz, width), "z")
+    routed = pick(column == place, held)
     sums = []
     for dy, gain, pre in (
-        (routed[:, :split], gain_cnx, pre_cnx),
-        (routed[:, split:], gain_sig, pre_sig),
+        (routed[:, :split], gain_cnx, heights[:, :split]),
+        (routed[:, split:], gain_sig, heights[:, split:]),
     ):
         height = pre.astype(F32)
         scaled = dy.astype(F32) * gain
@@ -218,9 +220,7 @@
             jnp.sum(scaled, axis=1),
             jnp.sum(scaled * height, axis=1),
         ]
-    sums, total = lax.optimization_barrier((jnp.stack(sums), total))
-    total = exchange(total.reshape(nz, block // nz, width), "z")
-    sums = lax.psum(sums, "enc")
+    sums = lax.psum(jnp.stack(sums), "enc")
     before_cnx, before_sig = pl.pallas_call(
         functools.partial(
             norm_kernel, (gain_cnx.shape[0] * enc_count, gain_sig.shape[0] * enc_count)
@@ -229,11 +229,11 @@
             jax.ShapeDtypeStruct(pre_cnx.shape, BF16),
             jax.ShapeDtypeStruct(pre_sig.shape[::-1], BF16),
         ],
-        in_specs=[VMEM] * 5,
+        in_specs=[VMEM] * 4,
         out_specs=[VMEM] * 2,
         cost_estimate=pl.CostEstimate(flops=1, bytes_accessed=1, transcendentals=0),
         name="norm",
-    )(sums, routed, gains, pre_cnx, pre_sig.T)
+    )(sums, routed, gains, heights)
     scale = 1.0 / math.sqrt(rows * nx * nz * rep_count)
     grad_cnx = jnp.sum(total[:, :, :split].astype(F32), axis=0) * scale
     grad_sig = jnp.sum(total[:, :, split:].astype(F32), axis=0) * scale

time: 125 us -> 129 us (1.032)
  waiting for transfers between devices: 25.5 us -> 30.6 us
  starting transfers between devices: 48.7 us -> 46.6 us
    all_to_all x3, waiting for transfers between devices: 16.5 us -> 30.6 us  [exchange(): return lax.all_to_all(blocks, axis, 0, 0, tiled=True)]
    ppermute x2, waiting for transfers between devices: 8.93 us -> 0.01 us  [shards(): lax.ppermute(part, 'x', shift(nx, k))]
    all_to_all x3, starting transfers between devices: 35.7 us -> 33.4 us  [exchange(): return lax.all_to_all(blocks, axis, 0, 0, tiled=True)]
  transfers between devices with their start and end apart: 8 -> 8, of which waited for: 5 -> 3; matrix products, arithmetic and copies ran while one was open for 19% -> 19% of each run, Pallas kernels for 3% -> 2%
where the time goes in v9:
time: 129 us; the launch traced here: 127 us
  starting transfers between devices  46.6 us (36%)
  waiting for transfers between devices  30.6 us (24%)
  local copies, waits for them, and re-layouts  16.4 us (13%)
  blocking collectives  15.6 us (12%)
  other arithmetic  7.52 us (6%)
  Pallas kernels  6.77 us (5%)
  matrix products  2.84 us (2%)
    all_to_all x3, starting transfers between devices, exchange(): return lax.all_to_all(blocks, axis, 0, 0, tiled=True)  33.4 us
    all_to_all x3, waiting for transfers between devices, exchange(): return lax.all_to_all(blocks, axis, 0, 0, tiled=True)  30.6 us
    psum x1, blocking collectives, shards(): sums = lax.psum(jnp.stack(sums), 'enc')  15.6 us
    another operation x1, local copies, waits for them, and re-layouts, shards(): jnp.stack([lax.dynamic_index_in_dim(weight, index, 2, keepdims=False).res...  6.5 us
    reshape x1, local copies, waits for them, and re-layouts, shards(): weight = jnp.stack([lax.dynamic_index_in_dim(weight, index, 2, keepdims=F...  5.89 us
    ppermute x2, starting transfers between devices, shards(): lax.ppermute(part, 'x', shift(nx, k))  5.83 us
    ppermute x1, starting transfers between devices, shards(): far_got = lax.ppermute(far_part, 'x', shift(nx, far))  3.45 us
    dot_general x2, matrix products, pick(): jnp.dot(chosen.astype(BF16), source, preferred_element_type=F32)  2.84 us
  transfers between devices with their start and end apart: 8, of which 3 were waited for; matrix products, arithmetic and copies ran while one was open for 19% of the time, Pallas kernels for 2%

profile of v9, /device:TPU:6, one launch (start us, length us, event | category | flops | bytes accessed | tf_op | source)
XLA Modules:
  0.0 127.2 jit_solution(3873447372157188308)
XLA Ops:
  0.7 2.3 %turn.1 = bf16[8,2,128,256]{3,2,1,0:T(8,128)(2,1)} custom-call(s32[1]{0:T(128)} %bitcast.1.core_ref, s32[1,64]{1,0:T(1,128)} %lengths_ref.1, bf16[256,256]{1,0:T(8,128)(2,1)} %cotangent_ref.1), custom_call_target="tpu_custom_call" | custom-call | tf_op jit(solution)/shard_map/turn/pallas_call | solution.py:127
  2.9 7.1 %all-to-all-start = ((bf16[8,2,128,256]{3,2,1,0:T(8,128)(2,1)}), bf16[8,2,128,256]{3,2,1,0:T(8,128)(2,1)S(1)}, u32[]{:S(2)}, u32[]{:S(2)}) async-start(bf16[8,2,128,256]{3,2,1,0:T(8,128)(2,1)} %turn.1), calls=%async_computation | async-start | bytes 2097152 | tf_op jit(solution)/shard_map/all_to_all | solution.py:24
  10.2 1.9 %collective-permute-start = (bf16[256,528]{1,0:T(8,128)(2,1)S(1)}, bf16[256,528]{1,0:T(8,128)(2,1)S(1)}, u32[]{:S(2)}, u32[]{:S(2)}) collective-permute-start(bf16[256,528]{1,0:T(8,128)(2,1)S(1)} %pad_maximum_fusion.2.own_ref), channel_id=1, source_target_pairs={{0,1},{1,0},{2,3},{3,2},{4,5},{5,4},{6,7},{7,6},{8,9},{9,8},{10,11... | collective-permute-start | bytes 811016 | tf_op jit(solution)/shard_map/ppermute | solution.py:137
  12.1 0.5 copy.50
  12.6 1.7 %pad_maximum_fusion = bf16[2048,528]{1,0:T(8,128)(2,1)S(1)} fusion(bf16[2048,144]{1,0:T(8,128)(2,1)S(1)} %copy.50, bf16[2048,384]{1,0:T(8,128)(2,1)} %param.16), kind=kLoop, calls=%fused_computation | loop fusion | flops 4325376 | bytes 4325376 | tf_op jit(solution)/shard_map/concatenate | solution.py:138
  14.3 0.2 constant_dynamic-slice_fusion.1
  14.6 1.9 %pad_maximum_fusion.1 = bf16[8,2,128,528]{3,2,0,1:T(8,128)(2,1)} fusion(bf16[8,1,128,528]{3,2,0,1:T(8,128)(2,1)S(1)} %bitcast.37, bf16[8,1,128,528]{3,2,0,1:T(8,128)(2,1)S(1)} %bitcast.36), kind=kLoop, calls=%fused_computation.1 | loop fusion | flops 1081344 | bytes 4325376 | tf_op jit(solution)/shard_map/stack | solution.py:141
  16.5 6.5 %copy.53 = bf16[8,2,128,528]{2,1,0,3:T(2,128)(2,1)} copy(bf16[8,2,128,528]{3,2,0,1:T(8,128)(2,1)} %pad_maximum_fusion.1) | data formatting | bytes 4325376 | tf_op jit(solution)/shard_map/stack | solution.py:141
  23.0 5.9 %reshape.91 = bf16[2048,528]{0,1:T(8,128)(2,1)} reshape(bf16[8,2,128,528]{2,1,0,3:T(2,128)(2,1)} %copy.53) | data formatting | bytes 4325376 | tf_op jit(solution)/shard_map/reshape | solution.py:147
  28.9 0.6 broadcast_in_dim.2.gain_ref
  29.5 9.2 %all-to-all-done.gathered_ref = bf16[8,2,128,256]{3,2,1,0:T(8,128)(2,1)S(1)} async-done(((bf16[8,2,128,256]{3,2,1,0:T(8,128)(2,1)}), bf16[8,2,128,256]{3,2,1,0:T(8,128)(2,1)S(1)}, u32[]{:S(2)}, u32[]{:S(2)}) %all-to-all-start) | async-done | bytes 1048608 | tf_op jit(solution)/shard_map/all_to_all | solution.py:24
  38.8 0.8 slice_bitcast_fusion
  39.6 1.9 %collective-permute-start.1 = (bf16[8,128,256]{2,1,0:T(8,128)(2,1)}, bf16[8,128,256]{2,1,0:T(8,128)(2,1)S(1)}, u32[]{:S(2)}, u32[]{:S(2)}) collective-permute-start(bf16[8,128,256]{2,1,0:T(8,128)(2,1)} %slice_bitcast_fusion), channel_id=1, source_target_pairs={{0,1},{1,0},{2,3},{3,2},{4,5},{5,4},{6,7},{7,6},{8,9},{9,8},{10,11... | collective-permute-start | bytes 1572872 | tf_op jit(solution)/shard_map/ppermute | solution.py:153
  41.7 2.5 %convolution_convert_fusion.2 = bf16[256,528]{0,1:T(8,128)(2,1)S(1)} fusion(bf16[2048,528]{0,1:T(8,128)(2,1)} %reshape.91, bf16[2048,256]{1,0:T(8,128)(2,1)S(1)} %bitcast.34, s32[256]{0:T(256)S(1)} %add.54), kind=kOutput, calls=%fused_computation.4 | convolution fusion | flops 623190016 | bytes 3482624 | tf_op jit(solution)/shard_map/dot_general | solution.py:28
  44.4 0.8 reshape.93
  45.3 1.4 %partial.3 = (f32[272,512]{1,0:T(8,128)S(1)}, bf16[272,512]{1,0:T(8,128)(2,1)}, bf16[272,512]{1,0:T(8,128)(2,1)S(1)}) custom-call(s32[1]{0:T(128)} %bitcast.6.here_ref, bf16[8,2,128,256]{3,2,1,0:T(8,128)(2,1)S(1)} %all-to-all-done.gathered_ref, bf16[256,528]{1,0:T(8,128)(2,1)S(1)} %pad_maximum_fusion.2.own_ref, ...), custom_call_target="tpu_custom_call" | custom-call | flops 415236096 | bytes 1622016 | tf_op jit(solution)/shard_map/partial/pallas_call | solution.py:161
  46.6 2.7 %collective-permute-start.2 = (bf16[272,512]{1,0:T(8,128)(2,1)}, bf16[272,512]{1,0:T(8,128)(2,1)}, u32[]{:S(2)}, u32[]{:S(2)}) collective-permute-start(bf16[272,512]{1,0:T(8,128)(2,1)} %get-tuple-element.23), channel_id=1, source_target_pairs={{0,32},{32,64},{64,96},{96,0},{1,33},{33,65},{65,97},{97,1},{2,34}... | collective-permute-start | bytes 835592 | tf_op jit(solution)/shard_map/ppermute | solution.py:198
  49.4 3.1 %collective-permute-start.4 = (bf16[272,512]{1,0:T(8,128)(2,1)S(1)}, bf16[272,512]{1,0:T(8,128)(2,1)}, u32[]{:S(2)}, u32[]{:S(2)}) collective-permute-start(bf16[272,512]{1,0:T(8,128)(2,1)S(1)} %get-tuple-element.24), channel_id=1, source_target_pairs={{0,96},{32,0},{64,32},{96,64},{1,97},{33,1},{65,33},{97,65},{2,98}... | collective-permute-start | bytes 835592 | tf_op jit(solution)/shard_map/ppermute | solution.py:198
  52.5 0.4 partial.2
  52.9 3.4 %collective-permute-start.3 = (bf16[272,512]{1,0:T(8,128)(2,1)S(1)}, bf16[272,512]{1,0:T(8,128)(2,1)S(1)}, u32[]{:S(2)}, u32[]{:S(2)}) collective-permute-start(bf16[272,512]{1,0:T(8,128)(2,1)S(1)} %partial.2), channel_id=1, source_target_pairs={{0,64},{32,96},{64,0},{96,32},{1,65},{33,97},{65,1},{97,33},{2,66}... | collective-permute-start | bytes 835592 | tf_op jit(solution)/shard_map/ppermute | solution.py:180
  56.3 22.8 %all-to-all-start.1 = ((bf16[64,4,528]{2,1,0:T(4,128)(2,1)}), bf16[64,4,528]{2,1,0:T(4,128)(2,1)S(1)}, u32[]{:S(2)}, u32[]{:S(2)}) async-start(bf16[64,4,528]{2,1,0:T(4,128)(2,1)} %reshape.93), calls=%async_computation.1 | async-start | bytes 655360 | tf_op jit(solution)/shard_map/all_to_all | solution.py:24
  79.5 1.2 add_convert_fusion
  80.8 0.8 pad_maximum_fusion.3
  81.6 20.9 %all-to-all-done.1 = bf16[64,4,528]{2,1,0:T(4,128)(2,1)S(1)} async-done(((bf16[64,4,528]{2,1,0:T(4,128)(2,1)}), bf16[64,4,528]{2,1,0:T(4,128)(2,1)S(1)}, u32[]{:S(2)}, u32[]{:S(2)}) %all-to-all-start.1) | async-done | bytes 270368 | tf_op jit(solution)/shard_map/all_to_all | solution.py:24
  102.7 3.6 %all-to-all-start.2 = ((bf16[16,16,528]{2,1,0:T(8,128)(2,1)}), bf16[16,16,528]{2,1,0:T(8,128)(2,1)S(1)}, u32[]{:S(2)}, u32[]{:S(2)}) async-start(bf16[16,16,528]{2,1,0:T(8,128)(2,1)} %bitcast.10), calls=%async_computation.2 | async-start | bytes 655360 | tf_op jit(solution)/shard_map/all_to_all | solution.py:24
  106.2 0.3 convolution_convert_fusion.dy_ref
  106.8 0.2 fusion.1
  107.1 15.6 %psum.7.sums_ref = f32[8,256]{1,0:T(8,128)} all-reduce(f32[8,256]{1,0:T(8,128)S(1)} %stack.39), channel_id=1, replica_groups=mesh['enc'=8,'x'=4,'z'=16,'rep'=2] {'enc'}, use_global_device_ids=true, to_apply=%region_10.11 | all-reduce | flops 2048 | bytes 16384 | tf_op jit(solution)/shard_map/psum | solution.py:223
  122.6 2.8 %norm.1 = (bf16[256,384]{1,0:T(8,128)(2,1)}, bf16[144,256]{1,0:T(8,128)(2,1)}) custom-call(f32[8,256]{1,0:T(8,128)} %psum.7.sums_ref, bf16[256,528]{1,0:T(8,128)(2,1)} %copy-done.1, f32[1,528]{1,0:T(1,128)} %broadcast_in_dim.2.gain_ref, bf16[256,528]{1,0:T(8,128)(2,1)} %copy-done), custom_call_target="tpu_custom_call" | custom-call | flops 1 | bytes 1 | tf_op jit(solution)/shard_map/norm/pallas_call | solution.py:224
  125.4 0.5 all-to-all-done.2
  125.9 0.6 broadcast_multiply_fusion
  126.6 0.6 broadcast_multiply_fusion.1
  (46 shorter events, 1.5 us)
Async XLA Ops:
  0.6 9.4 %copy-start.5 = (bf16[256,144]{0,1:T(8,128)(2,1)S(1)}, bf16[256,144]{0,1:T(8,128)(2,1)}, u32[]{:S(2)}) copy-start(bf16[256,144]{0,1:T(8,128)(2,1)} %param.12) | copy-start | bytes 221188
  0.6 9.5 %copy-start.4 = (bf16[256,384]{1,0:T(8,128)(2,1)S(1)}, bf16[256,384]{1,0:T(8,128)(2,1)}, u32[]{:S(2)}) copy-start(bf16[256,384]{1,0:T(8,128)(2,1)} %param.13) | copy-start | bytes 589828
  0.7 11.5 %copy-start.2 = (bf16[2048,144]{0,1:T(8,128)(2,1)S(1)}, bf16[2048,144]{0,1:T(8,128)(2,1)}, u32[]{:S(2)}) copy-start(bf16[2048,144]{0,1:T(8,128)(2,1)} %param.15) | copy-start | bytes 1769476
  2.9 35.8 %all-to-all-start = ((bf16[8,2,128,256]{3,2,1,0:T(8,128)(2,1)}), bf16[8,2,128,256]{3,2,1,0:T(8,128)(2,1)S(1)}, u32[]{:S(2)}, u32[]{:S(2)}) async-start(bf16[8,2,128,256]{3,2,1,0:T(8,128)(2,1)} %turn.1), calls=%async_computation | async-start | bytes 2097152 | tf_op jit(solution)/shard_map/all_to_all | solution.py:24
  10.2 19.3 %collective-permute-start = (bf16[256,528]{1,0:T(8,128)(2,1)S(1)}, bf16[256,528]{1,0:T(8,128)(2,1)S(1)}, u32[]{:S(2)}, u32[]{:S(2)}) collective-permute-start(bf16[256,528]{1,0:T(8,128)(2,1)S(1)} %pad_maximum_fusion.2.own_ref), channel_id=1, source_target_pairs={{0,1},{1,0},{2,3},{3,2},{4,5},{5,4},{6,7},{7,6},{8,9},{9,8},{10,11... | collective-permute-start | bytes 811016 | tf_op jit(solution)/shard_map/ppermute | solution.py:137
  14.6 1.9 %copy-start.7 = (f32[384]{0:T(512)S(1)}, f32[384]{0:T(512)}, u32[]{:S(2)}) copy-start(f32[384]{0:T(512)} %param.23) | copy-start | bytes 4612
  14.6 1.9 %copy-start.8 = (f32[144]{0:T(256)S(1)}, f32[144]{0:T(256)}, u32[]{:S(2)}) copy-start(f32[144]{0:T(256)} %param.22) | copy-start | bytes 1732
  23.0 6.5 %copy-start.9 = (s32[1,64]{1,0:T(1,128)S(1)}, s32[1,64]{1,0:T(1,128)}, u32[]{:S(2)}) copy-start(s32[1,64]{1,0:T(1,128)} %param.18) | copy-start | bytes 772
  39.6 5.7 %collective-permute-start.1 = (bf16[8,128,256]{2,1,0:T(8,128)(2,1)}, bf16[8,128,256]{2,1,0:T(8,128)(2,1)S(1)}, u32[]{:S(2)}, u32[]{:S(2)}) collective-permute-start(bf16[8,128,256]{2,1,0:T(8,128)(2,1)} %slice_bitcast_fusion), channel_id=1, source_target_pairs={{0,1},{1,0},{2,3},{3,2},{4,5},{5,4},{6,7},{7,6},{8,9},{9,8},{10,11... | collective-permute-start | bytes 1572872 | tf_op jit(solution)/shard_map/ppermute | solution.py:153
  45.3 33.9 %copy-start.10 = (s32[1,64]{1,0:T(1,128)S(1)}, s32[1,64]{1,0:T(1,128)}, u32[]{:S(2)}) copy-start(s32[1,64]{1,0:T(1,128)} %param.19) | copy-start | bytes 772
  45.3 33.9 %copy-start.6 = (bf16[256,144]{0,1:T(8,128)(2,1)S(1)}, bf16[256,144]{0,1:T(8,128)(2,1)}, u32[]{:S(2)}) copy-start(bf16[256,144]{0,1:T(8,128)(2,1)} %param.20) | copy-start | bytes 221188
  46.6 32.8 %collective-permute-start.2 = (bf16[272,512]{1,0:T(8,128)(2,1)}, bf16[272,512]{1,0:T(8,128)(2,1)}, u32[]{:S(2)}, u32[]{:S(2)}) collective-permute-start(bf16[272,512]{1,0:T(8,128)(2,1)} %get-tuple-element.23), channel_id=1, source_target_pairs={{0,32},{32,64},{64,96},{96,0},{1,33},{33,65},{65,97},{97,1},{2,34}... | collective-permute-start | bytes 835592 | tf_op jit(solution)/shard_map/ppermute | solution.py:198
  49.4 30.1 %collective-permute-start.4 = (bf16[272,512]{1,0:T(8,128)(2,1)S(1)}, bf16[272,512]{1,0:T(8,128)(2,1)}, u32[]{:S(2)}, u32[]{:S(2)}) collective-permute-start(bf16[272,512]{1,0:T(8,128)(2,1)S(1)} %get-tuple-element.24), channel_id=1, source_target_pairs={{0,96},{32,0},{64,32},{96,64},{1,97},{33,1},{65,33},{97,65},{2,98}... | collective-permute-start | bytes 835592 | tf_op jit(solution)/shard_map/ppermute | solution.py:198
  52.9 28.0 %copy-start.3 = (bf16[256,384]{1,0:T(8,128)(2,1)S(1)}, bf16[256,384]{1,0:T(8,128)(2,1)}, u32[]{:S(2)}) copy-start(bf16[256,384]{1,0:T(8,128)(2,1)} %param.21) | copy-start | bytes 589828
  52.9 26.6 %collective-permute-start.3 = (bf16[272,512]{1,0:T(8,128)(2,1)S(1)}, bf16[272,512]{1,0:T(8,128)(2,1)S(1)}, u32[]{:S(2)}, u32[]{:S(2)}) collective-permute-start(bf16[272,512]{1,0:T(8,128)(2,1)S(1)} %partial.2), channel_id=1, source_target_pairs={{0,64},{32,96},{64,0},{96,32},{1,65},{33,97},{65,1},{97,33},{2,66}... | collective-permute-start | bytes 835592 | tf_op jit(solution)/shard_map/ppermute | solution.py:180
  56.3 46.2 %all-to-all-start.1 = ((bf16[64,4,528]{2,1,0:T(4,128)(2,1)}), bf16[64,4,528]{2,1,0:T(4,128)(2,1)S(1)}, u32[]{:S(2)}, u32[]{:S(2)}) async-start(bf16[64,4,528]{2,1,0:T(4,128)(2,1)} %reshape.93), calls=%async_computation.1 | async-start | bytes 655360 | tf_op jit(solution)/shard_map/all_to_all | solution.py:24
  81.6 41.0 %copy-start = (bf16[256,528]{1,0:T(8,128)(2,1)}, bf16[256,528]{1,0:T(8,128)(2,1)S(1)}, u32[]{:S(2)}) copy-start(bf16[256,528]{1,0:T(8,128)(2,1)S(1)} %get-tuple-element.26.pre_ref) | copy-start | bytes 811012
  102.7 23.2 %all-to-all-start.2 = ((bf16[16,16,528]{2,1,0:T(8,128)(2,1)}), bf16[16,16,528]{2,1,0:T(8,128)(2,1)S(1)}, u32[]{:S(2)}, u32[]{:S(2)}) async-start(bf16[16,16,528]{2,1,0:T(8,128)(2,1)} %bitcast.10), calls=%async_computation.2 | async-start | bytes 655360 | tf_op jit(solution)/shard_map/all_to_all | solution.py:24
  106.5 16.1 %copy-start.1 = (bf16[256,528]{1,0:T(8,128)(2,1)}, bf16[256,528]{1,0:T(8,128)(2,1)S(1)}, u32[]{:S(2)}) copy-start(bf16[256,528]{1,0:T(8,128)(2,1)S(1)} %convolution_convert_fusion.dy_ref) | copy-start | bytes 811012
